TPU v7x, 256 devices: a whole 4x4x8 slice. The times are simulated.
256 devices in a mesh: tile: 32 (over z, x), ens: 8 (over y, core).
Axes of the slice: x: 4, y: 4, z: 8, core: 2. Of those that a mesh axis runs over, the one named last changes fastest.
Arguments:
- perturbations: bfloat16 [80, 16, 512, 128], P('ens', None, 'tile'), may hold values from -9 to 9
- innovations: float32 [65536], P('tile'), may hold values from -48 to 48
- obs_precision: float32 [65536], P('tile'), may hold values from 0.001 to 0.016
- obs_weights: float32 [16, 65536], P(None, 'tile'), may hold values from -1.5 to 1.5
- obs_cell: int32 [65536], P('tile'), may hold values from 0 to 2047
- obs_count: int32 [32], P('tile'), may hold values from 1 to 2048, as said below
Outputs:
- alpha_fields: float32 [80, 16, 512, 128], P('ens', None, 'tile')
- increment: float32 [16, 512, 128], P(None, 'tile')
Inputs may be any that keep to these rules, and one draw needn't show every extreme that they name: Tile t's observations fill slots 0 to obs_count[t] - 1 of its 2048 slots; the other slots are ignored; in every draw some tile is full. `obs_cell`: A cell of a tile is numbered x * 128 + y with x its row within the tile.
All inputs are finite; a program needn't handle non-finite values.
Results may differ from a plain program's by a relative error of at most 0.0004.
Values may be sent and summed in bfloat16 or wider, within the bound.
No kernel may reach another device: no remote copies, remote signals or barrier semaphores. Data moves between devices by JAX's collectives and lax.ppermute only.
A program may use at most 64 MiB of HBM per device.

v0:
```python
import math

import jax
import jax.numpy as jnp
from jax import lax
from jax.sharding import PartitionSpec as P

ITERS = 2


highest = lax.Precision.HIGHEST
vertical_spread = 2.0


def with_halo(x, sides, width):
    for axis, dim in sides:
        size, length = (lax.axis_size(axis), x.shape[dim])
        up = [(i, (i + 1) % size) for i in range(size)]
        down = [(j, i) for i, j in up]
        last = lax.slice_in_dim(x, length - width, length, axis=dim)
        initial = lax.slice_in_dim(x, 0, width, axis=dim)
        before = lax.ppermute(last, axis, up)
        after = lax.ppermute(initial, axis, down)
        x = jnp.concatenate([before, x, after], axis=dim)
    return x


def gauss_kernel(radius, spread):
    offsets = jnp.arange(-radius, radius + 1).astype(jnp.float32) / spread
    return jnp.exp(-offsets * offsets)


def x_kernel(radius):
    kernel = gauss_kernel(radius, float(radius))
    return kernel / jnp.sqrt(jnp.sum(kernel * kernel))


def band_matrix(length, spread):
    position = jnp.arange(length).astype(jnp.float32)
    spacing = (position[:, None] - position[None, :]) / spread
    entire = gauss_kernel(length, spread)
    return jnp.exp(-spacing * spacing) / jnp.sqrt(jnp.sum(entire * entire))


def along_x(padded, kernel, radius, row_count):
    result = kernel[0] * lax.slice_in_dim(padded, 0, row_count, axis=2)
    for offset in range(1, 2 * radius + 1):
        result = result + kernel[offset] * lax.slice_in_dim(
            padded, offset, offset + row_count, axis=2
        )
    return result


def observe(field_flat, weights, cell_ids, live_mask):
    picked = jnp.take(field_flat, cell_ids, axis=1)
    return live_mask * jnp.sum(weights * picked, axis=0)


def observe_adjoint(values, weights, cell_ids, live_mask, cell_total):
    addition = weights * (live_mask * values)[None, :]
    return jnp.zeros((weights.shape[0], cell_total), jnp.float32).at[:, cell_ids].add(addition)


def local(perturbations, innovations, obs_precision, obs_weights, obs_cell, obs_count):
    levels = perturbations.shape[1]
    row_count = perturbations.shape[2]
    columns = perturbations.shape[3]
    radius = row_count // 2
    cell_total = row_count * columns
    vertical = band_matrix(levels, vertical_spread)
    lateral = band_matrix(columns, columns / 16.0)
    kernel = x_kernel(radius)
    scale = 1.0 / math.sqrt(lax.axis_size("ens") * perturbations.shape[0])
    members = perturbations.astype(jnp.float32)
    live_mask = (jnp.arange(obs_cell.shape[0]) < obs_count[0]).astype(jnp.float32)

    def localize(fields):
        fields = jnp.einsum("lm,kmxy->klxy", vertical, fields, precision=highest)
        fields = jnp.einsum("klxy,yb->klxb", fields, lateral, precision=highest)
        padded = with_halo(fields, (("tile", 2),), radius)
        return along_x(padded, kernel, radius, row_count)

    def adjoint_localize(gradient):
        result = localize(members * gradient[None] * scale)
        return result

    def norm_squared(field):
        return lax.psum(jnp.sum(field * field), ("tile", "ens"))

    rhs_gradient = observe_adjoint(
        obs_precision * innovations, obs_weights, obs_cell, live_mask, cell_total
    )
    right_side = adjoint_localize(rhs_gradient.reshape(levels, row_count, columns))
    solution = jnp.zeros_like(right_side)
    residual = right_side
    direction = residual
    norm_now = norm_squared(residual)
    for iteration in range(ITERS):
        partial_value = jnp.sum(members * localize(direction), axis=0) * scale
        summed = lax.psum(partial_value, "ens")
        observed = observe(summed.reshape(levels, cell_total), obs_weights, obs_cell, live_mask)
        hessian_gradient = observe_adjoint(
            obs_precision * observed, obs_weights, obs_cell, live_mask, cell_total
        )
        applied = direction + adjoint_localize(hessian_gradient.reshape(levels, row_count, columns))
        step_size = norm_now / lax.psum(jnp.sum(direction * applied), ("tile", "ens"))
        solution = solution + step_size * direction
        residual = residual - step_size * applied
        norm_next = norm_squared(residual)
        direction = residual + norm_next / norm_now * direction
        norm_now = norm_next
    final_partial = jnp.sum(members * localize(solution), axis=0) * scale
    increment = lax.psum(final_partial, "ens")
    return (solution, increment)


def solution(mesh):
    placed = (
        P("ens", None, "tile", None),
        P("tile"),
        P("tile"),
        P(None, "tile"),
        P("tile"),
        P("tile"),
    )
    return jax.shard_map(
        local,
        mesh=mesh,
        in_specs=placed,
        out_specs=(P("ens", None, "tile", None), P(None, "tile", None)),
        check_vma=False,
    )
```

profile of v0, /device:TPU:1, one launch (start us, length us, event | category | flops | bytes accessed | tf_op | source)
XLA Modules:
  0.0 751.9 jit_solution(14852425023107698777)
XLA Ops:
  13.2 11.7 %scatter_custom_fusion = f32[16,2048]{0,1:T(8,128)S(1)} fusion(s32[2048]{0:T(1024)S(1)} %get-tuple-element.21, f32[2048,16]{1,0:T(8,128)S(1)} %copy.8, f32[]{:T(128)} %constant.19.clone.1), kind=kCustom, calls=%fused_computation.520 | custom fusion | flops 32768 | bytes 131076 | tf_op jit(solution)/shard_map/scatter-add | solution.py:61
  25.4 1.6 fusion.312
  27.0 1.4 fusion.294
  28.5 2.1 collective-permute-start
  30.7 6.8 collective-permute-start.1
  39.5 12.3 %collective-permute-done = f32[10,16,8,128]{3,2,1,0:T(8,128)} collective-permute-done((f32[10,16,8,128]{3,2,1,0:T(8,128)S(1)}, f32[10,16,8,128]{3,2,1,0:T(8,128)}, u32[]{:S(2)}, u32[]{:S(2)}) %collective-permute-start) | collective-permute-done | bytes 655392 | tf_op jit(solution)/shard_map/ppermute | solution.py:22
  51.8 18.9 %fusion.231 = f32[10,16,16,128]{3,2,1,0:T(8,128)S(1)} fusion(f32[10,16,16,128]{3,2,1,0:T(8,128)S(1)} %fusion.294, f32[10,16,8,128]{3,2,1,0:T(8,128)} %collective-permute-done.1, f32[10,16,8,128]{3,2,1,0:T(8,128)} %collective-permute-done, f32[]{:T(128)} %bitcast.24, f32[]{:T(128)} %bitcast.23, f32[]{:T(128)} %bitcast.22, f32[]{:T(128)} %bitcast.21, ...), kind=kLoop, calls=%fused_computation.411 | loop fusion | flops 16056320 | bytes 3932228 | tf_op jit(solution)/shard_map/add | solution.py:48
  70.7 1.6 fusion.309
  72.3 1.4 fusion.292
  74.0 4.8 collective-permute-start.3
  78.8 13.5 %collective-permute-done.2 = f32[10,16,8,128]{3,2,1,0:T(8,128)S(1)} collective-permute-done((f32[10,16,8,128]{3,2,1,0:T(8,128)S(1)}, f32[10,16,8,128]{3,2,1,0:T(8,128)S(1)}, u32[]{:S(2)}, u32[]{:S(2)}) %collective-permute-start.2) | collective-permute-done | bytes 655392 | tf_op jit(solution)/shard_map/ppermute | solution.py:22
  92.3 14.3 %fusion.2 = f32[16,16,128]{2,1,0:T(8,128)S(1)} fusion(bf16[10,16,16,128]{3,2,1,0:T(8,128)(2,1)S(1)} %copy-done, f32[10,16,16,128]{3,2,1,0:T(8,128)S(1)} %fusion.292, f32[10,16,8,128]{3,2,1,0:T(8,128)S(1)} %collective-permute-done.3, f32[10,16,8,128]{3,2,1,0:T(8,128)S(1)} %collective-permute-done.2, f32[]{:T(128)} %bitcast.24, f32[]{:T(128)} %bitcast.23, ...), kind=kLoop, calls=%fused_computation.182 | loop fusion | flops 17006592 | bytes 3407940 | tf_op jit(solution)/shard_map/reduce_sum | solution.py:99
  106.6 1.3 copy.10
  108.6 66.2 %all-reduce.5.cloned.1.call-done = f32[16,2048]{0,1:T(8,128)} async-done(((f32[16,2048]{0,1:T(8,128)}), f32[16,2048]{0,1:T(8,128)}) %all-reduce.5.cloned.1.call-update) | async-done | bytes 131088 | tf_op jit(solution)/shard_map/psum | solution.py:100
  174.8 8.9 %gather_fusion = f32[2048,16]{1,0:T(8,128)} fusion(f32[16,2048]{0,1:T(8,128)} %all-reduce.5.cloned.1.call-done, s32[2048]{0:T(1024)S(1)} %get-tuple-element.20), kind=kCustom, calls=%fused_computation.clone | custom fusion | bytes 270336 | tf_op jit(solution)/shard_map/jit(_take)/gather | solution.py:55
  183.7 1.9 fusion.315
  186.9 12.1 %scatter_custom_fusion.1 = f32[16,2048]{0,1:T(8,128)S(1)} fusion(s32[2048]{0:T(1024)S(1)} %get-tuple-element.21, f32[2048,16]{1,0:T(8,128)} %copy.12, f32[]{:T(128)} %constant.19.clone.1), kind=kCustom, calls=%fused_computation.518 | custom fusion | flops 32768 | bytes 131584 | tf_op jit(solution)/shard_map/scatter-add | solution.py:61
  199.5 1.6 fusion.306
  201.0 1.5 fusion.290
  203.9 4.1 collective-permute-start.5
  208.0 12.3 %collective-permute-done.4 = f32[10,16,8,128]{3,2,1,0:T(8,128)S(1)} collective-permute-done((f32[10,16,8,128]{3,2,1,0:T(8,128)S(1)}, f32[10,16,8,128]{3,2,1,0:T(8,128)S(1)}, u32[]{:S(2)}, u32[]{:S(2)}) %collective-permute-start.4) | collective-permute-done | bytes 655392 | tf_op jit(solution)/shard_map/ppermute | solution.py:22
  220.3 15.0 %multiply_reduce_fusion.1 = (f32[]{:T(128)}, f32[]{:T(128)}, f32[10,16,16,128]{3,2,1,0:T(8,128)S(1)}) fusion(f32[10,16,16,128]{3,2,1,0:T(8,128)S(1)} %fusion.231, f32[10,16,8,128]{3,2,1,0:T(8,128)S(1)} %collective-permute-done.5, f32[10,16,16,128]{3,2,1,0:T(8,128)S(1)} %fusion.290, f32[]{:T(128)} %bitcast.24, f32[]{:T(128)} %bitcast.23, f32[]{:T(128)} %bitcast.22, ...), kind=kLoop, calls=%fused_computation.510 | loop fusion | flops 17694720 | bytes 5242956 | tf_op jit(solution)/shard_map/reduce_sum | solution.py:106
  235.3 82.6 %all-reduce = (f32[]{:T(128)}, f32[]{:T(128)}) all-reduce(f32[]{:T(128)} %get-tuple-element.4, f32[]{:T(128)} %get-tuple-element.3), channel_id=1, replica_groups=mesh['tile'=32,'ens'=8] {'tile','ens'}, use_global_device_ids=true, to_apply=%region_5.0 | all-reduce | flops 2 | bytes 16 | tf_op jit(solution)/shard_map/psum | solution.py:88
  320.2 72.9 %psum.52 = f32[]{:T(128)} all-reduce(f32[]{:T(128)} %multiply_reduce_fusion), channel_id=1, replica_groups=mesh['tile'=32,'ens'=8] {'tile','ens'}, use_global_device_ids=true, to_apply=%region_13.15 | all-reduce | flops 1 | bytes 8 | tf_op jit(solution)/shard_map/psum | solution.py:88
  394.4 1.5 multiply_add_fusion.1
  395.9 1.6 fusion.303
  397.5 1.5 fusion.288
  399.6 4.4 collective-permute-start.7
  404.0 14.2 %collective-permute-done.6 = f32[10,16,8,128]{3,2,1,0:T(8,128)S(1)} collective-permute-done((f32[10,16,8,128]{3,2,1,0:T(8,128)S(1)}, f32[10,16,8,128]{3,2,1,0:T(8,128)S(1)}, u32[]{:S(2)}, u32[]{:S(2)}) %collective-permute-start.6) | collective-permute-done | bytes 655392 | tf_op jit(solution)/shard_map/ppermute | solution.py:22
  418.1 14.3 %fusion.4 = f32[16,16,128]{2,1,0:T(8,128)S(1)} fusion(bf16[10,16,16,128]{3,2,1,0:T(8,128)(2,1)S(1)} %copy-done, f32[10,16,16,128]{3,2,1,0:T(8,128)S(1)} %fusion.288, f32[10,16,8,128]{3,2,1,0:T(8,128)S(1)} %collective-permute-done.7, f32[10,16,8,128]{3,2,1,0:T(8,128)S(1)} %collective-permute-done.6, f32[]{:T(128)} %bitcast.24, f32[]{:T(128)} %bitcast.23, ...), kind=kLoop, calls=%fused_computation.184 | loop fusion | flops 17006592 | bytes 3407940 | tf_op jit(solution)/shard_map/reduce_sum | solution.py:99
  433.8 64.8 %all-reduce.7.cloned.1.call-done = f32[16,2048]{0,1:T(8,128)} async-done(((f32[16,2048]{0,1:T(8,128)}), f32[16,2048]{0,1:T(8,128)}) %all-reduce.7.cloned.1.call-update) | async-done | bytes 131088 | tf_op jit(solution)/shard_map/psum | solution.py:100
  498.7 8.9 %gather_fusion.1 = f32[2048,16]{1,0:T(8,128)} fusion(f32[16,2048]{0,1:T(8,128)} %all-reduce.7.cloned.1.call-done, s32[2048]{0:T(1024)S(1)} %get-tuple-element.20), kind=kCustom, calls=%fused_computation.1.clone | custom fusion | bytes 270336 | tf_op jit(solution)/shard_map/jit(_take)/gather | solution.py:55
  507.5 2.2 fusion.314
  511.1 13.0 %scatter_custom_fusion.2 = f32[16,2048]{0,1:T(8,128)} fusion(s32[2048]{0:T(1024)} %copy-done.10, f32[2048,16]{1,0:T(8,128)} %copy.16, f32[]{:T(128)} %constant.19.clone.1), kind=kCustom, calls=%fused_computation.516 | custom fusion | flops 32768 | bytes 131584 | tf_op jit(solution)/shard_map/scatter-add | solution.py:61
  524.1 1.5 copy.17
  525.7 1.6 fusion.300
  527.3 1.5 fusion.286
  530.2 4.1 collective-permute-start.9
  534.3 12.3 %collective-permute-done.8 = f32[10,16,8,128]{3,2,1,0:T(8,128)S(1)} collective-permute-done((f32[10,16,8,128]{3,2,1,0:T(8,128)S(1)}, f32[10,16,8,128]{3,2,1,0:T(8,128)S(1)}, u32[]{:S(2)}, u32[]{:S(2)}) %collective-permute-start.8) | collective-permute-done | bytes 655392 | tf_op jit(solution)/shard_map/ppermute | solution.py:22
  546.5 14.9 %fusion = f32[]{:T(128)} fusion(f32[10,16,16,128]{3,2,1,0:T(8,128)S(1)} %multiply_add_fusion.1, f32[10,16,16,128]{3,2,1,0:T(8,128)S(1)} %fusion.286, f32[10,16,8,128]{3,2,1,0:T(8,128)S(1)} %collective-permute-done.9, f32[10,16,8,128]{3,2,1,0:T(8,128)S(1)} %collective-permute-done.8, f32[]{:T(128)} %bitcast.24, f32[]{:T(128)} %bitcast.23, f32[]{:T(128)} %bitcast.22, ...), kind=kLoop, calls=%fused_computation.180 | loop fusion | flops 17039360 | bytes 3932232 | tf_op jit(solution)/shard_map/reduce_sum | solution.py:106
  561.4 82.5 %psum.54 = f32[]{:T(128)} all-reduce(f32[]{:T(128)} %fusion), channel_id=1, replica_groups=mesh['tile'=32,'ens'=8] {'tile','ens'}, use_global_device_ids=true, to_apply=%region_19.21 | all-reduce | flops 1 | bytes 8 | tf_op jit(solution)/shard_map/psum | solution.py:106
  645.4 1.6 fusion.297
  647.0 1.4 fusion.284
  648.7 5.0 collective-permute-start.11
  653.7 13.4 %collective-permute-done.10 = f32[10,16,8,128]{3,2,1,0:T(8,128)S(1)} collective-permute-done((f32[10,16,8,128]{3,2,1,0:T(8,128)S(1)}, f32[10,16,8,128]{3,2,1,0:T(8,128)S(1)}, u32[]{:S(2)}, u32[]{:S(2)}) %collective-permute-start.10) | collective-permute-done | bytes 655392 | tf_op jit(solution)/shard_map/ppermute | solution.py:22
  667.1 14.3 %fusion.6 = f32[16,16,128]{2,1,0:T(8,128)S(1)} fusion(bf16[10,16,16,128]{3,2,1,0:T(8,128)(2,1)S(1)} %copy-done, f32[10,16,16,128]{3,2,1,0:T(8,128)S(1)} %fusion.284, f32[10,16,8,128]{3,2,1,0:T(8,128)S(1)} %collective-permute-done.11, f32[10,16,8,128]{3,2,1,0:T(8,128)S(1)} %collective-permute-done.10, f32[]{:T(128)} %bitcast.24, f32[]{:T(128)} %bitcast.23, ...), kind=kLoop, calls=%fused_computation.186 | loop fusion | flops 17006592 | bytes 3407940 | tf_op jit(solution)/shard_map/reduce_sum | solution.py:112
  682.0 61.6 %all-reduce.9.cloned.1.call-done = f32[16,16,128]{2,1,0:T(8,128)} async-done(((f32[16,16,128]{2,1,0:T(8,128)}), f32[16,16,128]{2,1,0:T(8,128)}) %all-reduce.9.cloned.1.call-update) | async-done | bytes 131088 | tf_op jit(solution)/shard_map/psum | solution.py:113
  743.6 1.6 copy.72
  (75 shorter events, 16.9 us)
Async XLA Ops:
  7.2 167.6 %all-reduce.5.cloned.1.call-start = ((), (), s32[]{:S(2)}) async-start(), calls=%async_computation | async-start | bytes 2097152 | tf_op jit(solution)/shard_map/psum | solution.py:100
  11.2 175.7 %copy-start.10 = (s32[2048]{0:T(1024)}, s32[2048]{0:T(1024)S(1)}, u32[]{:S(2)}) copy-start(s32[2048]{0:T(1024)S(1)} %get-tuple-element.21) | copy-start | bytes 24580
  13.2 12.1 %copy-start = (bf16[10,16,16,128]{3,2,1,0:T(8,128)(2,1)S(1)}, bf16[10,16,16,128]{3,2,1,0:T(8,128)(2,1)}, u32[]{:S(2)}) copy-start(bf16[10,16,16,128]{3,2,1,0:T(8,128)(2,1)} %param.8) | copy-start | bytes 1966084
  28.5 23.2 %collective-permute-start = (f32[10,16,8,128]{3,2,1,0:T(8,128)S(1)}, f32[10,16,8,128]{3,2,1,0:T(8,128)}, u32[]{:S(2)}, u32[]{:S(2)}) collective-permute-start(f32[10,16,8,128]{3,2,1,0:T(8,128)S(1)} %get-tuple-element.18), channel_id=1, source_target_pairs={{0,8},{8,16},{16,24},{24,32},{32,40},{40,48},{48,56},{56,64},{64,7... | collective-permute-start | bytes 1966088 | tf_op jit(solution)/shard_map/ppermute | solution.py:22
  30.7 21.1 %collective-permute-start.1 = (f32[10,16,8,128]{3,2,1,0:T(8,128)S(1)}, f32[10,16,8,128]{3,2,1,0:T(8,128)}, u32[]{:S(2)}, u32[]{:S(2)}) collective-permute-start(f32[10,16,8,128]{3,2,1,0:T(8,128)S(1)} %get-tuple-element.19), channel_id=1, source_target_pairs={{8,0},{16,8},{24,16},{32,24},{40,32},{48,40},{56,48},{64,56},{72,6... | collective-permute-start | bytes 1966088 | tf_op jit(solution)/shard_map/ppermute | solution.py:23
  73.9 18.4 %collective-permute-start.2 = (f32[10,16,8,128]{3,2,1,0:T(8,128)S(1)}, f32[10,16,8,128]{3,2,1,0:T(8,128)S(1)}, u32[]{:S(2)}, u32[]{:S(2)}) collective-permute-start(f32[10,16,8,128]{3,2,1,0:T(8,128)S(1)} %get-tuple-element.16), channel_id=1, source_target_pairs={{0,8},{8,16},{16,24},{24,32},{32,40},{40,48},{48,56},{56,64},{64,7... | collective-permute-start | bytes 1966088 | tf_op jit(solution)/shard_map/ppermute | solution.py:22
  74.0 18.3 %collective-permute-start.3 = (f32[10,16,8,128]{3,2,1,0:T(8,128)S(1)}, f32[10,16,8,128]{3,2,1,0:T(8,128)S(1)}, u32[]{:S(2)}, u32[]{:S(2)}) collective-permute-start(f32[10,16,8,128]{3,2,1,0:T(8,128)S(1)} %get-tuple-element.17), channel_id=1, source_target_pairs={{8,0},{16,8},{24,16},{32,24},{40,32},{48,40},{56,48},{64,56},{72,6... | collective-permute-start | bytes 1966088 | tf_op jit(solution)/shard_map/ppermute | solution.py:23
  106.6 1.7 copy-start.7
  106.6 1.7 copy-start.4
  108.0 390.7 %all-reduce.7.cloned.1.call-start = ((), (), s32[]{:S(2)}) async-start(), calls=%async_computation.1 | async-start | bytes 2097152 | tf_op jit(solution)/shard_map/psum | solution.py:100
  108.3 77.3 %copy-start.8 = (pred[2048]{0:T(1024)(128)(4,1)}, pred[2048]{0:T(1024)(128)(4,1)S(1)}, u32[]{:S(2)}) copy-start(pred[2048]{0:T(1024)(128)(4,1)S(1)} %compare_and_fusion) | copy-start | bytes 6148
  108.6 76.9 %copy-start.2 = (f32[16,2048]{0,1:T(8,128)}, f32[16,2048]{0,1:T(8,128)S(1)}, u32[]{:S(2)}) copy-start(f32[16,2048]{0,1:T(8,128)S(1)} %copy.11) | copy-start | bytes 393220
  183.7 1.9 copy-start.5
  202.7 17.6 %collective-permute-start.4 = (f32[10,16,8,128]{3,2,1,0:T(8,128)S(1)}, f32[10,16,8,128]{3,2,1,0:T(8,128)S(1)}, u32[]{:S(2)}, u32[]{:S(2)}) collective-permute-start(f32[10,16,8,128]{3,2,1,0:T(8,128)S(1)} %get-tuple-element.14), channel_id=1, source_target_pairs={{0,8},{8,16},{16,24},{24,32},{32,40},{40,48},{48,56},{56,64},{64,7... | collective-permute-start | bytes 1966088 | tf_op jit(solution)/shard_map/ppermute | solution.py:22
  203.9 16.3 %collective-permute-start.5 = (f32[10,16,8,128]{3,2,1,0:T(8,128)S(1)}, f32[10,16,8,128]{3,2,1,0:T(8,128)S(1)}, u32[]{:S(2)}, u32[]{:S(2)}) collective-permute-start(f32[10,16,8,128]{3,2,1,0:T(8,128)S(1)} %get-tuple-element.15), channel_id=1, source_target_pairs={{8,0},{16,8},{24,16},{32,24},{40,32},{48,40},{56,48},{64,56},{72,6... | collective-permute-start | bytes 1966088 | tf_op jit(solution)/shard_map/ppermute | solution.py:23
  235.3 84.9 %copy-start.1 = (f32[10,16,16,128]{3,2,1,0:T(8,128)}, f32[10,16,16,128]{3,2,1,0:T(8,128)S(1)}, u32[]{:S(2)}) copy-start(f32[10,16,16,128]{3,2,1,0:T(8,128)S(1)} %get-tuple-element.7) | copy-start | bytes 3932164
  399.1 19.0 %collective-permute-start.6 = (f32[10,16,8,128]{3,2,1,0:T(8,128)S(1)}, f32[10,16,8,128]{3,2,1,0:T(8,128)S(1)}, u32[]{:S(2)}, u32[]{:S(2)}) collective-permute-start(f32[10,16,8,128]{3,2,1,0:T(8,128)S(1)} %get-tuple-element.12), channel_id=1, source_target_pairs={{0,8},{8,16},{16,24},{24,32},{32,40},{40,48},{48,56},{56,64},{64,7... | collective-permute-start | bytes 1966088 | tf_op jit(solution)/shard_map/ppermute | solution.py:22
  399.6 18.5 %collective-permute-start.7 = (f32[10,16,8,128]{3,2,1,0:T(8,128)S(1)}, f32[10,16,8,128]{3,2,1,0:T(8,128)S(1)}, u32[]{:S(2)}, u32[]{:S(2)}) collective-permute-start(f32[10,16,8,128]{3,2,1,0:T(8,128)S(1)} %get-tuple-element.13), channel_id=1, source_target_pairs={{8,0},{16,8},{24,16},{32,24},{40,32},{48,40},{56,48},{64,56},{72,6... | collective-permute-start | bytes 1966088 | tf_op jit(solution)/shard_map/ppermute | solution.py:23
  433.8 73.8 %copy-start.9 = (pred[2048]{0:T(1024)(128)(4,1)S(1)}, pred[2048]{0:T(1024)(128)(4,1)}, u32[]{:S(2)}) copy-start(pred[2048]{0:T(1024)(128)(4,1)} %copy-done.8) | copy-start | bytes 6148
  433.8 309.8 %all-reduce.9.cloned.1.call-start = ((), (), s32[]{:S(2)}) async-start(), calls=%async_computation.2 | async-start | bytes 262144 | tf_op jit(solution)/shard_map/psum | solution.py:113
  507.5 2.2 copy-start.6
  528.9 17.6 %collective-permute-start.8 = (f32[10,16,8,128]{3,2,1,0:T(8,128)S(1)}, f32[10,16,8,128]{3,2,1,0:T(8,128)S(1)}, u32[]{:S(2)}, u32[]{:S(2)}) collective-permute-start(f32[10,16,8,128]{3,2,1,0:T(8,128)S(1)} %get-tuple-element.10), channel_id=1, source_target_pairs={{0,8},{8,16},{16,24},{24,32},{32,40},{40,48},{48,56},{56,64},{64,7... | collective-permute-start | bytes 1966088 | tf_op jit(solution)/shard_map/ppermute | solution.py:22
  530.2 16.3 %collective-permute-start.9 = (f32[10,16,8,128]{3,2,1,0:T(8,128)S(1)}, f32[10,16,8,128]{3,2,1,0:T(8,128)S(1)}, u32[]{:S(2)}, u32[]{:S(2)}) collective-permute-start(f32[10,16,8,128]{3,2,1,0:T(8,128)S(1)} %get-tuple-element.11), channel_id=1, source_target_pairs={{8,0},{16,8},{24,16},{32,24},{40,32},{48,40},{56,48},{64,56},{72,6... | collective-permute-start | bytes 1966088 | tf_op jit(solution)/shard_map/ppermute | solution.py:23
  645.4 1.6 copy-start.3
  648.6 18.5 %collective-permute-start.10 = (f32[10,16,8,128]{3,2,1,0:T(8,128)S(1)}, f32[10,16,8,128]{3,2,1,0:T(8,128)S(1)}, u32[]{:S(2)}, u32[]{:S(2)}) collective-permute-start(f32[10,16,8,128]{3,2,1,0:T(8,128)S(1)} %get-tuple-element.8), channel_id=1, source_target_pairs={{0,8},{8,16},{16,24},{24,32},{32,40},{40,48},{48,56},{56,64},{64,7... | collective-permute-start | bytes 1966088 | tf_op jit(solution)/shard_map/ppermute | solution.py:22
  648.7 18.4 %collective-permute-start.11 = (f32[10,16,8,128]{3,2,1,0:T(8,128)S(1)}, f32[10,16,8,128]{3,2,1,0:T(8,128)S(1)}, u32[]{:S(2)}, u32[]{:S(2)}) collective-permute-start(f32[10,16,8,128]{3,2,1,0:T(8,128)S(1)} %get-tuple-element.9), channel_id=1, source_target_pairs={{8,0},{16,8},{24,16},{32,24},{40,32},{48,40},{56,48},{64,56},{72,6... | collective-permute-start | bytes 1966088 | tf_op jit(solution)/shard_map/ppermute | solution.py:23
Sparse Core Ops, SparseCore 0:
  108.1 66.6 all-reduce.4
  433.9 64.7 all-reduce.6
  682.2 61.4 all-reduce.8
where the time goes:
time: 760 us; the launch traced here: 752 us
  waiting for transfers between devices  270 us (36%)
  blocking collectives  238 us (31%)
  other arithmetic  141 us (19%)
  starting transfers between devices  34.8 us (5%)
  local copies, waits for them, and re-layouts  28.9 us (4%)
  between operations  21.1 us (3%)
  matrix products  18.1 us (2%)
    psum x2, blocking collectives, norm_squared(): return lax.psum(jnp.sum(field * field), ('tile', 'ens'))  155 us
    psum x2, waiting for transfers between devices, local(): summed = lax.psum(partial_value, 'ens')  131 us
    psum x1, blocking collectives, local(): lax.psum(jnp.sum(direction * applied), ('tile', 'ens'))  82.5 us
    ppermute x6, waiting for transfers between devices, with_halo(): before = lax.ppermute(last, axis, up)  77.8 us
    psum x1, waiting for transfers between devices, local(): increment = lax.psum(final_partial, 'ens')  61.6 us
    scatter-add x3, other arithmetic, observe_adjoint(): jnp.zeros((weights.shape[0], cell_total), jnp.float32).at[:, cell_ids]  36.8 us
    reduce_sum x2, other arithmetic, local(): jnp.sum(direction * applied)  29.9 us
    ppermute x6, starting transfers between devices, with_halo(): after = lax.ppermute(initial, axis, down)  29.1 us
  transfers between devices with their start and end apart: 15, of which 9 were waited for; matrix products, arithmetic and copies ran while one was open for 0% of the time, Pallas kernels for 0%

commit v1 on v0

v1 whole, which is shorter than its diff:
```python
import math

import jax
import jax.numpy as jnp
import numpy as np
from jax import lax
from jax.experimental import pallas as pl
from jax.experimental.pallas import tpu as pltpu
from jax.sharding import PartitionSpec as P

F32 = jnp.float32
BF16 = jnp.bfloat16
VERTICAL_SPREAD = 2.0
VMEM_LIMIT = 40 * 1024 * 1024


def gauss(radius, spread):
    offsets = np.arange(-radius, radius + 1) / spread
    return np.exp(-offsets * offsets)


def band(length, spread):
    position = np.arange(length)
    spacing = (position[:, None] - position[None, :]) / spread
    return np.exp(-spacing * spacing) / np.sqrt(np.sum(gauss(length, spread) ** 2))


def bf16_pair(matrix):
    matrix = matrix.astype(np.float32)
    high = matrix.astype(jnp.bfloat16)
    low = (matrix - high.astype(np.float32)).astype(jnp.bfloat16)
    return high, low


def local_matrices(levels, rows, columns, power, scale):
    radius = rows // 2
    kernel = gauss(radius, float(radius))
    kernel = kernel / np.sqrt(np.sum(kernel * kernel))
    vertical = band(levels, VERTICAL_SPREAD)
    lateral = band(columns, columns / 16.0)
    if power == 2:
        kernel = np.convolve(kernel, kernel)
        vertical = vertical @ vertical
        lateral = lateral @ lateral
    reach = (len(kernel) - 1) // 2
    blocks = []
    for tile in (-1, 0, 1):
        offset = tile * rows + np.arange(rows)[None, :] - np.arange(rows)[:, None]
        inside = np.abs(offset) <= reach
        along = np.where(inside, kernel[np.clip(offset + reach, 0, 2 * reach)], 0.0)
        blocks.append(np.kron(vertical, along))
    rows_high, rows_low = bf16_pair(np.concatenate(blocks, axis=1) * scale)
    pair_high, pair_low = bf16_pair(np.kron(np.eye(2), lateral))
    return np.concatenate([rows_high, rows_low], axis=0), pair_high, pair_low


def split(x):
    high = x.astype(BF16)
    return high, (x - high.astype(F32)).astype(BF16)


def dot(a, b):
    return jnp.dot(a, b, preferred_element_type=F32)


def column_hits(cell, columns):
    return jnp.where(
        lax.broadcasted_iota(jnp.int32, (columns, cell.shape[1]), 0) == cell % columns, 1.0, 0.0
    ).astype(BF16)


def adjoint(values, weights_ref, cell_ref, rows, columns):
    levels, slots = weights_ref.shape
    total = levels * rows
    chunk = 256
    field = jnp.zeros((2 * total, columns), F32)
    for start in range(0, slots, chunk):
        cell = cell_ref[:, start : start + chunk]
        hits = column_hits(cell, columns)
        here = lax.broadcasted_iota(jnp.int32, (rows, chunk), 0) == cell // columns
        weighted = weights_ref[:, start : start + chunk] * values[:, start : start + chunk]
        parts = [jnp.where(here, weighted[level : level + 1], 0.0) for level in range(levels)]
        high, low = split(jnp.concatenate(parts, axis=0))
        both = jnp.concatenate([high, low], axis=0)
        field = field + lax.dot_general(both, hits, (((1,), (1,)), ((), ())), preferred_element_type=F32)
    return field[:total] + field[total:]


def observe(field, weights_ref, cell_ref, live, rows, columns):
    levels, slots = weights_ref.shape
    chunk = 256
    high, low = split(field)
    both = jnp.concatenate([high, low], axis=1)
    observed = []
    for start in range(0, slots, chunk):
        cell = cell_ref[:, start : start + chunk]
        hits = column_hits(cell, columns)
        picked = dot(both, jnp.concatenate([hits, hits], axis=0))
        here = lax.broadcasted_iota(jnp.int32, (rows, chunk), 0) == cell // columns
        total = jnp.zeros((rows, chunk), F32)
        for level in range(levels):
            weight = weights_ref[level : level + 1, start : start + chunk]
            total = total + jnp.where(here, picked[level * rows : (level + 1) * rows], 0.0) * weight
        observed.append(jnp.sum(total, axis=0, keepdims=True))
    return jnp.concatenate(observed, axis=1) * live


def live_slots(count_ref, slots):
    return jnp.where(lax.broadcasted_iota(jnp.int32, (1, slots), 1) < count_ref[0], 1.0, 0.0)


def localized(first, p_refs, g_refs, rows_ref, pair_high_ref, pair_low_ref):
    total = g_refs[0].shape[0]
    sides = []
    for member in (first, first + 1):
        sides.append(jnp.concatenate([p[member].astype(F32) * g[...] for p, g in zip(p_refs, g_refs)], axis=0))
    high, low = split(jnp.concatenate(sides, axis=1))
    mixed = dot(rows_ref[...], high)
    mixed = mixed[:total] + mixed[total:] + dot(rows_ref[:total], low)
    high, low = split(mixed)
    across = dot(jnp.concatenate([high, low], axis=0), pair_high_ref[...])
    return across[:total] + across[total:] + dot(high, pair_low_ref[...])


def as_rows(line, width=128):
    return jnp.concatenate([line[:, i : i + width] for i in range(0, line.shape[1], width)], axis=0)


def as_line(block):
    return jnp.concatenate([block[i : i + 1] for i in range(block.shape[0])], axis=1)


def start_kernel(rows, columns, count, weights, cell, precision, innovations, field):
    live = live_slots(count, weights.shape[1])
    values = live * precision[...] * innovations[...]
    field[...] = adjoint(values, weights, cell, rows, columns)


def forward_kernel(rows, columns, count, p0, p1, p2, g0, g1, g2, mix, pair_high, pair_low, weights, cell, message):
    members = p0.shape[0]
    field = jnp.zeros(g0.shape, F32)
    for first in range(0, members, 2):
        spread = localized(first, (p0, p1, p2), (g0, g1, g2), mix, pair_high, pair_low)
        field = field + p1[first].astype(F32) * spread[:, :columns] + p1[first + 1].astype(F32) * spread[:, columns:]
    observed = as_rows(observe(field, weights, cell, live_slots(count, weights.shape[1]), rows, columns))
    peers = message.shape[0]
    lines = observed.shape[0]
    share = field.shape[0] // peers
    for peer in range(peers):
        message[peer, :lines] = observed
        message[peer, lines:] = field[peer * share : (peer + 1) * share]


def middle_kernel(rows, columns, count, message, weights, cell, precision, field, observed, share):
    summed = jnp.sum(message[...], axis=0)
    lines = observed.shape[0]
    observed[...] = summed[:lines]
    share[...] = summed[lines:]
    values = precision[...] * as_line(summed[:lines])
    field[...] = adjoint(values, weights, cell, rows, columns)


def alpha_kernel(p0, p1, p2, g0, g1, g2, mix, pair_high, pair_low, alpha):
    columns = g0.shape[1]
    for first in range(0, p0.shape[0], 2):
        spread = localized(first, (p0, p1, p2), (g0, g1, g2), mix, pair_high, pair_low)
        alpha[first] = spread[:, :columns]
        alpha[first + 1] = spread[:, columns:]


def scalars_kernel(count, message, once, precision, innovations, scalars, share):
    summed = jnp.sum(message[...], axis=0)
    lines = once.shape[0]
    share[...] = summed[lines:]
    z2 = summed[:lines]
    z1 = once[...]
    rho = precision[...]
    slot = lax.broadcasted_iota(jnp.int32, rho.shape, 0) * rho.shape[1] + lax.broadcasted_iota(jnp.int32, rho.shape, 1)
    c = jnp.where(slot < count[0], rho * innovations[...], 0.0)

    def total(x):
        return jnp.sum(jnp.sum(x, axis=0, keepdims=True), axis=1, keepdims=True)

    d = c + rho * z1
    e = z1 + z2
    size = total(d * d)
    shift = jnp.where(size > 0.0, total(c * d) / jnp.where(size > 0.0, size, 1.0), 0.0)
    v = c - shift * d
    w = z1 - shift * e
    values = [
        shift,
        total(c * z1),
        total(d * z1),
        total(v * w),
        total(v * e + d * w),
        total(d * e),
        total(v * z1 + c * w),
        total(d * z1 + c * e),
        total(rho * w * w),
        total(rho * w * e),
        total(rho * e * e),
        total(rho * w * z1),
        total(rho * e * z1),
        total(rho * z1 * z1),
    ]
    lane = lax.broadcasted_iota(jnp.int32, (1, scalars.shape[1]), 1)
    line = jnp.zeros((1, scalars.shape[1]), F32)
    for i, value in enumerate(values):
        line = jnp.where(lane == i, value, line)
    scalars[...] = jnp.broadcast_to(line, scalars.shape)


def final_kernel(scalars, alpha0, alpha1, inc0, inc1, alpha, increment):
    table = scalars[...]

    def column(i):
        return table[:, i : i + 1]

    def total(x):
        return jnp.sum(x, axis=0, keepdims=True)

    cz = total(column(1))
    step0 = cz / total(column(2))
    delta = step0 - column(0)
    rr1 = total(column(3) - delta * column(4) + delta * delta * column(5))
    beta = rr1 / cz
    pq1 = rr1 + beta * total(column(6) - delta * column(7)) + beta * beta * cz
    pq1 = pq1 + total(column(8) - 2.0 * delta * column(9) + delta * delta * column(10))
    pq1 = pq1 + 2.0 * beta * total(column(11) - delta * column(12)) + beta * beta * total(column(13))
    step1 = rr1 / pq1
    first = step0 + step1 * (1.0 - step0 + beta)
    second = -step1 * step0
    increment[...] = first * inc0[...] + second * inc1[...]
    for member in range(alpha.shape[0]):
        alpha[member] = first * alpha0[member] + second * alpha1[member]


def call(kernel, outs, *args):
    smem = [0] if args[0].dtype == jnp.int32 and args[0].shape == (1,) else []
    vmem = pl.BlockSpec(memory_space=pltpu.VMEM)
    single = not isinstance(outs, list)
    shapes = [jax.ShapeDtypeStruct(shape, F32) for shape in ([outs] if single else outs)]
    return pl.pallas_call(
        kernel,
        out_shape=shapes[0] if single else shapes,
        in_specs=[pl.BlockSpec(memory_space=pltpu.SMEM) if i in smem else vmem for i in range(len(args))],
        out_specs=vmem if single else [vmem] * len(shapes),
        compiler_params=pltpu.CompilerParams(vmem_limit_bytes=VMEM_LIMIT),
    )(*args)


def neighbours(x):
    size = lax.axis_size("tile")
    up = [(i, (i + 1) % size) for i in range(size)]
    down = [(j, i) for i, j in up]
    return lax.ppermute(x, "tile", up), lax.ppermute(x, "tile", down)


def local(perturbations, innovations, obs_precision, obs_weights, obs_cell, obs_count):
    members, levels, rows, columns = perturbations.shape
    slots = obs_cell.shape[0]
    cells = levels * rows
    ens, tiles = lax.axis_size("ens"), lax.axis_size("tile")
    everyone = ens * members
    lines = slots // 128
    share = cells // ens
    mix2, high2, low2 = local_matrices(levels, rows, columns, 2, 1.0 / everyone)
    mix1, high1, low1 = local_matrices(levels, rows, columns, 1, 1.0 / math.sqrt(everyone))

    p = perturbations.reshape(members, cells, columns)
    p_before, p_after = neighbours(p)
    cell = obs_cell.reshape(1, slots)
    precision = obs_precision.reshape(1, slots)
    innovations_line = innovations.reshape(1, slots)
    shape = (rows, columns)

    def bound(kernel):
        def run(*refs):
            kernel(*shape, *refs)

        return run

    def forward(g, g_before, g_after):
        return call(
            bound(forward_kernel), (ens, lines + share, columns),
            obs_count, p_before, p, p_after, g_before, g, g_after, mix2, high2, low2, obs_weights, cell,
        )

    def alpha_of(g, g_before, g_after):
        return call(
            alpha_kernel, (members, cells, columns),
            p_before, p, p_after, g_before, g, g_after, mix1, high1, low1,
        )

    g0 = call(bound(start_kernel), (cells, columns), obs_count, obs_weights, cell, precision, innovations_line)
    g0_before, g0_after = neighbours(g0)
    message = lax.all_to_all(forward(g0, g0_before, g0_after), "ens", 0, 0)
    g1, once, share0 = call(
        bound(middle_kernel), [(cells, columns), (lines, 128), (share, columns)],
        obs_count, message, obs_weights, cell, precision,
    )
    g1_before, g1_after = neighbours(g1)
    alpha0 = alpha_of(g0, g0_before, g0_after)
    message = lax.all_to_all(forward(g1, g1_before, g1_after), "ens", 0, 0)
    scalars, share1 = call(
        scalars_kernel, [(tiles, 128), (share, columns)],
        obs_count, message, once, obs_precision.reshape(lines, 128), innovations.reshape(lines, 128),
    )
    alpha1 = alpha_of(g1, g1_before, g1_after)
    both = jnp.concatenate([share0, share1], axis=0)
    both = lax.all_to_all(jnp.broadcast_to(both[None], (ens,) + both.shape), "ens", 0, 0)
    inc0 = both[:, :share].reshape(cells, columns)
    inc1 = both[:, share:].reshape(cells, columns)
    scalars = lax.all_to_all(scalars, "tile", 0, 0, tiled=True)
    alpha, increment = call(
        final_kernel, [(members, cells, columns), (cells, columns)],
        scalars, alpha0, alpha1, inc0, inc1,
    )
    return alpha.reshape(perturbations.shape), increment.reshape(levels, rows, columns)


def solution(mesh):
    placed = (
        P("ens", None, "tile", None),
        P("tile"),
        P("tile"),
        P(None, "tile"),
        P("tile"),
        P("tile"),
    )
    return jax.shard_map(
        local,
        mesh=mesh,
        in_specs=placed,
        out_specs=(P("ens", None, "tile", None), P(None, "tile", None)),
        check_vma=False,
    )
```

time: 760 us -> 113 us (0.15)
  waiting for transfers between devices: 270 us -> 17.7 us
  blocking collectives: 238 us -> 21.9 us
  other arithmetic: 141 us -> 0.01 us
  Pallas kernels: 0 us -> 22.9 us
  between operations: 21.1 us -> 1.54 us
  matrix products: 18.1 us -> 0 us
  local copies, waits for them, and re-layouts: 28.9 us -> 15.7 us
    psum x3 -> x0, blocking collectives: 238 us -> none  [the longest x2 155 us: norm_squared(): return lax.psum(jnp.sum(field * field), ('tile', 'ens'))]
    psum x3 -> x0, waiting for transfers between devices: 193 us -> none  [the longest x2 131 us: local(): summed = lax.psum(partial_value, 'ens')]
    reduce_sum x11 -> x0, other arithmetic: 79.6 us -> none  [the longest x2 29.9 us: local(): jnp.sum(direction * applied)]
    ppermute x12 -> x6, waiting for transfers between devices: 77.8 us -> 10.2 us  [neighbours(): return (lax.ppermute(x, 'tile', up), lax.ppermute(x, 'tile', down))]
    scatter-add x3 -> x0, other arithmetic: 36.8 us -> none  [observe_adjoint(): jnp.zeros((weights.shape[0], cell_total), jnp.float32).at[:, cell_ids]]
    pallas_call x0 -> x8, Pallas kernels: none -> 22.9 us  [call(): pl.pallas_call(kernel, out_shape=shapes[0] if single else shapes, in_spec...]
    all_to_all x0 -> x2, blocking collectives: none -> 21.9 us  [the longest x1 11.4 us: local(): message = lax.all_to_all(forward(g0, g0_before, g0_after), 'ens', 0, 0)]
    add x3 -> x0, other arithmetic: 20.6 us -> none  [the longest x1 18.9 us: along_x(): result + kernel[offset] * lax.slice_in_dim(padded, offset, offset + row_c...]
  transfers between devices with their start and end apart: 15 -> 8, of which waited for: 9 -> 3; matrix products, arithmetic and copies ran while one was open for 0% -> 1% of each run, Pallas kernels for 0% -> 8%
where the time goes in v1:
time: 113 us; the launch traced here: 112 us
  starting transfers between devices  31.9 us (28%)
  Pallas kernels  22.9 us (20%)
  blocking collectives  21.9 us (19%)
  waiting for transfers between devices  17.7 us (16%)
  local copies, waits for them, and re-layouts  15.7 us (14%)
  between operations  1.54 us (1%)
    pallas_call x8, Pallas kernels, call(): pl.pallas_call(kernel, out_shape=shapes[0] if single else shapes, in_spec...  22.9 us
    ppermute x6, starting transfers between devices, neighbours(): return (lax.ppermute(x, 'tile', up), lax.ppermute(x, 'tile', down))  18.8 us
    unnamed x60, local copies, waits for them, and re-layouts  14 us
    all_to_all x1, blocking collectives, local(): message = lax.all_to_all(forward(g0, g0_before, g0_after), 'ens', 0, 0)  11.4 us
    all_to_all x1, blocking collectives, local(): message = lax.all_to_all(forward(g1, g1_before, g1_after), 'ens', 0, 0)  10.5 us
    ppermute x6, waiting for transfers between devices, neighbours(): return (lax.ppermute(x, 'tile', up), lax.ppermute(x, 'tile', down))  10.2 us
    all_to_all x1, starting transfers between devices, local(): scalars = lax.all_to_all(scalars, 'tile', 0, 0, tiled=True)  8.22 us
    all_to_all x1, waiting for transfers between devices, local(): scalars = lax.all_to_all(scalars, 'tile', 0, 0, tiled=True)  7.44 us
  transfers between devices with their start and end apart: 8, of which 3 were waited for; matrix products, arithmetic and copies ran while one was open for 1% of the time, Pallas kernels for 8%

profile of v1, /device:TPU:1, one launch (start us, length us, event | category | flops | bytes accessed | tf_op | source)
XLA Modules:
  0.0 111.6 jit_solution(17940906863669175905)
XLA Ops:
  0.6 2.1 %collective-permute-start = (bf16[10,256,128]{2,1,0:T(8,128)(2,1)}, bf16[10,256,128]{2,1,0:T(8,128)(2,1)S(1)}, u32[]{:S(2)}, u32[]{:S(2)}) collective-permute-start(bf16[10,256,128]{2,1,0:T(8,128)(2,1)} %bitcast.14), channel_id=1, source_target_pairs={{0,8},{8,16},{16,24},{24,32},{32,40},{40,48},{48,56},{56,64},{64,7... | collective-permute-start | bytes 1966088 | tf_op jit(solution)/shard_map/ppermute | solution.py:256
  2.7 6.7 %collective-permute-start.1 = (bf16[10,256,128]{2,1,0:T(8,128)(2,1)}, bf16[10,256,128]{2,1,0:T(8,128)(2,1)S(1)}, u32[]{:S(2)}, u32[]{:S(2)}) collective-permute-start(bf16[10,256,128]{2,1,0:T(8,128)(2,1)} %bitcast.15), channel_id=1, source_target_pairs={{8,0},{16,8},{24,16},{32,24},{40,32},{48,40},{56,48},{64,56},{72,6... | collective-permute-start | bytes 1966088 | tf_op jit(solution)/shard_map/ppermute | solution.py:256
  10.1 0.9 copy-done.7
  11.0 0.7 copy-done.25
  11.7 0.7 copy-done.26
  12.4 0.7 copy-done.28
  13.1 0.7 shard_map.131.refs_5_.g1
  13.8 0.1 collective-permute-start.2
  13.9 4.8 %collective-permute-start.3 = (f32[256,128]{1,0:T(8,128)S(1)}, f32[256,128]{1,0:T(8,128)S(1)}, u32[]{:S(2)}, u32[]{:S(2)}) collective-permute-start(f32[256,128]{1,0:T(8,128)S(1)} %shard_map.131.refs_5_.g1), channel_id=1, source_target_pairs={{8,0},{16,8},{24,16},{32,24},{40,32},{48,40},{56,48},{64,56},{72,6... | collective-permute-start | bytes 393224 | tf_op jit(solution)/shard_map/ppermute | solution.py:256
  18.6 8.1 %collective-permute-done.2.refs_4_.g0 = f32[256,128]{1,0:T(8,128)S(1)} collective-permute-done((f32[256,128]{1,0:T(8,128)S(1)}, f32[256,128]{1,0:T(8,128)S(1)}, u32[]{:S(2)}, u32[]{:S(2)}) %collective-permute-start.2) | collective-permute-done | bytes 131104 | tf_op jit(solution)/shard_map/ppermute | solution.py:256
  26.8 0.0 collective-permute-done.3.refs_6_.g2
  26.8 0.0 collective-permute-done.refs_1_.p0
  26.8 0.0 collective-permute-done.1.refs_3_.p2
  26.8 0.0 copy-start
  26.8 1.2 %copy-done = bf16[10,16,16,128]{3,2,1,0:T(8,128)(2,1)S(1)} copy-done((bf16[10,16,16,128]{3,2,1,0:T(8,128)(2,1)S(1)}, bf16[10,16,16,128]{3,2,1,0:T(8,128)(2,1)}, u32[]{:S(2)}) %copy-start) | copy-done | bytes 655384
  28.0 1.1 %copy-done.5 = bf16[512,768]{1,0:T(8,128)(2,1)S(1)} copy-done((bf16[512,768]{1,0:T(8,128)(2,1)S(1)}, bf16[512,768]{1,0:T(8,128)(2,1)}, u32[]{:S(2)}) %copy-start.5) | copy-done | bytes 786456
  29.1 0.9 copy-done.15
  30.0 0.9 copy-done.17
  30.9 5.2 %shard_map.132 = f32[8,48,128]{2,1,0:T(8,128)S(1)} custom-call(s32[1]{0:T(128)S(6)} %copy.15.refs_0_.count, bf16[10,256,128]{2,1,0:T(8,128)(2,1)S(1)} %collective-permute-done.refs_1_.p0, bf16[10,256,128]{2,1,0:T(8,128)(2,1)S(1)} %bitcast.16, bf16[10,256,128]{2,1,0:T(8,128)(2,1)S(1)} %collective-permute-done.1.refs_3_.p2, ...), custom_call_target="tpu_custom_call" | custom-call | tf_op jit(solution)/shard_map/pallas_call | solution.py:243
  36.1 0.0 copy-done.11
  36.1 11.4 %all_to_all.26.refs_1_ = f32[8,48,128]{2,1,0:T(8,128)S(1)} all-to-all(f32[8,48,128]{2,1,0:T(8,128)S(1)} %shard_map.132), channel_id=1, replica_groups=mesh['tile'=32,'ens'=8] {'ens'}, dimensions={0} | all-to-all | bytes 393216 | tf_op jit(solution)/shard_map/all_to_all | solution.py:297
  47.5 0.7 shard_map.133
  48.2 0.0 copy-start.27
  48.3 0.0 copy-start.29
  48.3 0.1 collective-permute-start.4
  48.4 5.1 %collective-permute-start.5 = (f32[256,128]{1,0:T(8,128)S(1)}, f32[256,128]{1,0:T(8,128)S(1)}, u32[]{:S(2)}, u32[]{:S(2)}) collective-permute-start(f32[256,128]{1,0:T(8,128)S(1)} %get-tuple-element.9.refs_5_.g1), channel_id=1, source_target_pairs={{8,0},{16,8},{24,16},{32,24},{40,32},{48,40},{56,48},{64,56},{72,6... | collective-permute-start | bytes 393224 | tf_op jit(solution)/shard_map/ppermute | solution.py:256
  53.4 2.1 %collective-permute-done.4.refs_4_.g0 = f32[256,128]{1,0:T(8,128)S(1)} collective-permute-done((f32[256,128]{1,0:T(8,128)S(1)}, f32[256,128]{1,0:T(8,128)S(1)}, u32[]{:S(2)}, u32[]{:S(2)}) %collective-permute-start.4) | collective-permute-done | bytes 131104 | tf_op jit(solution)/shard_map/ppermute | solution.py:256
  55.5 0.0 collective-permute-done.5.refs_6_.g2
  55.6 5.2 %shard_map.134 = f32[8,48,128]{2,1,0:T(8,128)S(1)} custom-call(s32[1]{0:T(128)S(6)} %copy.15.refs_0_.count, bf16[10,256,128]{2,1,0:T(8,128)(2,1)S(1)} %collective-permute-done.refs_1_.p0, bf16[10,256,128]{2,1,0:T(8,128)(2,1)S(1)} %bitcast.17, bf16[10,256,128]{2,1,0:T(8,128)(2,1)S(1)} %collective-permute-done.1.refs_3_.p2, ...), custom_call_target="tpu_custom_call" | custom-call | tf_op jit(solution)/shard_map/pallas_call | solution.py:243
  60.8 0.6 copy-done.21
  61.4 10.5 %all_to_all.27.message = f32[8,48,128]{2,1,0:T(8,128)S(1)} all-to-all(f32[8,48,128]{2,1,0:T(8,128)S(1)} %shard_map.134), channel_id=1, replica_groups=mesh['tile'=32,'ens'=8] {'ens'}, dimensions={0} | all-to-all | bytes 393216 | tf_op jit(solution)/shard_map/all_to_all | solution.py:304
  71.9 0.8 shard_map.135
  72.7 0.7 broadcast_in_dim.2
  73.4 4.9 %all-to-all-start.3 = ((f32[8,64,128]{2,1,0:T(8,128)}), f32[8,64,128]{2,1,0:T(8,128)}, u32[]{:S(2)}, u32[]{:S(2)}) async-start(f32[8,64,128]{2,1,0:T(8,128)} %broadcast_in_dim.2), calls=%async_computation.3 | async-start | bytes 524288 | tf_op jit(solution)/shard_map/all_to_all | solution.py:311
  78.3 1.1 %copy-done.4 = bf16[512,768]{1,0:T(8,128)(2,1)S(1)} copy-done((bf16[512,768]{1,0:T(8,128)(2,1)S(1)}, bf16[512,768]{1,0:T(8,128)(2,1)}, u32[]{:S(2)}) %copy-start.4) | copy-done | bytes 786456
  79.4 0.9 copy-done.9
  80.3 0.9 copy-done.12
  81.2 0.9 copy-done.14
  82.1 4.3 %shard_map.136.alpha0 = f32[10,256,128]{2,1,0:T(8,128)S(1)} custom-call(bf16[10,256,128]{2,1,0:T(8,128)(2,1)S(1)} %collective-permute-done.refs_1_.p0, bf16[10,256,128]{2,1,0:T(8,128)(2,1)S(1)} %bitcast.18, bf16[10,256,128]{2,1,0:T(8,128)(2,1)S(1)} %collective-permute-done.1.refs_3_.p2, f32[256,128]{1,0:T(8,128)S(1)} %copy-done.12, ...), custom_call_target="tpu_custom_call" | custom-call | tf_op jit(solution)/shard_map/pallas_call | solution.py:243
  86.5 4.3 %shard_map.137.alpha1 = f32[10,256,128]{2,1,0:T(8,128)S(1)} custom-call(bf16[10,256,128]{2,1,0:T(8,128)(2,1)S(1)} %collective-permute-done.refs_1_.p0, bf16[10,256,128]{2,1,0:T(8,128)(2,1)S(1)} %bitcast.19, bf16[10,256,128]{2,1,0:T(8,128)(2,1)S(1)} %collective-permute-done.1.refs_3_.p2, f32[256,128]{1,0:T(8,128)S(1)} %copy-done.22, ...), custom_call_target="tpu_custom_call" | custom-call | tf_op jit(solution)/shard_map/pallas_call | solution.py:243
  90.8 0.0 copy-start.2
  90.8 1.0 copy-done.2
  91.9 0.0 all-to-all-done.3
  91.9 8.2 %all-to-all-start.2 = ((f32[32,1,128]{2,1,0:T(1,128)}), f32[32,1,128]{2,1,0:T(1,128)S(1)}, u32[]{:S(2)}, u32[]{:S(2)}) async-start(f32[32,1,128]{2,1,0:T(1,128)} %bitcast.7), calls=%async_computation.2 | async-start | bytes 32768 | tf_op jit(solution)/shard_map/all_to_all | solution.py:314
  100.1 1.0 fusion
  101.1 7.4 %all-to-all-done.2 = f32[32,1,128]{2,1,0:T(1,128)S(1)} async-done(((f32[32,1,128]{2,1,0:T(1,128)}), f32[32,1,128]{2,1,0:T(1,128)S(1)}, u32[]{:S(2)}, u32[]{:S(2)}) %all-to-all-start.2) | async-done | bytes 16416 | tf_op jit(solution)/shard_map/all_to_all | solution.py:314
  108.6 1.3 %copy-done.3 = f32[10,256,128]{2,1,0:T(8,128)S(1)} copy-done((f32[10,256,128]{2,1,0:T(8,128)S(1)}, f32[10,256,128]{2,1,0:T(8,128)}, u32[]{:S(2)}) %copy-start.3) | copy-done | bytes 1310744
  109.9 1.8 %shard_map.138 = (f32[10,256,128]{2,1,0:T(8,128)}, f32[256,128]{1,0:T(8,128)}) custom-call(f32[32,128]{1,0:T(8,128)S(1)} %bitcast.29, f32[10,256,128]{2,1,0:T(8,128)S(1)} %shard_map.136.alpha0, f32[10,256,128]{2,1,0:T(8,128)S(1)} %copy-done.3, f32[256,128]{1,0:T(8,128)S(1)} %bitcast.21, f32[256,128]{1,0:T(8,128)S(1)} %bitcast.20), custom_call_target="tpu_custom_call" | custom-call | tf_op jit(solution)/shard_map/pallas_call | solution.py:243
  (41 shorter events, 0.1 us)
Async XLA Ops:
  0.6 26.2 %collective-permute-start = (bf16[10,256,128]{2,1,0:T(8,128)(2,1)}, bf16[10,256,128]{2,1,0:T(8,128)(2,1)S(1)}, u32[]{:S(2)}, u32[]{:S(2)}) collective-permute-start(bf16[10,256,128]{2,1,0:T(8,128)(2,1)} %bitcast.14), channel_id=1, source_target_pairs={{0,8},{8,16},{16,24},{24,32},{32,40},{40,48},{48,56},{56,64},{64,7... | collective-permute-start | bytes 1966088 | tf_op jit(solution)/shard_map/ppermute | solution.py:256
  2.7 24.1 %collective-permute-start.1 = (bf16[10,256,128]{2,1,0:T(8,128)(2,1)}, bf16[10,256,128]{2,1,0:T(8,128)(2,1)S(1)}, u32[]{:S(2)}, u32[]{:S(2)}) collective-permute-start(bf16[10,256,128]{2,1,0:T(8,128)(2,1)} %bitcast.15), channel_id=1, source_target_pairs={{8,0},{16,8},{24,16},{32,24},{40,32},{48,40},{56,48},{64,56},{72,6... | collective-permute-start | bytes 1966088 | tf_op jit(solution)/shard_map/ppermute | solution.py:256
  10.1 0.9 copy-start.7
  11.0 0.7 copy-start.25
  11.7 0.7 copy-start.26
  12.4 0.7 copy-start.28
  13.0 42.5 %copy-start.16 = (bf16[256,256]{1,0:T(8,128)(2,1)S(1)}, bf16[256,256]{1,0:T(8,128)(2,1)}, u32[]{:S(2)}) copy-start(bf16[256,256]{1,0:T(8,128)(2,1)} %constant.13.clone.refs_8_) | copy-start | bytes 393220
  13.1 42.5 %copy-start.18 = (bf16[256,256]{1,0:T(8,128)(2,1)S(1)}, bf16[256,256]{1,0:T(8,128)(2,1)}, u32[]{:S(2)}) copy-start(bf16[256,256]{1,0:T(8,128)(2,1)} %constant.14.clone.refs_9_) | copy-start | bytes 393220
  13.8 13.0 %collective-permute-start.2 = (f32[256,128]{1,0:T(8,128)S(1)}, f32[256,128]{1,0:T(8,128)S(1)}, u32[]{:S(2)}, u32[]{:S(2)}) collective-permute-start(f32[256,128]{1,0:T(8,128)S(1)} %shard_map.131.refs_5_.g1), channel_id=1, source_target_pairs={{0,8},{8,16},{16,24},{24,32},{32,40},{40,48},{48,56},{56,64},{64,7... | collective-permute-start | bytes 393224 | tf_op jit(solution)/shard_map/ppermute | solution.py:256
  13.9 12.9 %collective-permute-start.3 = (f32[256,128]{1,0:T(8,128)S(1)}, f32[256,128]{1,0:T(8,128)S(1)}, u32[]{:S(2)}, u32[]{:S(2)}) collective-permute-start(f32[256,128]{1,0:T(8,128)S(1)} %shard_map.131.refs_5_.g1), channel_id=1, source_target_pairs={{8,0},{16,8},{24,16},{32,24},{40,32},{48,40},{56,48},{64,56},{72,6... | collective-permute-start | bytes 393224 | tf_op jit(solution)/shard_map/ppermute | solution.py:256
  26.8 9.3 %copy-start.11 = (f32[256,128]{1,0:T(8,128)}, f32[256,128]{1,0:T(8,128)S(1)}, u32[]{:S(2)}) copy-start(f32[256,128]{1,0:T(8,128)S(1)} %collective-permute-done.2.refs_4_.g0) | copy-start | bytes 393220
  26.8 9.3 %copy-start.13 = (f32[256,128]{1,0:T(8,128)}, f32[256,128]{1,0:T(8,128)S(1)}, u32[]{:S(2)}) copy-start(f32[256,128]{1,0:T(8,128)S(1)} %collective-permute-done.3.refs_6_.g2) | copy-start | bytes 393220
  26.8 1.2 %copy-start = (bf16[10,16,16,128]{3,2,1,0:T(8,128)(2,1)S(1)}, bf16[10,16,16,128]{3,2,1,0:T(8,128)(2,1)}, u32[]{:S(2)}) copy-start(bf16[10,16,16,128]{3,2,1,0:T(8,128)(2,1)} %param.12) | copy-start | bytes 1966084
  28.0 1.1 %copy-start.5 = (bf16[512,768]{1,0:T(8,128)(2,1)S(1)}, bf16[512,768]{1,0:T(8,128)(2,1)}, u32[]{:S(2)}) copy-start(bf16[512,768]{1,0:T(8,128)(2,1)} %constant.12.clone.refs_7_) | copy-start | bytes 2359300
  29.1 0.9 copy-start.15
  30.0 0.9 copy-start.17
  30.9 24.6 %copy-start.1 = (bf16[10,16,16,128]{3,2,1,0:T(8,128)(2,1)S(1)}, bf16[10,16,16,128]{3,2,1,0:T(8,128)(2,1)}, u32[]{:S(2)}) copy-start(bf16[10,16,16,128]{3,2,1,0:T(8,128)(2,1)} %param.12) | copy-start | bytes 1966084
  30.9 24.6 %copy-start.6 = (bf16[512,768]{1,0:T(8,128)(2,1)S(1)}, bf16[512,768]{1,0:T(8,128)(2,1)}, u32[]{:S(2)}) copy-start(bf16[512,768]{1,0:T(8,128)(2,1)} %constant.12.clone.refs_7_) | copy-start | bytes 2359300
  48.2 12.5 %copy-start.19 = (f32[256,128]{1,0:T(8,128)}, f32[256,128]{1,0:T(8,128)S(1)}, u32[]{:S(2)}) copy-start(f32[256,128]{1,0:T(8,128)S(1)} %get-tuple-element.9.refs_5_.g1) | copy-start | bytes 393220
  48.2 23.7 %copy-start.27 = (f32[2048]{0:T(1024)S(1)}, f32[2048]{0:T(1024)}, u32[]{:S(2)}) copy-start(f32[2048]{0:T(1024)} %param.14) | copy-start | bytes 24580
  48.3 23.6 %copy-start.29 = (f32[2048]{0:T(1024)S(1)}, f32[2048]{0:T(1024)}, u32[]{:S(2)}) copy-start(f32[2048]{0:T(1024)} %param.13) | copy-start | bytes 24580
  48.3 7.2 %collective-permute-start.4 = (f32[256,128]{1,0:T(8,128)S(1)}, f32[256,128]{1,0:T(8,128)S(1)}, u32[]{:S(2)}, u32[]{:S(2)}) collective-permute-start(f32[256,128]{1,0:T(8,128)S(1)} %get-tuple-element.9.refs_5_.g1), channel_id=1, source_target_pairs={{0,8},{8,16},{16,24},{24,32},{32,40},{40,48},{48,56},{56,64},{64,7... | collective-permute-start | bytes 393224 | tf_op jit(solution)/shard_map/ppermute | solution.py:256
  48.4 7.2 %collective-permute-start.5 = (f32[256,128]{1,0:T(8,128)S(1)}, f32[256,128]{1,0:T(8,128)S(1)}, u32[]{:S(2)}, u32[]{:S(2)}) collective-permute-start(f32[256,128]{1,0:T(8,128)S(1)} %get-tuple-element.9.refs_5_.g1), channel_id=1, source_target_pairs={{8,0},{16,8},{24,16},{32,24},{40,32},{48,40},{56,48},{64,56},{72,6... | collective-permute-start | bytes 393224 | tf_op jit(solution)/shard_map/ppermute | solution.py:256
  55.5 5.2 %copy-start.23 = (f32[256,128]{1,0:T(8,128)}, f32[256,128]{1,0:T(8,128)S(1)}, u32[]{:S(2)}) copy-start(f32[256,128]{1,0:T(8,128)S(1)} %collective-permute-done.5.refs_6_.g2) | copy-start | bytes 393220
  60.8 0.6 copy-start.21
  61.4 16.9 %copy-start.8 = (bf16[256,256]{1,0:T(8,128)(2,1)S(1)}, bf16[256,256]{1,0:T(8,128)(2,1)}, u32[]{:S(2)}) copy-start(bf16[256,256]{1,0:T(8,128)(2,1)} %constant.16.clone.pair_high) | copy-start | bytes 393220
  73.4 18.5 %all-to-all-start.3 = ((f32[8,64,128]{2,1,0:T(8,128)}), f32[8,64,128]{2,1,0:T(8,128)}, u32[]{:S(2)}, u32[]{:S(2)}) async-start(f32[8,64,128]{2,1,0:T(8,128)} %broadcast_in_dim.2), calls=%async_computation.3 | async-start | bytes 524288 | tf_op jit(solution)/shard_map/all_to_all | solution.py:311
  78.3 1.1 %copy-start.4 = (bf16[512,768]{1,0:T(8,128)(2,1)S(1)}, bf16[512,768]{1,0:T(8,128)(2,1)}, u32[]{:S(2)}) copy-start(bf16[512,768]{1,0:T(8,128)(2,1)} %constant.15.clone.mix) | copy-start | bytes 2359300
  79.4 0.9 copy-start.9
  80.3 0.9 copy-start.12
  81.2 0.9 copy-start.14
  82.1 4.3 %copy-start.10 = (bf16[256,256]{1,0:T(8,128)(2,1)S(1)}, bf16[256,256]{1,0:T(8,128)(2,1)}, u32[]{:S(2)}) copy-start(bf16[256,256]{1,0:T(8,128)(2,1)} %constant.17.clone.pair_low) | copy-start | bytes 393220
  82.1 4.3 %copy-start.20 = (f32[256,128]{1,0:T(8,128)S(1)}, f32[256,128]{1,0:T(8,128)}, u32[]{:S(2)}) copy-start(f32[256,128]{1,0:T(8,128)} %copy-done.19) | copy-start | bytes 393220
  82.1 4.3 %copy-start.22 = (f32[256,128]{1,0:T(8,128)S(1)}, f32[256,128]{1,0:T(8,128)}, u32[]{:S(2)}) copy-start(f32[256,128]{1,0:T(8,128)} %copy-done.21) | copy-start | bytes 393220
  82.1 4.4 %copy-start.24 = (f32[256,128]{1,0:T(8,128)S(1)}, f32[256,128]{1,0:T(8,128)}, u32[]{:S(2)}) copy-start(f32[256,128]{1,0:T(8,128)} %copy-done.23) | copy-start | bytes 393220
  90.8 1.1 copy-start.2
  91.9 16.7 %all-to-all-start.2 = ((f32[32,1,128]{2,1,0:T(1,128)}), f32[32,1,128]{2,1,0:T(1,128)S(1)}, u32[]{:S(2)}, u32[]{:S(2)}) async-start(f32[32,1,128]{2,1,0:T(1,128)} %bitcast.7), calls=%async_computation.2 | async-start | bytes 32768 | tf_op jit(solution)/shard_map/all_to_all | solution.py:314
  108.6 1.3 %copy-start.3 = (f32[10,256,128]{2,1,0:T(8,128)S(1)}, f32[10,256,128]{2,1,0:T(8,128)}, u32[]{:S(2)}) copy-start(f32[10,256,128]{2,1,0:T(8,128)} %copy-done.2) | copy-start | bytes 3932164

commit v2 on v1

--- a/solution.py
+++ b/solution.py
@@ -11,7 +11,8 @@
 F32 = jnp.float32
 BF16 = jnp.bfloat16
 VERTICAL_SPREAD = 2.0
-VMEM_LIMIT = 40 * 1024 * 1024
+CORES = 2
+VMEM_LIMIT = 12 * 1024 * 1024
 
 
 def gauss(radius, spread):
@@ -51,7 +52,11 @@
         blocks.append(np.kron(vertical, along))
     rows_high, rows_low = bf16_pair(np.concatenate(blocks, axis=1) * scale)
     pair_high, pair_low = bf16_pair(np.kron(np.eye(2), lateral))
-    return np.concatenate([rows_high, rows_low], axis=0), pair_high, pair_low
+    mix = np.concatenate([rows_high, rows_low], axis=0)
+    total = levels * rows
+    own = mix[:, total : 2 * total]
+    sides = np.concatenate([mix[:, :total], mix[:, 2 * total :]], axis=1)
+    return mix, own, sides, pair_high, pair_low
 
 
 def split(x):
@@ -122,6 +127,15 @@
     return across[:total] + across[total:] + dot(high, pair_low_ref[...])
 
 
+def summed_members(field, weigh, p_refs, g_refs, rows_ref, pair_high_ref, pair_low_ref):
+    columns = g_refs[0].shape[1]
+    for first in range(0, weigh.shape[0], 2):
+        spread = localized(first, p_refs, g_refs, rows_ref, pair_high_ref, pair_low_ref)
+        field = field + weigh[first].astype(F32) * spread[:, :columns]
+        field = field + weigh[first + 1].astype(F32) * spread[:, columns:]
+    return field
+
+
 def as_rows(line, width=128):
     return jnp.concatenate([line[:, i : i + width] for i in range(0, line.shape[1], width)], axis=0)
 
@@ -136,31 +150,30 @@
     field[...] = adjoint(values, weights, cell, rows, columns)
 
 
-def forward_kernel(rows, columns, count, p0, p1, p2, g0, g1, g2, mix, pair_high, pair_low, weights, cell, message):
-    members = p0.shape[0]
-    field = jnp.zeros(g0.shape, F32)
-    for first in range(0, members, 2):
-        spread = localized(first, (p0, p1, p2), (g0, g1, g2), mix, pair_high, pair_low)
-        field = field + p1[first].astype(F32) * spread[:, :columns] + p1[first + 1].astype(F32) * spread[:, columns:]
+def own_kernel(p, g, mix, pair_high, pair_low, field):
+    field[...] = summed_members(jnp.zeros(g.shape, F32), p, [p], [g], mix, pair_high, pair_low)
+
+
+def forward_kernel(rows, columns, count, place, p0, p, p2, g0, g2, own, mix, pair_high, pair_low, weights, cell, kept, given, whole):
+    field = summed_members(own[...], p, [p0, p2], [g0, g2], mix, pair_high, pair_low)
+    whole[...] = field
     observed = as_rows(observe(field, weights, cell, live_slots(count, weights.shape[1]), rows, columns))
-    peers = message.shape[0]
     lines = observed.shape[0]
-    share = field.shape[0] // peers
-    for peer in range(peers):
-        message[peer, :lines] = observed
-        message[peer, lines:] = field[peer * share : (peer + 1) * share]
-
-
-def middle_kernel(rows, columns, count, message, weights, cell, precision, field, observed, share):
-    summed = jnp.sum(message[...], axis=0)
-    lines = observed.shape[0]
-    observed[...] = summed[:lines]
-    share[...] = summed[lines:]
-    values = precision[...] * as_line(summed[:lines])
-    field[...] = adjoint(values, weights, cell, rows, columns)
-
-
-def alpha_kernel(p0, p1, p2, g0, g1, g2, mix, pair_high, pair_low, alpha):
+    half = field.shape[0] // CORES
+    core = lax.rem(place[0], CORES)
+    for message, at in ((kept, core), (given, 1 - core)):
+        message[:lines] = observed
+        message[lines:] = whole[pl.ds(pl.multiple_of(at * half, half), half)]
+
+
+def middle_kernel(rows, columns, count, *refs):
+    *messages, weights, cell, precision, after, field, observed = refs
+    summed = sum(message[...] for message in messages)
+    observed[...] = summed
+    field[...] = adjoint(precision[...] * as_line(summed), weights, cell, rows, columns)
+
+
+def alpha_kernel(p0, p1, p2, g0, g1, g2, mix, pair_high, pair_low, after, alpha):
     columns = g0.shape[1]
     for first in range(0, p0.shape[0], 2):
         spread = localized(first, (p0, p1, p2), (g0, g1, g2), mix, pair_high, pair_low)
@@ -168,11 +181,11 @@
         alpha[first + 1] = spread[:, columns:]
 
 
-def scalars_kernel(count, message, once, precision, innovations, scalars, share):
-    summed = jnp.sum(message[...], axis=0)
+def scalars_kernel(count, *refs):
+    *messages, once, precision, innovations, after, scalars, half = refs
     lines = once.shape[0]
-    share[...] = summed[lines:]
-    z2 = summed[:lines]
+    z2 = sum(message[:lines] for message in messages)
+    half[...] = sum(message[lines:] for message in messages)
     z1 = once[...]
     rho = precision[...]
     slot = lax.broadcasted_iota(jnp.int32, rho.shape, 0) * rho.shape[1] + lax.broadcasted_iota(jnp.int32, rho.shape, 1)
@@ -210,7 +223,7 @@
     scalars[...] = jnp.broadcast_to(line, scalars.shape)
 
 
-def final_kernel(scalars, alpha0, alpha1, inc0, inc1, alpha, increment):
+def combination(scalars):
     table = scalars[...]
 
     def column(i):
@@ -228,25 +241,47 @@
     pq1 = pq1 + total(column(8) - 2.0 * delta * column(9) + delta * delta * column(10))
     pq1 = pq1 + 2.0 * beta * total(column(11) - delta * column(12)) + beta * beta * total(column(13))
     step1 = rr1 / pq1
-    first = step0 + step1 * (1.0 - step0 + beta)
-    second = -step1 * step0
-    increment[...] = first * inc0[...] + second * inc1[...]
+    return step0 + step1 * (1.0 - step0 + beta), -step1 * step0
+
+
+def final_kernel(scalars, alpha0, alpha1, alpha):
+    first, second = combination(scalars)
     for member in range(alpha.shape[0]):
         alpha[member] = first * alpha0[member] + second * alpha1[member]
 
 
-def call(kernel, outs, *args):
-    smem = [0] if args[0].dtype == jnp.int32 and args[0].shape == (1,) else []
-    vmem = pl.BlockSpec(memory_space=pltpu.VMEM)
+def increment_kernel(place, scalars, mine0, mine1, other0, other1, increment):
+    first, second = combination(scalars)
+    core = lax.rem(place[0], CORES)
+    half = mine0.shape[0]
+    for part0, part1, at in ((mine0, mine1, core), (other0, other1, 1 - core)):
+        increment[pl.ds(pl.multiple_of(at * half, half), half)] = first * part0[...] + second * part1[...]
+
+
+def in_vmem(x):
+    return x, pl.BlockSpec(memory_space=pltpu.VMEM)
+
+
+def in_smem(x):
+    return x, pl.BlockSpec(memory_space=pltpu.SMEM)
+
+
+def anywhere(x):
+    return x, pl.BlockSpec(memory_space=pl.ANY)
+
+
+def call(kernel, outs, args, scratch=()):
     single = not isinstance(outs, list)
     shapes = [jax.ShapeDtypeStruct(shape, F32) for shape in ([outs] if single else outs)]
+    out_spec = pl.BlockSpec(memory_space=pltpu.VMEM)
     return pl.pallas_call(
         kernel,
         out_shape=shapes[0] if single else shapes,
-        in_specs=[pl.BlockSpec(memory_space=pltpu.SMEM) if i in smem else vmem for i in range(len(args))],
-        out_specs=vmem if single else [vmem] * len(shapes),
+        in_specs=[spec for _, spec in args],
+        out_specs=out_spec if single else [out_spec] * len(shapes),
+        scratch_shapes=list(scratch),
         compiler_params=pltpu.CompilerParams(vmem_limit_bytes=VMEM_LIMIT),
-    )(*args)
+    )(*[x for x, _ in args])
 
 
 def neighbours(x):
@@ -263,9 +298,8 @@
     ens, tiles = lax.axis_size("ens"), lax.axis_size("tile")
     everyone = ens * members
     lines = slots // 128
-    share = cells // ens
-    mix2, high2, low2 = local_matrices(levels, rows, columns, 2, 1.0 / everyone)
-    mix1, high1, low1 = local_matrices(levels, rows, columns, 1, 1.0 / math.sqrt(everyone))
+    _, own2, sides2, high2, low2 = local_matrices(levels, rows, columns, 2, 1.0 / everyone)
+    mix1, _, _, high1, low1 = local_matrices(levels, rows, columns, 1, 1.0 / math.sqrt(everyone))
 
     p = perturbations.reshape(members, cells, columns)
     p_before, p_after = neighbours(p)
@@ -280,41 +314,69 @@
 
         return run
 
-    def forward(g, g_before, g_after):
-        return call(
-            bound(forward_kernel), (ens, lines + share, columns),
-            obs_count, p_before, p, p_after, g_before, g, g_after, mix2, high2, low2, obs_weights, cell,
+    field_shape = (cells, columns)
+    half = cells // CORES
+    chips = ens // CORES
+    place = lax.axis_index("ens").reshape(1)
+    vmem = lambda *xs: [in_vmem(x) for x in xs]
+
+    def own(g):
+        return call(own_kernel, field_shape, vmem(p, g, own2, high2, low2))
+
+    def forward(own_part, g_before, g_after):
+        kept, given = call(
+            bound(forward_kernel), [(lines + half, columns)] * 2,
+            [in_smem(obs_count), in_smem(place)]
+            + vmem(p_before, p, p_after, g_before, g_after, own_part, sides2, high2, low2, obs_weights, cell),
+            [pltpu.VMEM(field_shape, F32)],
         )
-
-    def alpha_of(g, g_before, g_after):
+        return kept + other_core(given)
+
+    def other_core(x):
+        return lax.ppermute(x, "ens", [(i, i ^ 1) for i in range(ens)])
+
+    def from_chips(x):
+        arrived = [x]
+        for back in range(1, chips):
+            route = [(c * CORES + core, (c + back) % chips * CORES + core) for c in range(chips) for core in range(CORES)]
+            arrived.append(lax.ppermute(x, "ens", route))
+        return arrived
+
+    def alpha_of(g, g_before, g_after, after):
         return call(
             alpha_kernel, (members, cells, columns),
-            p_before, p, p_after, g_before, g, g_after, mix1, high1, low1,
+            vmem(p_before, p, p_after, g_before, g, g_after, mix1, high1, low1) + [anywhere(after)],
         )
 
-    g0 = call(bound(start_kernel), (cells, columns), obs_count, obs_weights, cell, precision, innovations_line)
+    g0 = call(
+        bound(start_kernel), field_shape,
+        [in_smem(obs_count)] + vmem(obs_weights, cell, precision, innovations_line),
+    )
     g0_before, g0_after = neighbours(g0)
-    message = lax.all_to_all(forward(g0, g0_before, g0_after), "ens", 0, 0)
-    g1, once, share0 = call(
-        bound(middle_kernel), [(cells, columns), (lines, 128), (share, columns)],
-        obs_count, message, obs_weights, cell, precision,
+    sent = forward(own(g0), g0_before, g0_after)
+    messages = from_chips(sent[:lines])
+    alpha0 = alpha_of(g0, g0_before, g0_after, sent)
+    g1, once = call(
+        bound(middle_kernel), [field_shape, (lines, 128)],
+        [in_smem(obs_count)] + vmem(*messages, obs_weights, cell, precision) + [anywhere(alpha0)],
     )
     g1_before, g1_after = neighbours(g1)
-    alpha0 = alpha_of(g0, g0_before, g0_after)
-    message = lax.all_to_all(forward(g1, g1_before, g1_after), "ens", 0, 0)
-    scalars, share1 = call(
-        scalars_kernel, [(tiles, 128), (share, columns)],
-        obs_count, message, once, obs_precision.reshape(lines, 128), innovations.reshape(lines, 128),
-    )
-    alpha1 = alpha_of(g1, g1_before, g1_after)
-    both = jnp.concatenate([share0, share1], axis=0)
-    both = lax.all_to_all(jnp.broadcast_to(both[None], (ens,) + both.shape), "ens", 0, 0)
-    inc0 = both[:, :share].reshape(cells, columns)
-    inc1 = both[:, share:].reshape(cells, columns)
-    scalars = lax.all_to_all(scalars, "tile", 0, 0, tiled=True)
-    alpha, increment = call(
-        final_kernel, [(members, cells, columns), (cells, columns)],
-        scalars, alpha0, alpha1, inc0, inc1,
+    own_part = own(g1)
+    half0, own_part = lax.optimization_barrier((sent[lines:], own_part))
+    half0 = sum(from_chips(half0))
+    sent = forward(own_part, g1_before, g1_after)
+    messages = from_chips(sent)
+    alpha1 = alpha_of(g1, g1_before, g1_after, sent)
+    scalars, half1 = call(
+        scalars_kernel, [(tiles, 128), (half, columns)],
+        [in_smem(obs_count)] + vmem(*messages, once, obs_precision.reshape(lines, 128), innovations.reshape(lines, 128))
+        + [anywhere(alpha1)],
+    )
+    other0, other1 = other_core(half0), other_core(half1)
+    scalars = lax.all_to_all(scalars.reshape(tiles, 1, 128), "tile", 0, 0).reshape(tiles, 128)
+    alpha = call(final_kernel, (members, cells, columns), vmem(scalars, alpha0, alpha1))
+    increment = call(
+        increment_kernel, field_shape, [in_smem(place)] + vmem(scalars, half0, half1, other0, other1)
     )
     return alpha.reshape(perturbations.shape), increment.reshape(levels, rows, columns)
 

time: 113 us -> 90.2 us (0.80)
  blocking collectives: 21.9 us -> 11.6 us
  local copies, waits for them, and re-layouts: 15.7 us -> 6.89 us
  waiting for transfers between devices: 17.7 us -> 13.9 us
  Pallas kernels: 22.9 us -> 24.2 us
    ppermute x0 -> x13, starting transfers between devices: none -> 16.6 us  [the longest x9 10.9 us: from_chips(): arrived.append(lax.ppermute(x, 'ens', route))]
    all_to_all x2 -> x0, starting transfers between devices: 13.1 us -> none  [the longest x1 8.22 us: local(): scalars = lax.all_to_all(scalars, 'tile', 0, 0, tiled=True)]
    all_to_all x2 -> x1, blocking collectives: 21.9 us -> 11.6 us  [local(): lax.all_to_all(scalars.reshape(tiles, 1, 128), 'tile', 0, 0)]
    all_to_all x2 -> x0, waiting for transfers between devices: 7.44 us -> none  [the longest x1 7.44 us: local(): scalars = lax.all_to_all(scalars, 'tile', 0, 0, tiled=True)]
    unnamed x60 -> x38, local copies, waits for them, and re-layouts: 14 us -> 6.89 us
    ppermute x6, starting transfers between devices: 18.8 us -> 15.1 us  [neighbours(): return (lax.ppermute(x, 'tile', up), lax.ppermute(x, 'tile', down))]
    ppermute x0 -> x13, waiting for transfers between devices: none -> 2.56 us  [the longest x9 1.64 us: from_chips(): arrived.append(lax.ppermute(x, 'ens', route))]
    pallas_call x8 -> x11, Pallas kernels: 22.9 us -> 24.2 us  [call(): pl.pallas_call(kernel, out_shape=shapes[0] if single else shapes, in_spec...]
  transfers between devices with their start and end apart: 8 -> 19, of which waited for: 3 -> 6; matrix products, arithmetic and copies ran while one was open for 1% -> 0% of each run, Pallas kernels for 8% -> 16%
where the time goes in v2:
time: 90.2 us; the launch traced here: 89.9 us
  starting transfers between devices  31.7 us (35%)
  Pallas kernels  24.2 us (27%)
  waiting for transfers between devices  13.9 us (15%)
  blocking collectives  11.6 us (13%)
  local copies, waits for them, and re-layouts  6.89 us (8%)
  between operations  1.56 us (2%)
    pallas_call x11, Pallas kernels, call(): pl.pallas_call(kernel, out_shape=shapes[0] if single else shapes, in_spec...  24.2 us
    ppermute x6, starting transfers between devices, neighbours(): return (lax.ppermute(x, 'tile', up), lax.ppermute(x, 'tile', down))  15.1 us
    all_to_all x1, blocking collectives, local(): lax.all_to_all(scalars.reshape(tiles, 1, 128), 'tile', 0, 0)  11.6 us
    ppermute x6, waiting for transfers between devices, neighbours(): return (lax.ppermute(x, 'tile', up), lax.ppermute(x, 'tile', down))  11.4 us
    ppermute x9, starting transfers between devices, from_chips(): arrived.append(lax.ppermute(x, 'ens', route))  10.9 us
    unnamed x38, local copies, waits for them, and re-layouts  6.89 us
    ppermute x4, starting transfers between devices, other_core(): return lax.ppermute(x, 'ens', [(i, i ^ 1) for i in range(ens)])  5.71 us
  transfers between devices with their start and end apart: 19, of which 6 were waited for; matrix products, arithmetic and copies ran while one was open for 0% of the time, Pallas kernels for 16%

profile of v2, /device:TPU:1, one launch (start us, length us, event | category | flops | bytes accessed | tf_op | source)
XLA Modules:
  0.0 89.9 jit_solution(10923611471126561488)
XLA Ops:
  0.6 8.7 %collective-permute-start.1 = (bf16[10,256,128]{2,1,0:T(8,128)(2,1)}, bf16[10,256,128]{2,1,0:T(8,128)(2,1)S(1)}, u32[]{:S(2)}, u32[]{:S(2)}) collective-permute-start(bf16[10,256,128]{2,1,0:T(8,128)(2,1)} %bitcast.13), channel_id=1, source_target_pairs={{8,0},{16,8},{24,16},{32,24},{40,32},{48,40},{56,48},{64,56},{72,6... | collective-permute-start | bytes 1966088 | tf_op jit(solution)/shard_map/ppermute | solution.py:291
  9.3 0.0 collective-permute-start
  10.0 0.9 copy-done.3
  10.9 0.7 copy-done.13
  11.6 0.7 copy-done.15
  12.3 0.7 copy-done.17
  13.0 0.7 shard_map.140.g.g1
  13.7 4.9 %collective-permute-start.3 = (f32[256,128]{1,0:T(8,128)S(1)}, f32[256,128]{1,0:T(8,128)S(1)}, u32[]{:S(2)}, u32[]{:S(2)}) collective-permute-start(f32[256,128]{1,0:T(8,128)S(1)} %shard_map.140.g.g1), channel_id=1, source_target_pairs={{8,0},{16,8},{24,16},{32,24},{40,32},{48,40},{56,48},{64,56},{72,6... | collective-permute-start | bytes 393224 | tf_op jit(solution)/shard_map/ppermute | solution.py:291
  18.6 1.1 %copy-done = bf16[10,16,16,128]{3,2,1,0:T(8,128)(2,1)S(1)} copy-done((bf16[10,16,16,128]{3,2,1,0:T(8,128)(2,1)S(1)}, bf16[10,16,16,128]{3,2,1,0:T(8,128)(2,1)}, u32[]{:S(2)}) %copy-start) | copy-done | bytes 655384
  19.7 0.9 %copy-done.6 = bf16[256,256]{1,0:T(8,128)(2,1)S(1)} copy-done((bf16[256,256]{1,0:T(8,128)(2,1)S(1)}, bf16[256,256]{1,0:T(8,128)(2,1)}, u32[]{:S(2)}) %copy-start.6) | copy-done | bytes 131096
  20.6 0.9 %copy-done.8 = bf16[256,256]{1,0:T(8,128)(2,1)S(1)} copy-done((bf16[256,256]{1,0:T(8,128)(2,1)S(1)}, bf16[256,256]{1,0:T(8,128)(2,1)}, u32[]{:S(2)}) %copy-start.8) | copy-done | bytes 131096
  21.5 0.9 %copy-done.10 = bf16[512,256]{1,0:T(8,128)(2,1)S(1)} copy-done((bf16[512,256]{1,0:T(8,128)(2,1)S(1)}, bf16[512,256]{1,0:T(8,128)(2,1)}, u32[]{:S(2)}) %copy-start.10) | copy-done | bytes 262168
  22.4 1.4 %shard_map.141.refs_7_ = f32[256,128]{1,0:T(8,128)S(1)} custom-call(bf16[10,256,128]{2,1,0:T(8,128)(2,1)S(1)} %bitcast.15, f32[256,128]{1,0:T(8,128)S(1)} %shard_map.140.g.g1, bf16[512,256]{1,0:T(8,128)(2,1)S(1)} %copy-done.10, bf16[256,256]{1,0:T(8,128)(2,1)S(1)} %copy-done.8, bf16[256,256]{1,0:T(8,128)(2,1)S(1)} %copy-done.6), custom_call_target="tpu_custom_call" | custom-call | tf_op jit(solution)/shard_map/pallas_call | solution.py:277
  23.9 1.9 %collective-permute-done.3.refs_6_.g2 = f32[256,128]{1,0:T(8,128)S(1)} collective-permute-done((f32[256,128]{1,0:T(8,128)S(1)}, f32[256,128]{1,0:T(8,128)S(1)}, u32[]{:S(2)}, u32[]{:S(2)}) %collective-permute-start.3) | collective-permute-done | bytes 131104 | tf_op jit(solution)/shard_map/ppermute | solution.py:291
  25.7 5.2 %collective-permute-done.2.refs_5_.g0 = f32[256,128]{1,0:T(8,128)S(1)} collective-permute-done((f32[256,128]{1,0:T(8,128)S(1)}, f32[256,128]{1,0:T(8,128)S(1)}, u32[]{:S(2)}, u32[]{:S(2)}) %collective-permute-start.2) | collective-permute-done | bytes 131104 | tf_op jit(solution)/shard_map/ppermute | solution.py:291
  31.0 0.0 copy-start.2
  31.0 0.0 copy-start.11
  31.0 0.0 copy-start.12
  31.0 4.0 %shard_map.142 = (f32[144,128]{1,0:T(8,128)S(1)}, f32[144,128]{1,0:T(8,128)S(1)}) custom-call(s32[1]{0:T(128)S(6)} %copy.16.refs_0_.count, s32[1]{0:T(128)} %bitcast.refs_1_.place, bf16[10,256,128]{2,1,0:T(8,128)(2,1)S(1)} %collective-permute-done.refs_2_.p0, bf16[10,256,128]{2,1,0:T(8,128)(2,1)S(1)} %bitcast.16, ...), custom_call_target="tpu_custom_call" | custom-call | tf_op jit(solution)/shard_map/pallas_call | solution.py:277
  35.0 1.9 %collective-permute-start.4 = (f32[144,128]{1,0:T(8,128)S(1)}, f32[144,128]{1,0:T(8,128)S(1)}, u32[]{:S(2)}, u32[]{:S(2)}) collective-permute-start(f32[144,128]{1,0:T(8,128)S(1)} %get-tuple-element.13), channel_id=1, source_target_pairs={{0,1},{1,0},{2,3},{3,2},{4,5},{5,4},{6,7},{7,6},{8,9},{9,8},{10,11... | collective-permute-start | bytes 221192 | tf_op jit(solution)/shard_map/ppermute | solution.py:336
  37.0 0.9 %collective-permute-done.4 = f32[144,128]{1,0:T(8,128)S(1)} collective-permute-done((f32[144,128]{1,0:T(8,128)S(1)}, f32[144,128]{1,0:T(8,128)S(1)}, u32[]{:S(2)}, u32[]{:S(2)}) %collective-permute-start.4) | collective-permute-done | bytes 73760 | tf_op jit(solution)/shard_map/ppermute | solution.py:336
  37.9 0.0 copy-start.16
  37.9 2.8 %collective-permute-start.7 = (f32[16,128]{1,0:T(8,128)S(1)}, f32[16,128]{1,0:T(8,128)S(1)}, u32[]{:S(2)}, u32[]{:S(2)}) collective-permute-start(f32[16,128]{1,0:T(8,128)S(1)} %slice.8.refs_1_), channel_id=1, source_target_pairs={{0,6},{1,7},{2,0},{3,1},{4,2},{5,3},{6,4},{7,5},{8,14},{9,15},{10,... | collective-permute-start | bytes 24584 | tf_op jit(solution)/shard_map/ppermute | solution.py:342
  40.7 0.3 collective-permute-start.6
  41.1 0.7 collective-permute-start.5
  41.8 4.4 %shard_map.143.refs_8_.alpha0 = f32[10,256,128]{2,1,0:T(8,128)S(1)} custom-call(bf16[10,256,128]{2,1,0:T(8,128)(2,1)S(1)} %collective-permute-done.refs_2_.p0, bf16[10,256,128]{2,1,0:T(8,128)(2,1)S(1)} %bitcast.17, bf16[10,256,128]{2,1,0:T(8,128)(2,1)S(1)} %collective-permute-done.1.refs_4_.p2, f32[256,128]{1,0:T(8,128)S(1)} %collective-permute-done.2.refs_5_.g0, ...), custom_call_target="tpu_custom_call" | custom-call | tf_op jit(solution)/shard_map/pallas_call | solution.py:277
  46.2 0.7 shard_map.144
  47.0 0.1 collective-permute-start.9
  47.1 1.5 %collective-permute-start.8 = (f32[256,128]{1,0:T(8,128)S(1)}, f32[256,128]{1,0:T(8,128)S(1)}, u32[]{:S(2)}, u32[]{:S(2)}) collective-permute-start(f32[256,128]{1,0:T(8,128)S(1)} %get-tuple-element.14.g.g1), channel_id=1, source_target_pairs={{0,8},{8,16},{16,24},{24,32},{32,40},{40,48},{48,56},{56,64},{64,7... | collective-permute-start | bytes 393224 | tf_op jit(solution)/shard_map/ppermute | solution.py:291
  48.5 1.5 %shard_map.145.refs_7_ = f32[256,128]{1,0:T(8,128)S(1)} custom-call(bf16[10,256,128]{2,1,0:T(8,128)(2,1)S(1)} %bitcast.18, f32[256,128]{1,0:T(8,128)S(1)} %get-tuple-element.14.g.g1, bf16[512,256]{1,0:T(8,128)(2,1)S(1)} %copy-done.10, bf16[256,256]{1,0:T(8,128)(2,1)S(1)} %copy-done.9, bf16[256,256]{1,0:T(8,128)(2,1)S(1)} %copy-done.7), custom_call_target="tpu_custom_call" | custom-call | tf_op jit(solution)/shard_map/pallas_call | solution.py:277
  50.0 0.9 collective-permute-done.9.refs_6_.g2
  50.9 3.4 %collective-permute-done.8.refs_5_.g0 = f32[256,128]{1,0:T(8,128)S(1)} collective-permute-done((f32[256,128]{1,0:T(8,128)S(1)}, f32[256,128]{1,0:T(8,128)S(1)}, u32[]{:S(2)}, u32[]{:S(2)}) %collective-permute-start.8) | collective-permute-done | bytes 131104 | tf_op jit(solution)/shard_map/ppermute | solution.py:291
  54.3 4.0 %shard_map.146 = (f32[144,128]{1,0:T(8,128)S(1)}, f32[144,128]{1,0:T(8,128)S(1)}) custom-call(s32[1]{0:T(128)S(6)} %copy.16.refs_0_.count, s32[1]{0:T(128)} %bitcast.refs_1_.place, bf16[10,256,128]{2,1,0:T(8,128)(2,1)S(1)} %collective-permute-done.refs_2_.p0, bf16[10,256,128]{2,1,0:T(8,128)(2,1)S(1)} %bitcast.19, ...), custom_call_target="tpu_custom_call" | custom-call | tf_op jit(solution)/shard_map/pallas_call | solution.py:277
  58.2 2.6 %collective-permute-start.10 = (f32[144,128]{1,0:T(8,128)S(1)}, f32[144,128]{1,0:T(8,128)S(1)}, u32[]{:S(2)}, u32[]{:S(2)}) collective-permute-start(f32[144,128]{1,0:T(8,128)S(1)} %get-tuple-element.17), channel_id=1, source_target_pairs={{0,1},{1,0},{2,3},{3,2},{4,5},{5,4},{6,7},{7,6},{8,9},{9,8},{10,11... | collective-permute-start | bytes 221192 | tf_op jit(solution)/shard_map/ppermute | solution.py:336
  60.9 2.0 %collective-permute-start.16 = (f32[128,128]{1,0:T(8,128)S(1)}, f32[128,128]{1,0:T(8,128)S(1)}, u32[]{:S(2)}, u32[]{:S(2)}) collective-permute-start(f32[128,128]{1,0:T(8,128)S(1)} %slice.9), channel_id=1, source_target_pairs={{0,6},{1,7},{2,0},{3,1},{4,2},{5,3},{6,4},{7,5},{8,14},{9,15},{10,... | collective-permute-start | bytes 196616 | tf_op jit(solution)/shard_map/ppermute | solution.py:342
  62.9 1.4 %collective-permute-start.15 = (f32[128,128]{1,0:T(8,128)S(1)}, f32[128,128]{1,0:T(8,128)S(1)}, u32[]{:S(2)}, u32[]{:S(2)}) collective-permute-start(f32[128,128]{1,0:T(8,128)S(1)} %slice.9), channel_id=1, source_target_pairs={{0,4},{1,5},{2,6},{3,7},{4,0},{5,1},{6,2},{7,3},{8,12},{9,13},{10,... | collective-permute-start | bytes 196616 | tf_op jit(solution)/shard_map/ppermute | solution.py:342
  64.3 3.0 %collective-permute-start.13 = (f32[144,128]{1,0:T(8,128)S(1)}, f32[144,128]{1,0:T(8,128)S(1)}, u32[]{:S(2)}, u32[]{:S(2)}) collective-permute-start(f32[144,128]{1,0:T(8,128)S(1)} %add.16.after.refs_0_), channel_id=1, source_target_pairs={{0,6},{1,7},{2,0},{3,1},{4,2},{5,3},{6,4},{7,5},{8,14},{9,15},{10,... | collective-permute-start | bytes 221192 | tf_op jit(solution)/shard_map/ppermute | solution.py:342
  67.3 0.4 collective-permute-start.12
  67.6 0.3 collective-permute-start.11
  68.0 1.6 %collective-permute-done.14 = f32[128,128]{1,0:T(8,128)S(1)} collective-permute-done((f32[128,128]{1,0:T(8,128)S(1)}, f32[128,128]{1,0:T(8,128)S(1)}, u32[]{:S(2)}, u32[]{:S(2)}) %collective-permute-start.14) | collective-permute-done | bytes 65568 | tf_op jit(solution)/shard_map/ppermute | solution.py:342
  69.6 0.0 copy-start.18
  69.6 1.1 %collective-permute-start.17 = (f32[128,128]{1,0:T(8,128)S(1)}, f32[128,128]{1,0:T(8,128)S(1)}, u32[]{:S(2)}, u32[]{:S(2)}) collective-permute-start(f32[128,128]{1,0:T(8,128)S(1)} %add_add_fusion.mine0), channel_id=1, source_target_pairs={{0,1},{1,0},{2,3},{3,2},{4,5},{5,4},{6,7},{7,6},{8,9},{9,8},{10,11... | collective-permute-start | bytes 196616 | tf_op jit(solution)/shard_map/ppermute | solution.py:336
  70.7 4.4 %shard_map.147.refs_7_.alpha1 = f32[10,256,128]{2,1,0:T(8,128)S(1)} custom-call(bf16[10,256,128]{2,1,0:T(8,128)(2,1)S(1)} %collective-permute-done.refs_2_.p0, bf16[10,256,128]{2,1,0:T(8,128)(2,1)S(1)} %bitcast.20, bf16[10,256,128]{2,1,0:T(8,128)(2,1)S(1)} %collective-permute-done.1.refs_4_.p2, f32[256,128]{1,0:T(8,128)S(1)} %collective-permute-done.8.refs_5_.g0, ...), custom_call_target="tpu_custom_call" | custom-call | tf_op jit(solution)/shard_map/pallas_call | solution.py:277
  75.1 0.2 shard_map.148
  75.3 0.1 collective-permute-start.18
  75.4 11.6 %all_to_all.5 = f32[32,1,128]{2,1,0:T(1,128)S(1)} all-to-all(f32[32,1,128]{2,1,0:T(1,128)S(1)} %bitcast.32), channel_id=1, replica_groups=mesh['tile'=32,'ens'=8] {'tile'}, dimensions={0} | all-to-all | bytes 32768 | tf_op jit(solution)/shard_map/all_to_all | solution.py:376
  87.0 1.7 %shard_map.149 = f32[10,256,128]{2,1,0:T(8,128)} custom-call(f32[32,128]{1,0:T(8,128)S(1)} %bitcast.21, f32[10,256,128]{2,1,0:T(8,128)S(1)} %shard_map.143.refs_8_.alpha0, f32[10,256,128]{2,1,0:T(8,128)S(1)} %shard_map.147.refs_7_.alpha1), custom_call_target="tpu_custom_call" | custom-call | tf_op jit(solution)/shard_map/pallas_call | solution.py:277
  88.7 1.2 %shard_map.150 = f32[256,128]{1,0:T(8,128)} custom-call(s32[1]{0:T(128)} %bitcast.refs_1_.place, f32[32,128]{1,0:T(8,128)S(1)} %bitcast.22, f32[128,128]{1,0:T(8,128)S(1)} %add_add_fusion.mine0, f32[128,128]{1,0:T(8,128)S(1)} %get-tuple-element.21.mine1, f32[128,128]{1,0:T(8,128)S(1)} %collective-permute-done.17.other0, ...), custom_call_target="tpu_custom_call" | custom-call | tf_op jit(solution)/shard_map/pallas_call | solution.py:277
  (45 shorter events, 0.1 us)
Async XLA Ops:
  0.6 30.3 %copy-start.14 = (s32[2048]{0:T(1024)S(1)}, s32[2048]{0:T(1024)}, u32[]{:S(2)}) copy-start(s32[2048]{0:T(1024)} %param.17) | copy-start | bytes 24580
  0.6 30.3 %collective-permute-start.1 = (bf16[10,256,128]{2,1,0:T(8,128)(2,1)}, bf16[10,256,128]{2,1,0:T(8,128)(2,1)S(1)}, u32[]{:S(2)}, u32[]{:S(2)}) collective-permute-start(bf16[10,256,128]{2,1,0:T(8,128)(2,1)} %bitcast.13), channel_id=1, source_target_pairs={{8,0},{16,8},{24,16},{32,24},{40,32},{48,40},{56,48},{64,56},{72,6... | collective-permute-start | bytes 1966088 | tf_op jit(solution)/shard_map/ppermute | solution.py:291
  9.3 21.6 %collective-permute-start = (bf16[10,256,128]{2,1,0:T(8,128)(2,1)}, bf16[10,256,128]{2,1,0:T(8,128)(2,1)S(1)}, u32[]{:S(2)}, u32[]{:S(2)}) collective-permute-start(bf16[10,256,128]{2,1,0:T(8,128)(2,1)} %bitcast.14), channel_id=1, source_target_pairs={{0,8},{8,16},{16,24},{24,32},{32,40},{40,48},{48,56},{56,64},{64,7... | collective-permute-start | bytes 1966088 | tf_op jit(solution)/shard_map/ppermute | solution.py:291
  10.0 0.9 %copy-start.3 = (f32[16,2048]{1,0:T(8,128)S(1)}, f32[16,2048]{1,0:T(8,128)}, u32[]{:S(2)}) copy-start(f32[16,2048]{1,0:T(8,128)} %refs_11_.3) | copy-start | bytes 393220
  10.9 0.7 copy-start.13
  11.6 0.7 copy-start.15
  12.3 0.7 copy-start.17
  13.0 18.0 %copy-start.4 = (f32[16,2048]{1,0:T(8,128)S(1)}, f32[16,2048]{1,0:T(8,128)}, u32[]{:S(2)}) copy-start(f32[16,2048]{1,0:T(8,128)} %refs_11_.3) | copy-start | bytes 393220
  13.0 18.0 %copy-start.7 = (bf16[256,256]{1,0:T(8,128)(2,1)S(1)}, bf16[256,256]{1,0:T(8,128)(2,1)}, u32[]{:S(2)}) copy-start(bf16[256,256]{1,0:T(8,128)(2,1)} %constant.20.clone.pair_low.refs_10_) | copy-start | bytes 393220
  13.7 12.0 %collective-permute-start.3 = (f32[256,128]{1,0:T(8,128)S(1)}, f32[256,128]{1,0:T(8,128)S(1)}, u32[]{:S(2)}, u32[]{:S(2)}) collective-permute-start(f32[256,128]{1,0:T(8,128)S(1)} %shard_map.140.g.g1), channel_id=1, source_target_pairs={{8,0},{16,8},{24,16},{32,24},{40,32},{48,40},{56,48},{64,56},{72,6... | collective-permute-start | bytes 393224 | tf_op jit(solution)/shard_map/ppermute | solution.py:291
  18.6 12.4 %collective-permute-start.2 = (f32[256,128]{1,0:T(8,128)S(1)}, f32[256,128]{1,0:T(8,128)S(1)}, u32[]{:S(2)}, u32[]{:S(2)}) collective-permute-start(f32[256,128]{1,0:T(8,128)S(1)} %shard_map.140.g.g1), channel_id=1, source_target_pairs={{0,8},{8,16},{16,24},{24,32},{32,40},{40,48},{48,56},{56,64},{64,7... | collective-permute-start | bytes 393224 | tf_op jit(solution)/shard_map/ppermute | solution.py:291
  18.6 1.1 %copy-start = (bf16[10,16,16,128]{3,2,1,0:T(8,128)(2,1)S(1)}, bf16[10,16,16,128]{3,2,1,0:T(8,128)(2,1)}, u32[]{:S(2)}) copy-start(bf16[10,16,16,128]{3,2,1,0:T(8,128)(2,1)} %param.13) | copy-start | bytes 1966084
  19.7 0.9 %copy-start.6 = (bf16[256,256]{1,0:T(8,128)(2,1)S(1)}, bf16[256,256]{1,0:T(8,128)(2,1)}, u32[]{:S(2)}) copy-start(bf16[256,256]{1,0:T(8,128)(2,1)} %constant.20.clone.pair_low.refs_10_) | copy-start | bytes 393220
  20.6 0.9 %copy-start.8 = (bf16[256,256]{1,0:T(8,128)(2,1)S(1)}, bf16[256,256]{1,0:T(8,128)(2,1)}, u32[]{:S(2)}) copy-start(bf16[256,256]{1,0:T(8,128)(2,1)} %constant.19.clone.pair_high.refs_9_) | copy-start | bytes 393220
  21.5 0.9 %copy-start.10 = (bf16[512,256]{1,0:T(8,128)(2,1)S(1)}, bf16[512,256]{1,0:T(8,128)(2,1)}, u32[]{:S(2)}) copy-start(bf16[512,256]{1,0:T(8,128)(2,1)} %constant.18.clone.mix) | copy-start | bytes 786436
  22.4 8.6 %copy-start.1 = (bf16[10,16,16,128]{3,2,1,0:T(8,128)(2,1)S(1)}, bf16[10,16,16,128]{3,2,1,0:T(8,128)(2,1)}, u32[]{:S(2)}) copy-start(bf16[10,16,16,128]{3,2,1,0:T(8,128)(2,1)} %param.13) | copy-start | bytes 1966084
  22.4 8.6 %copy-start.5 = (bf16[512,512]{1,0:T(8,128)(2,1)S(1)}, bf16[512,512]{1,0:T(8,128)(2,1)}, u32[]{:S(2)}) copy-start(bf16[512,512]{1,0:T(8,128)(2,1)} %constant.21.clone.refs_8_) | copy-start | bytes 1572868
  22.4 8.6 %copy-start.9 = (bf16[256,256]{1,0:T(8,128)(2,1)S(1)}, bf16[256,256]{1,0:T(8,128)(2,1)}, u32[]{:S(2)}) copy-start(bf16[256,256]{1,0:T(8,128)(2,1)} %constant.19.clone.pair_high.refs_9_) | copy-start | bytes 393220
  31.0 10.8 %copy-start.2 = (bf16[512,768]{1,0:T(8,128)(2,1)S(1)}, bf16[512,768]{1,0:T(8,128)(2,1)}, u32[]{:S(2)}) copy-start(bf16[512,768]{1,0:T(8,128)(2,1)} %constant.22.clone.mix) | copy-start | bytes 2359300
  31.0 10.8 %copy-start.11 = (bf16[256,256]{1,0:T(8,128)(2,1)S(1)}, bf16[256,256]{1,0:T(8,128)(2,1)}, u32[]{:S(2)}) copy-start(bf16[256,256]{1,0:T(8,128)(2,1)} %constant.24.clone.pair_low) | copy-start | bytes 393220
  31.0 10.8 %copy-start.12 = (bf16[256,256]{1,0:T(8,128)(2,1)S(1)}, bf16[256,256]{1,0:T(8,128)(2,1)}, u32[]{:S(2)}) copy-start(bf16[256,256]{1,0:T(8,128)(2,1)} %constant.23.clone.pair_high) | copy-start | bytes 393220
  35.0 2.9 %collective-permute-start.4 = (f32[144,128]{1,0:T(8,128)S(1)}, f32[144,128]{1,0:T(8,128)S(1)}, u32[]{:S(2)}, u32[]{:S(2)}) collective-permute-start(f32[144,128]{1,0:T(8,128)S(1)} %get-tuple-element.13), channel_id=1, source_target_pairs={{0,1},{1,0},{2,3},{3,2},{4,5},{5,4},{6,7},{7,6},{8,9},{9,8},{10,11... | collective-permute-start | bytes 221192 | tf_op jit(solution)/shard_map/ppermute | solution.py:336
  37.9 8.3 %copy-start.16 = (f32[2048]{0:T(1024)S(1)}, f32[2048]{0:T(1024)}, u32[]{:S(2)}) copy-start(f32[2048]{0:T(1024)} %param.15) | copy-start | bytes 24580
  37.9 8.3 %collective-permute-start.7 = (f32[16,128]{1,0:T(8,128)S(1)}, f32[16,128]{1,0:T(8,128)S(1)}, u32[]{:S(2)}, u32[]{:S(2)}) collective-permute-start(f32[16,128]{1,0:T(8,128)S(1)} %slice.8.refs_1_), channel_id=1, source_target_pairs={{0,6},{1,7},{2,0},{3,1},{4,2},{5,3},{6,4},{7,5},{8,14},{9,15},{10,... | collective-permute-start | bytes 24584 | tf_op jit(solution)/shard_map/ppermute | solution.py:342
  40.7 5.5 %collective-permute-start.6 = (f32[16,128]{1,0:T(8,128)S(1)}, f32[16,128]{1,0:T(8,128)S(1)}, u32[]{:S(2)}, u32[]{:S(2)}) collective-permute-start(f32[16,128]{1,0:T(8,128)S(1)} %slice.8.refs_1_), channel_id=1, source_target_pairs={{0,4},{1,5},{2,6},{3,7},{4,0},{5,1},{6,2},{7,3},{8,12},{9,13},{10,... | collective-permute-start | bytes 24584 | tf_op jit(solution)/shard_map/ppermute | solution.py:342
  41.1 5.2 %collective-permute-start.5 = (f32[16,128]{1,0:T(8,128)S(1)}, f32[16,128]{1,0:T(8,128)S(1)}, u32[]{:S(2)}, u32[]{:S(2)}) collective-permute-start(f32[16,128]{1,0:T(8,128)S(1)} %slice.8.refs_1_), channel_id=1, source_target_pairs={{0,2},{1,3},{2,4},{3,5},{4,6},{5,7},{6,0},{7,1},{8,10},{9,11},{10,... | collective-permute-start | bytes 24584 | tf_op jit(solution)/shard_map/ppermute | solution.py:342
  47.0 3.9 %collective-permute-start.9 = (f32[256,128]{1,0:T(8,128)S(1)}, f32[256,128]{1,0:T(8,128)S(1)}, u32[]{:S(2)}, u32[]{:S(2)}) collective-permute-start(f32[256,128]{1,0:T(8,128)S(1)} %get-tuple-element.14.g.g1), channel_id=1, source_target_pairs={{8,0},{16,8},{24,16},{32,24},{40,32},{48,40},{56,48},{64,56},{72,6... | collective-permute-start | bytes 393224 | tf_op jit(solution)/shard_map/ppermute | solution.py:291
  47.1 7.2 %collective-permute-start.8 = (f32[256,128]{1,0:T(8,128)S(1)}, f32[256,128]{1,0:T(8,128)S(1)}, u32[]{:S(2)}, u32[]{:S(2)}) collective-permute-start(f32[256,128]{1,0:T(8,128)S(1)} %get-tuple-element.14.g.g1), channel_id=1, source_target_pairs={{0,8},{8,16},{16,24},{24,32},{32,40},{40,48},{48,56},{56,64},{64,7... | collective-permute-start | bytes 393224 | tf_op jit(solution)/shard_map/ppermute | solution.py:291
  58.2 6.0 %collective-permute-start.10 = (f32[144,128]{1,0:T(8,128)S(1)}, f32[144,128]{1,0:T(8,128)S(1)}, u32[]{:S(2)}, u32[]{:S(2)}) collective-permute-start(f32[144,128]{1,0:T(8,128)S(1)} %get-tuple-element.17), channel_id=1, source_target_pairs={{0,1},{1,0},{2,3},{3,2},{4,5},{5,4},{6,7},{7,6},{8,9},{9,8},{10,11... | collective-permute-start | bytes 221192 | tf_op jit(solution)/shard_map/ppermute | solution.py:336
  60.9 6.8 %collective-permute-start.16 = (f32[128,128]{1,0:T(8,128)S(1)}, f32[128,128]{1,0:T(8,128)S(1)}, u32[]{:S(2)}, u32[]{:S(2)}) collective-permute-start(f32[128,128]{1,0:T(8,128)S(1)} %slice.9), channel_id=1, source_target_pairs={{0,6},{1,7},{2,0},{3,1},{4,2},{5,3},{6,4},{7,5},{8,14},{9,15},{10,... | collective-permute-start | bytes 196616 | tf_op jit(solution)/shard_map/ppermute | solution.py:342
  62.9 5.1 %collective-permute-start.15 = (f32[128,128]{1,0:T(8,128)S(1)}, f32[128,128]{1,0:T(8,128)S(1)}, u32[]{:S(2)}, u32[]{:S(2)}) collective-permute-start(f32[128,128]{1,0:T(8,128)S(1)} %slice.9), channel_id=1, source_target_pairs={{0,4},{1,5},{2,6},{3,7},{4,0},{5,1},{6,2},{7,3},{8,12},{9,13},{10,... | collective-permute-start | bytes 196616 | tf_op jit(solution)/shard_map/ppermute | solution.py:342
  64.3 5.3 %collective-permute-start.14 = (f32[128,128]{1,0:T(8,128)S(1)}, f32[128,128]{1,0:T(8,128)S(1)}, u32[]{:S(2)}, u32[]{:S(2)}) collective-permute-start(f32[128,128]{1,0:T(8,128)S(1)} %slice.9), channel_id=1, source_target_pairs={{0,2},{1,3},{2,4},{3,5},{4,6},{5,7},{6,0},{7,1},{8,10},{9,11},{10,... | collective-permute-start | bytes 196616 | tf_op jit(solution)/shard_map/ppermute | solution.py:342
  64.3 10.8 %collective-permute-start.13 = (f32[144,128]{1,0:T(8,128)S(1)}, f32[144,128]{1,0:T(8,128)S(1)}, u32[]{:S(2)}, u32[]{:S(2)}) collective-permute-start(f32[144,128]{1,0:T(8,128)S(1)} %add.16.after.refs_0_), channel_id=1, source_target_pairs={{0,6},{1,7},{2,0},{3,1},{4,2},{5,3},{6,4},{7,5},{8,14},{9,15},{10,... | collective-permute-start | bytes 221192 | tf_op jit(solution)/shard_map/ppermute | solution.py:342
  67.3 7.8 %collective-permute-start.12 = (f32[144,128]{1,0:T(8,128)S(1)}, f32[144,128]{1,0:T(8,128)S(1)}, u32[]{:S(2)}, u32[]{:S(2)}) collective-permute-start(f32[144,128]{1,0:T(8,128)S(1)} %add.16.after.refs_0_), channel_id=1, source_target_pairs={{0,4},{1,5},{2,6},{3,7},{4,0},{5,1},{6,2},{7,3},{8,12},{9,13},{10,... | collective-permute-start | bytes 221192 | tf_op jit(solution)/shard_map/ppermute | solution.py:342
  67.6 7.5 %collective-permute-start.11 = (f32[144,128]{1,0:T(8,128)S(1)}, f32[144,128]{1,0:T(8,128)S(1)}, u32[]{:S(2)}, u32[]{:S(2)}) collective-permute-start(f32[144,128]{1,0:T(8,128)S(1)} %add.16.after.refs_0_), channel_id=1, source_target_pairs={{0,2},{1,3},{2,4},{3,5},{4,6},{5,7},{6,0},{7,1},{8,10},{9,11},{10,... | collective-permute-start | bytes 221192 | tf_op jit(solution)/shard_map/ppermute | solution.py:342
  69.6 5.5 %copy-start.18 = (f32[2048]{0:T(1024)S(1)}, f32[2048]{0:T(1024)}, u32[]{:S(2)}) copy-start(f32[2048]{0:T(1024)} %param.14) | copy-start | bytes 24580
  69.6 19.1 %collective-permute-start.17 = (f32[128,128]{1,0:T(8,128)S(1)}, f32[128,128]{1,0:T(8,128)S(1)}, u32[]{:S(2)}, u32[]{:S(2)}) collective-permute-start(f32[128,128]{1,0:T(8,128)S(1)} %add_add_fusion.mine0), channel_id=1, source_target_pairs={{0,1},{1,0},{2,3},{3,2},{4,5},{5,4},{6,7},{7,6},{8,9},{9,8},{10,11... | collective-permute-start | bytes 196616 | tf_op jit(solution)/shard_map/ppermute | solution.py:336
  75.3 13.4 %collective-permute-start.18 = (f32[128,128]{1,0:T(8,128)S(1)}, f32[128,128]{1,0:T(8,128)S(1)}, u32[]{:S(2)}, u32[]{:S(2)}) collective-permute-start(f32[128,128]{1,0:T(8,128)S(1)} %get-tuple-element.21.mine1), channel_id=1, source_target_pairs={{0,1},{1,0},{2,3},{3,2},{4,5},{5,4},{6,7},{7,6},{8,9},{9,8},{10,11... | collective-permute-start | bytes 196616 | tf_op jit(solution)/shard_map/ppermute | solution.py:336

commit v3 on v2

--- a/solution.py
+++ b/solution.py
@@ -54,9 +54,7 @@
     pair_high, pair_low = bf16_pair(np.kron(np.eye(2), lateral))
     mix = np.concatenate([rows_high, rows_low], axis=0)
     total = levels * rows
-    own = mix[:, total : 2 * total]
-    sides = np.concatenate([mix[:, :total], mix[:, 2 * total :]], axis=1)
-    return mix, own, sides, pair_high, pair_low
+    return mix, [mix[:, i : i + total] for i in range(0, 3 * total, total)], pair_high, pair_low
 
 
 def split(x):
@@ -114,25 +112,32 @@
     return jnp.where(lax.broadcasted_iota(jnp.int32, (1, slots), 1) < count_ref[0], 1.0, 0.0)
 
 
-def localized(first, p_refs, g_refs, rows_ref, pair_high_ref, pair_low_ref):
+def mixed_pairs(p_refs, g_refs, rows_ref, mixed):
     total = g_refs[0].shape[0]
-    sides = []
-    for member in (first, first + 1):
-        sides.append(jnp.concatenate([p[member].astype(F32) * g[...] for p, g in zip(p_refs, g_refs)], axis=0))
-    high, low = split(jnp.concatenate(sides, axis=1))
-    mixed = dot(rows_ref[...], high)
-    mixed = mixed[:total] + mixed[total:] + dot(rows_ref[:total], low)
-    high, low = split(mixed)
-    across = dot(jnp.concatenate([high, low], axis=0), pair_high_ref[...])
-    return across[:total] + across[total:] + dot(high, pair_low_ref[...])
-
-
-def summed_members(field, weigh, p_refs, g_refs, rows_ref, pair_high_ref, pair_low_ref):
+    for pair in range(mixed.shape[0]):
+        sides = []
+        for member in (2 * pair, 2 * pair + 1):
+            sides.append(jnp.concatenate([p[member].astype(F32) * g[...] for p, g in zip(p_refs, g_refs)], axis=0))
+        high, low = split(jnp.concatenate(sides, axis=1))
+        product = dot(rows_ref[...], high)
+        high, low = split(product[:total] + product[total:] + dot(rows_ref[:total], low))
+        mixed[pair, :total] = high
+        mixed[pair, total:] = low
+
+
+def across_columns(pair, mixed, pair_high_ref, pair_low_ref):
+    total = mixed.shape[1] // 2
+    product = dot(mixed[pair], pair_high_ref[...])
+    return product[:total] + product[total:] + dot(mixed[pair, :total], pair_low_ref[...])
+
+
+def summed_members(field, weigh, p_refs, g_refs, rows_ref, pair_high_ref, pair_low_ref, mixed):
     columns = g_refs[0].shape[1]
-    for first in range(0, weigh.shape[0], 2):
-        spread = localized(first, p_refs, g_refs, rows_ref, pair_high_ref, pair_low_ref)
-        field = field + weigh[first].astype(F32) * spread[:, :columns]
-        field = field + weigh[first + 1].astype(F32) * spread[:, columns:]
+    mixed_pairs(p_refs, g_refs, rows_ref, mixed)
+    for pair in range(mixed.shape[0]):
+        spread = across_columns(pair, mixed, pair_high_ref, pair_low_ref)
+        field = field + weigh[2 * pair].astype(F32) * spread[:, :columns]
+        field = field + weigh[2 * pair + 1].astype(F32) * spread[:, columns:]
     return field
 
 
@@ -150,20 +155,33 @@
     field[...] = adjoint(values, weights, cell, rows, columns)
 
 
-def own_kernel(p, g, mix, pair_high, pair_low, field):
-    field[...] = summed_members(jnp.zeros(g.shape, F32), p, [p], [g], mix, pair_high, pair_low)
-
-
-def forward_kernel(rows, columns, count, place, p0, p, p2, g0, g2, own, mix, pair_high, pair_low, weights, cell, kept, given, whole):
-    field = summed_members(own[...], p, [p0, p2], [g0, g2], mix, pair_high, pair_low)
-    whole[...] = field
-    observed = as_rows(observe(field, weights, cell, live_slots(count, weights.shape[1]), rows, columns))
+def own_kernel(p, g, mix, pair_high, pair_low, field, mixed):
+    field[...] = summed_members(jnp.zeros(g.shape, F32), p, [p], [g], mix, pair_high, pair_low, mixed)
+
+
+def side_kernel(p, p_side, g_side, part, mix, pair_high, pair_low, field, mixed):
+    field[...] = summed_members(part[...], p, [p_side], [g_side], mix, pair_high, pair_low, mixed)
+
+
+def first_kernel(rows, columns, count, p, p_side, g_side, part, mix, pair_high, pair_low, weights, cell, observed, field, mixed):
+    whole = summed_members(part[...], p, [p_side], [g_side], mix, pair_high, pair_low, mixed)
+    observed[...] = as_rows(observe(whole, weights, cell, live_slots(count, weights.shape[1]), rows, columns))
+    field[...] = whole
+
+
+def second_kernel(rows, columns, count, place, p, p_side, g_side, part, mix, pair_high, pair_low, weights, cell, field0,
+                  kept, given, field1, mixed):
+    whole = summed_members(part[...], p, [p_side], [g_side], mix, pair_high, pair_low, mixed)
+    field1[...] = whole
+    observed = as_rows(observe(whole, weights, cell, live_slots(count, weights.shape[1]), rows, columns))
     lines = observed.shape[0]
-    half = field.shape[0] // CORES
+    half = whole.shape[0] // CORES
     core = lax.rem(place[0], CORES)
     for message, at in ((kept, core), (given, 1 - core)):
+        rows_of_half = pl.ds(pl.multiple_of(at * half, half), half)
         message[:lines] = observed
-        message[lines:] = whole[pl.ds(pl.multiple_of(at * half, half), half)]
+        message[lines : lines + half] = field0[rows_of_half]
+        message[lines + half :] = field1[rows_of_half]
 
 
 def middle_kernel(rows, columns, count, *refs):
@@ -173,19 +191,22 @@
     field[...] = adjoint(precision[...] * as_line(summed), weights, cell, rows, columns)
 
 
-def alpha_kernel(p0, p1, p2, g0, g1, g2, mix, pair_high, pair_low, after, alpha):
+def alpha_kernel(p0, p1, p2, g0, g1, g2, mix, pair_high, pair_low, after, alpha, mixed):
     columns = g0.shape[1]
-    for first in range(0, p0.shape[0], 2):
-        spread = localized(first, (p0, p1, p2), (g0, g1, g2), mix, pair_high, pair_low)
-        alpha[first] = spread[:, :columns]
-        alpha[first + 1] = spread[:, columns:]
+    mixed_pairs((p0, p1, p2), (g0, g1, g2), mix, mixed)
+    for pair in range(mixed.shape[0]):
+        spread = across_columns(pair, mixed, pair_high, pair_low)
+        alpha[2 * pair] = spread[:, :columns]
+        alpha[2 * pair + 1] = spread[:, columns:]
 
 
 def scalars_kernel(count, *refs):
-    *messages, once, precision, innovations, after, scalars, half = refs
+    *messages, once, precision, innovations, after, scalars, halves = refs
     lines = once.shape[0]
     z2 = sum(message[:lines] for message in messages)
-    half[...] = sum(message[lines:] for message in messages)
+    half = halves.shape[1]
+    for i in range(2):
+        halves[i] = sum(message[lines + i * half : lines + (i + 1) * half] for message in messages)
     z1 = once[...]
     rho = precision[...]
     slot = lax.broadcasted_iota(jnp.int32, rho.shape, 0) * rho.shape[1] + lax.broadcasted_iota(jnp.int32, rho.shape, 1)
@@ -244,18 +265,14 @@
     return step0 + step1 * (1.0 - step0 + beta), -step1 * step0
 
 
-def final_kernel(scalars, alpha0, alpha1, alpha):
+def final_kernel(place, scalars, alpha0, alpha1, mine, other, alpha, increment):
     first, second = combination(scalars)
     for member in range(alpha.shape[0]):
         alpha[member] = first * alpha0[member] + second * alpha1[member]
-
-
-def increment_kernel(place, scalars, mine0, mine1, other0, other1, increment):
-    first, second = combination(scalars)
     core = lax.rem(place[0], CORES)
-    half = mine0.shape[0]
-    for part0, part1, at in ((mine0, mine1, core), (other0, other1, 1 - core)):
-        increment[pl.ds(pl.multiple_of(at * half, half), half)] = first * part0[...] + second * part1[...]
+    half = mine.shape[1]
+    for part, at in ((mine, core), (other, 1 - core)):
+        increment[pl.ds(pl.multiple_of(at * half, half), half)] = first * part[0] + second * part[1]
 
 
 def in_vmem(x):
@@ -298,11 +315,10 @@
     ens, tiles = lax.axis_size("ens"), lax.axis_size("tile")
     everyone = ens * members
     lines = slots // 128
-    _, own2, sides2, high2, low2 = local_matrices(levels, rows, columns, 2, 1.0 / everyone)
-    mix1, _, _, high1, low1 = local_matrices(levels, rows, columns, 1, 1.0 / math.sqrt(everyone))
+    _, mix2, high2, low2 = local_matrices(levels, rows, columns, 2, 1.0 / everyone)
+    mix1, _, high1, low1 = local_matrices(levels, rows, columns, 1, 1.0 / math.sqrt(everyone))
 
     p = perturbations.reshape(members, cells, columns)
-    p_before, p_after = neighbours(p)
     cell = obs_cell.reshape(1, slots)
     precision = obs_precision.reshape(1, slots)
     innovations_line = innovations.reshape(1, slots)
@@ -320,17 +336,11 @@
     place = lax.axis_index("ens").reshape(1)
     vmem = lambda *xs: [in_vmem(x) for x in xs]
 
-    def own(g):
-        return call(own_kernel, field_shape, vmem(p, g, own2, high2, low2))
-
-    def forward(own_part, g_before, g_after):
-        kept, given = call(
-            bound(forward_kernel), [(lines + half, columns)] * 2,
-            [in_smem(obs_count), in_smem(place)]
-            + vmem(p_before, p, p_after, g_before, g_after, own_part, sides2, high2, low2, obs_weights, cell),
-            [pltpu.VMEM(field_shape, F32)],
-        )
-        return kept + other_core(given)
+    mixed = pltpu.VMEM((members // 2, 2 * cells, CORES * columns), BF16)
+
+    def own_and_after(g, g_after):
+        part = call(own_kernel, field_shape, vmem(p, g, mix2[1], high2, low2), [mixed])
+        return call(side_kernel, field_shape, vmem(p, p_after, g_after, part, mix2[2], high2, low2), [mixed])
 
     def other_core(x):
         return lax.ppermute(x, "ens", [(i, i ^ 1) for i in range(ens)])
@@ -345,38 +355,50 @@
     def alpha_of(g, g_before, g_after, after):
         return call(
             alpha_kernel, (members, cells, columns),
-            vmem(p_before, p, p_after, g_before, g, g_after, mix1, high1, low1) + [anywhere(after)],
+            vmem(p_before, p, p_after, g_before, g, g_after, mix1, high1, low1) + [anywhere(after)], [mixed],
         )
 
+    p_before, p_after = neighbours(p)
     g0 = call(
         bound(start_kernel), field_shape,
         [in_smem(obs_count)] + vmem(obs_weights, cell, precision, innovations_line),
     )
     g0_before, g0_after = neighbours(g0)
-    sent = forward(own(g0), g0_before, g0_after)
-    messages = from_chips(sent[:lines])
+    part = own_and_after(g0, g0_after)
+    seen, field0 = call(
+        bound(first_kernel), [(lines, columns), field_shape],
+        [in_smem(obs_count)] + vmem(p, p_before, g0_before, part, mix2[0], high2, low2, obs_weights, cell), [mixed],
+    )
+    sent = seen + other_core(seen)
+    messages = from_chips(sent)
     alpha0 = alpha_of(g0, g0_before, g0_after, sent)
     g1, once = call(
         bound(middle_kernel), [field_shape, (lines, 128)],
         [in_smem(obs_count)] + vmem(*messages, obs_weights, cell, precision) + [anywhere(alpha0)],
     )
     g1_before, g1_after = neighbours(g1)
-    own_part = own(g1)
-    half0, own_part = lax.optimization_barrier((sent[lines:], own_part))
-    half0 = sum(from_chips(half0))
-    sent = forward(own_part, g1_before, g1_after)
+    part = own_and_after(g1, g1_after)
+    message = (lines + 2 * half, columns)
+    kept, given = call(
+        bound(second_kernel), [message, message],
+        [in_smem(obs_count), in_smem(place)]
+        + vmem(p, p_before, g1_before, part, mix2[0], high2, low2, obs_weights, cell, field0),
+        [pltpu.VMEM(field_shape, F32), mixed],
+    )
+    sent = kept + other_core(given)
     messages = from_chips(sent)
     alpha1 = alpha_of(g1, g1_before, g1_after, sent)
-    scalars, half1 = call(
-        scalars_kernel, [(tiles, 128), (half, columns)],
-        [in_smem(obs_count)] + vmem(*messages, once, obs_precision.reshape(lines, 128), innovations.reshape(lines, 128))
+    scalars, mine = call(
+        scalars_kernel, [(tiles, 128), (2, half, columns)],
+        [in_smem(obs_count)]
+        + vmem(*messages, once, obs_precision.reshape(lines, 128), innovations.reshape(lines, 128))
         + [anywhere(alpha1)],
     )
-    other0, other1 = other_core(half0), other_core(half1)
+    other = other_core(mine)
     scalars = lax.all_to_all(scalars.reshape(tiles, 1, 128), "tile", 0, 0).reshape(tiles, 128)
-    alpha = call(final_kernel, (members, cells, columns), vmem(scalars, alpha0, alpha1))
-    increment = call(
-        increment_kernel, field_shape, [in_smem(place)] + vmem(scalars, half0, half1, other0, other1)
+    alpha, increment = call(
+        final_kernel, [(members, cells, columns), field_shape],
+        [in_smem(place)] + vmem(scalars, alpha0, alpha1, mine, other),
     )
     return alpha.reshape(perturbations.shape), increment.reshape(levels, rows, columns)
 

time: 90.2 us -> 86.1 us (0.955)
  starting transfers between devices: 31.7 us -> 27.4 us
  Pallas kernels: 24.2 us -> 21 us
  local copies, waits for them, and re-layouts: 6.89 us -> 8.5 us
  waiting for transfers between devices: 13.9 us -> 15.1 us
    ppermute x9 -> x6, starting transfers between devices: 10.9 us -> 6.13 us  [from_chips(): arrived.append(lax.ppermute(x, 'ens', route))]
    ppermute x9 -> x6, waiting for transfers between devices: 1.64 us -> 5.32 us  [from_chips(): arrived.append(lax.ppermute(x, 'ens', route))]
    ppermute x6, waiting for transfers between devices: 11.4 us -> 7.91 us  [neighbours(): return (lax.ppermute(x, 'tile', up), lax.ppermute(x, 'tile', down))]
    pallas_call x11 -> x12, Pallas kernels: 24.2 us -> 21 us  [call(): pl.pallas_call(kernel, out_shape=shapes[0] if single else shapes, in_spec...]
    unnamed x38 -> x62, local copies, waits for them, and re-layouts: 6.89 us -> 8.5 us
    ppermute x4 -> x3, waiting for transfers between devices: 0.92 us -> 1.83 us  [other_core(): return lax.ppermute(x, 'ens', [(i, i ^ 1) for i in range(ens)])]
    ppermute x4 -> x3, starting transfers between devices: 5.71 us -> 6.27 us  [other_core(): return lax.ppermute(x, 'ens', [(i, i ^ 1) for i in range(ens)])]
  transfers between devices with their start and end apart: 19 -> 15, of which waited for: 6 -> 9; matrix products, arithmetic and copies ran while one was open for 0% -> 0% of each run, Pallas kernels for 16% -> 16%
where the time goes in v3:
time: 86.1 us; the launch traced here: 85.6 us
  starting transfers between devices  27.4 us (32%)
  Pallas kernels  21 us (24%)
  waiting for transfers between devices  15.1 us (18%)
  blocking collectives  12 us (14%)
  local copies, waits for them, and re-layouts  8.5 us (10%)
  between operations  1.59 us (2%)
    pallas_call x12, Pallas kernels, call(): pl.pallas_call(kernel, out_shape=shapes[0] if single else shapes, in_spec...  21 us
    ppermute x6, starting transfers between devices, neighbours(): return (lax.ppermute(x, 'tile', up), lax.ppermute(x, 'tile', down))  15 us
    all_to_all x1, blocking collectives, local(): lax.all_to_all(scalars.reshape(tiles, 1, 128), 'tile', 0, 0)  12 us
    unnamed x62, local copies, waits for them, and re-layouts  8.5 us
    ppermute x6, waiting for transfers between devices, neighbours(): return (lax.ppermute(x, 'tile', up), lax.ppermute(x, 'tile', down))  7.91 us
    ppermute x3, starting transfers between devices, other_core(): return lax.ppermute(x, 'ens', [(i, i ^ 1) for i in range(ens)])  6.27 us
    ppermute x6, starting transfers between devices, from_chips(): arrived.append(lax.ppermute(x, 'ens', route))  6.13 us
    ppermute x6, waiting for transfers between devices, from_chips(): arrived.append(lax.ppermute(x, 'ens', route))  5.32 us
  transfers between devices with their start and end apart: 15, of which 9 were waited for; matrix products, arithmetic and copies ran while one was open for 0% of the time, Pallas kernels for 16%

profile of v3, /device:TPU:1, one launch (start us, length us, event | category | flops | bytes accessed | tf_op | source)
XLA Modules:
  0.0 85.6 jit_solution(3687880162351070163)
XLA Ops:
  0.6 8.7 %collective-permute-start.2 = (bf16[10,256,128]{2,1,0:T(8,128)(2,1)}, bf16[10,256,128]{2,1,0:T(8,128)(2,1)S(1)}, u32[]{:S(2)}, u32[]{:S(2)}) collective-permute-start(bf16[10,256,128]{2,1,0:T(8,128)(2,1)} %bitcast.13), channel_id=1, source_target_pairs={{8,0},{16,8},{24,16},{32,24},{40,32},{48,40},{56,48},{64,56},{72,6... | collective-permute-start | bytes 1966088 | tf_op jit(solution)/shard_map/ppermute | solution.py:308
  10.0 0.9 %copy-done.8 = f32[16,2048]{1,0:T(8,128)S(1)} copy-done((f32[16,2048]{1,0:T(8,128)S(1)}, f32[16,2048]{1,0:T(8,128)}, u32[]{:S(2)}) %copy-start.8) | copy-done | bytes 131096
  10.9 0.7 copy-done.21
  11.6 0.7 copy-done.25
  12.3 0.7 copy-done.27
  13.0 0.7 shard_map.149.g.g1
  13.7 4.9 %collective-permute-start.3 = (f32[256,128]{1,0:T(8,128)S(1)}, f32[256,128]{1,0:T(8,128)S(1)}, u32[]{:S(2)}, u32[]{:S(2)}) collective-permute-start(f32[256,128]{1,0:T(8,128)S(1)} %shard_map.149.g.g1), channel_id=1, source_target_pairs={{8,0},{16,8},{24,16},{32,24},{40,32},{48,40},{56,48},{64,56},{72,6... | collective-permute-start | bytes 393224 | tf_op jit(solution)/shard_map/ppermute | solution.py:308
  18.6 1.1 %copy-done = bf16[10,16,16,128]{3,2,1,0:T(8,128)(2,1)S(1)} copy-done((bf16[10,16,16,128]{3,2,1,0:T(8,128)(2,1)S(1)}, bf16[10,16,16,128]{3,2,1,0:T(8,128)(2,1)}, u32[]{:S(2)}) %copy-start) | copy-done | bytes 655384
  19.6 0.9 %copy-done.2 = bf16[256,256]{1,0:T(8,128)(2,1)S(1)} copy-done((bf16[256,256]{1,0:T(8,128)(2,1)S(1)}, bf16[256,256]{1,0:T(8,128)(2,1)}, u32[]{:S(2)}) %copy-start.2) | copy-done | bytes 131096
  20.6 0.9 %copy-done.4 = bf16[256,256]{1,0:T(8,128)(2,1)S(1)} copy-done((bf16[256,256]{1,0:T(8,128)(2,1)S(1)}, bf16[256,256]{1,0:T(8,128)(2,1)}, u32[]{:S(2)}) %copy-start.4) | copy-done | bytes 131096
  21.5 0.9 %copy-done.15 = bf16[512,256]{1,0:T(8,128)(2,1)S(1)} copy-done((bf16[512,256]{1,0:T(8,128)(2,1)S(1)}, bf16[512,256]{1,0:T(8,128)(2,1)}, u32[]{:S(2)}) %copy-start.15) | copy-done | bytes 262168
  22.4 1.2 %shard_map.150.part = f32[256,128]{1,0:T(8,128)S(1)} custom-call(bf16[10,256,128]{2,1,0:T(8,128)(2,1)S(1)} %bitcast.15, f32[256,128]{1,0:T(8,128)S(1)} %shard_map.149.g.g1, bf16[512,256]{1,0:T(8,128)(2,1)S(1)} %copy-done.15, bf16[256,256]{1,0:T(8,128)(2,1)S(1)} %copy-done.4, bf16[256,256]{1,0:T(8,128)(2,1)S(1)} %copy-done.2), custom_call_target="tpu_custom_call" | custom-call | tf_op jit(solution)/shard_map/pallas_call | solution.py:294
  23.6 0.0 copy-start.3
  23.6 0.0 copy-start.5
  23.7 2.0 %collective-permute-done.3.g_side.g2 = f32[256,128]{1,0:T(8,128)S(1)} collective-permute-done((f32[256,128]{1,0:T(8,128)S(1)}, f32[256,128]{1,0:T(8,128)S(1)}, u32[]{:S(2)}, u32[]{:S(2)}) %collective-permute-start.3) | collective-permute-done | bytes 131104 | tf_op jit(solution)/shard_map/ppermute | solution.py:308
  25.7 1.2 %shard_map.151.refs_4_ = f32[256,128]{1,0:T(8,128)S(1)} custom-call(bf16[10,256,128]{2,1,0:T(8,128)(2,1)S(1)} %bitcast.16, bf16[10,256,128]{2,1,0:T(8,128)(2,1)S(1)} %collective-permute-done.2.p_side.p2, f32[256,128]{1,0:T(8,128)S(1)} %collective-permute-done.3.g_side.g2, f32[256,128]{1,0:T(8,128)S(1)} %shard_map.150.part, bf16[512,256]{1,0:T(8,128)(2,1)S(1)} %copy-done.13, ...), custom_call_target="tpu_custom_call" | custom-call | tf_op jit(solution)/shard_map/pallas_call | solution.py:294
  27.0 0.0 copy-start.17
  27.0 3.9 %collective-permute-done.1.refs_3_.g0 = f32[256,128]{1,0:T(8,128)S(1)} collective-permute-done((f32[256,128]{1,0:T(8,128)S(1)}, f32[256,128]{1,0:T(8,128)S(1)}, u32[]{:S(2)}, u32[]{:S(2)}) %collective-permute-start.1) | collective-permute-done | bytes 131104 | tf_op jit(solution)/shard_map/ppermute | solution.py:308
  31.0 1.7 %shard_map.152 = (f32[16,128]{1,0:T(8,128)S(1)}, f32[256,128]{1,0:T(8,128)S(1)}) custom-call(s32[1]{0:T(128)S(6)} %copy.17.refs_0_.count, bf16[10,256,128]{2,1,0:T(8,128)(2,1)S(1)} %bitcast.17, bf16[10,256,128]{2,1,0:T(8,128)(2,1)S(1)} %collective-permute-done.refs_2_.p0.refs_3_, f32[256,128]{1,0:T(8,128)S(1)} %collective-permute-done.1.refs_3_.g0, ...), custom_call_target="tpu_custom_call" | custom-call | tf_op jit(solution)/shard_map/pallas_call | solution.py:294
  32.7 1.9 %collective-permute-start.4 = (f32[16,128]{1,0:T(8,128)S(1)}, f32[16,128]{1,0:T(8,128)S(1)}, u32[]{:S(2)}, u32[]{:S(2)}) collective-permute-start(f32[16,128]{1,0:T(8,128)S(1)} %get-tuple-element.12), channel_id=1, source_target_pairs={{0,1},{1,0},{2,3},{3,2},{4,5},{5,4},{6,7},{7,6},{8,9},{9,8},{10,11... | collective-permute-start | bytes 24584 | tf_op jit(solution)/shard_map/ppermute | solution.py:346
  34.6 0.8 collective-permute-done.4
  35.5 2.7 %collective-permute-start.7 = (f32[16,128]{1,0:T(8,128)S(1)}, f32[16,128]{1,0:T(8,128)S(1)}, u32[]{:S(2)}, u32[]{:S(2)}) collective-permute-start(f32[16,128]{1,0:T(8,128)S(1)} %add.6.after.refs_1_), channel_id=1, source_target_pairs={{0,6},{1,7},{2,0},{3,1},{4,2},{5,3},{6,4},{7,5},{8,14},{9,15},{10,... | collective-permute-start | bytes 24584 | tf_op jit(solution)/shard_map/ppermute | solution.py:352
  38.2 0.4 collective-permute-start.6
  38.5 0.7 collective-permute-start.5
  39.2 2.4 %shard_map.153.refs_8_.alpha0 = f32[10,256,128]{2,1,0:T(8,128)S(1)} custom-call(bf16[10,256,128]{2,1,0:T(8,128)(2,1)S(1)} %collective-permute-done.refs_2_.p0.refs_3_, bf16[10,256,128]{2,1,0:T(8,128)(2,1)S(1)} %bitcast.18, bf16[10,256,128]{2,1,0:T(8,128)(2,1)S(1)} %collective-permute-done.2.p_side.p2, f32[256,128]{1,0:T(8,128)S(1)} %collective-permute-done.1.refs_3_.g0, ...), custom_call_target="tpu_custom_call" | custom-call | tf_op jit(solution)/shard_map/pallas_call | solution.py:294
  41.7 0.5 collective-permute-done.6.refs_3_
  42.2 0.1 collective-permute-done.5.refs_2_
  42.3 1.4 %shard_map.154 = (f32[256,128]{1,0:T(8,128)}, f32[16,128]{1,0:T(8,128)S(1)}) custom-call(s32[1]{0:T(128)S(6)} %copy.17.refs_0_.count, f32[16,128]{1,0:T(8,128)S(1)} %add.6.after.refs_1_, f32[16,128]{1,0:T(8,128)S(1)} %collective-permute-done.5.refs_2_, f32[16,128]{1,0:T(8,128)S(1)} %collective-permute-done.6.refs_3_, ...), custom_call_target="tpu_custom_call" | custom-call | tf_op jit(solution)/shard_map/pallas_call | solution.py:294
  43.7 0.6 copy-done.29
  44.3 1.3 %collective-permute-start.9 = (f32[256,128]{1,0:T(8,128)}, f32[256,128]{1,0:T(8,128)}, u32[]{:S(2)}, u32[]{:S(2)}) collective-permute-start(f32[256,128]{1,0:T(8,128)} %get-tuple-element.13.g.g1), channel_id=1, source_target_pairs={{8,0},{16,8},{24,16},{32,24},{40,32},{48,40},{56,48},{64,56},{72,6... | collective-permute-start | bytes 393224 | tf_op jit(solution)/shard_map/ppermute | solution.py:308
  45.6 0.2 collective-permute-start.8
  45.7 0.9 %copy-done.16 = bf16[512,256]{1,0:T(8,128)(2,1)S(1)} copy-done((bf16[512,256]{1,0:T(8,128)(2,1)S(1)}, bf16[512,256]{1,0:T(8,128)(2,1)}, u32[]{:S(2)}) %copy-start.16) | copy-done | bytes 262168
  46.7 2.2 %shard_map.155.part = f32[256,128]{1,0:T(8,128)S(1)} custom-call(bf16[10,256,128]{2,1,0:T(8,128)(2,1)S(1)} %bitcast.19, f32[256,128]{1,0:T(8,128)} %get-tuple-element.13.g.g1, bf16[512,256]{1,0:T(8,128)(2,1)S(1)} %copy-done.16, bf16[256,256]{1,0:T(8,128)(2,1)S(1)} %copy-done.5, bf16[256,256]{1,0:T(8,128)(2,1)S(1)} %copy-done.3), custom_call_target="tpu_custom_call" | custom-call | tf_op jit(solution)/shard_map/pallas_call | solution.py:294
  48.9 2.2 %shard_map.156.refs_5_ = f32[256,128]{1,0:T(8,128)S(1)} custom-call(bf16[10,256,128]{2,1,0:T(8,128)(2,1)S(1)} %bitcast.20, bf16[10,256,128]{2,1,0:T(8,128)(2,1)S(1)} %collective-permute-done.2.p_side.p2, f32[256,128]{1,0:T(8,128)} %collective-permute-done.9.g_side.g2, f32[256,128]{1,0:T(8,128)S(1)} %shard_map.155.part, bf16[512,256]{1,0:T(8,128)(2,1)S(1)} %copy-done.14, ...), custom_call_target="tpu_custom_call" | custom-call | tf_op jit(solution)/shard_map/pallas_call | solution.py:294
  51.1 1.9 %collective-permute-done.8.refs_4_.g0 = f32[256,128]{1,0:T(8,128)} collective-permute-done((f32[256,128]{1,0:T(8,128)}, f32[256,128]{1,0:T(8,128)}, u32[]{:S(2)}, u32[]{:S(2)}) %collective-permute-start.8) | collective-permute-done | bytes 131104 | tf_op jit(solution)/shard_map/ppermute | solution.py:308
  53.1 2.7 %shard_map.157 = (f32[272,128]{1,0:T(8,128)S(1)}, f32[272,128]{1,0:T(8,128)S(1)}) custom-call(s32[1]{0:T(128)S(6)} %copy.17.refs_0_.count, s32[1]{0:T(128)} %bitcast.refs_1_.place, bf16[10,256,128]{2,1,0:T(8,128)(2,1)S(1)} %bitcast.21, bf16[10,256,128]{2,1,0:T(8,128)(2,1)S(1)} %collective-permute-done.refs_2_.p0.refs_3_, ...), custom_call_target="tpu_custom_call" | custom-call | tf_op jit(solution)/shard_map/pallas_call | solution.py:294
  55.8 3.5 %collective-permute-start.10 = (f32[272,128]{1,0:T(8,128)S(1)}, f32[272,128]{1,0:T(8,128)S(1)}, u32[]{:S(2)}, u32[]{:S(2)}) collective-permute-start(f32[272,128]{1,0:T(8,128)S(1)} %get-tuple-element.16), channel_id=1, source_target_pairs={{0,1},{1,0},{2,3},{3,2},{4,5},{5,4},{6,7},{7,6},{8,9},{9,8},{10,11... | collective-permute-start | bytes 417800 | tf_op jit(solution)/shard_map/ppermute | solution.py:346
  59.3 1.0 %collective-permute-done.10 = f32[272,128]{1,0:T(8,128)S(1)} collective-permute-done((f32[272,128]{1,0:T(8,128)S(1)}, f32[272,128]{1,0:T(8,128)S(1)}, u32[]{:S(2)}, u32[]{:S(2)}) %collective-permute-start.10) | collective-permute-done | bytes 139296 | tf_op jit(solution)/shard_map/ppermute | solution.py:346
  60.4 0.6 collective-permute-start.13
  61.0 1.4 %collective-permute-start.12 = (f32[272,128]{1,0:T(8,128)S(1)}, f32[272,128]{1,0:T(8,128)S(1)}, u32[]{:S(2)}, u32[]{:S(2)}) collective-permute-start(f32[272,128]{1,0:T(8,128)S(1)} %add.7.after.refs_0_), channel_id=1, source_target_pairs={{0,4},{1,5},{2,6},{3,7},{4,0},{5,1},{6,2},{7,3},{8,12},{9,13},{10,... | collective-permute-start | bytes 417800 | tf_op jit(solution)/shard_map/ppermute | solution.py:352
  62.4 0.3 collective-permute-start.11
  62.7 3.4 %shard_map.158.refs_7_.alpha1 = f32[10,256,128]{2,1,0:T(8,128)S(1)} custom-call(bf16[10,256,128]{2,1,0:T(8,128)(2,1)S(1)} %collective-permute-done.refs_2_.p0.refs_3_, bf16[10,256,128]{2,1,0:T(8,128)(2,1)S(1)} %bitcast.22, bf16[10,256,128]{2,1,0:T(8,128)(2,1)S(1)} %collective-permute-done.2.p_side.p2, f32[256,128]{1,0:T(8,128)} %collective-permute-done.8.refs_4_.g0, ...), custom_call_target="tpu_custom_call" | custom-call | tf_op jit(solution)/shard_map/pallas_call | solution.py:294
  66.2 0.9 %collective-permute-done.12.refs_2_ = f32[272,128]{1,0:T(8,128)S(1)} collective-permute-done((f32[272,128]{1,0:T(8,128)S(1)}, f32[272,128]{1,0:T(8,128)S(1)}, u32[]{:S(2)}, u32[]{:S(2)}) %collective-permute-start.12) | collective-permute-done | bytes 139296 | tf_op jit(solution)/shard_map/ppermute | solution.py:352
  67.1 3.8 %collective-permute-done.11.refs_1_ = f32[272,128]{1,0:T(8,128)S(1)} collective-permute-done((f32[272,128]{1,0:T(8,128)S(1)}, f32[272,128]{1,0:T(8,128)S(1)}, u32[]{:S(2)}, u32[]{:S(2)}) %collective-permute-start.11) | collective-permute-done | bytes 139296 | tf_op jit(solution)/shard_map/ppermute | solution.py:352
  70.9 0.2 shard_map.159
  71.1 0.8 collective-permute-start.14
  71.8 12.0 %all_to_all.5 = f32[32,1,128]{2,1,0:T(1,128)S(1)} all-to-all(f32[32,1,128]{2,1,0:T(1,128)S(1)} %bitcast.33), channel_id=1, replica_groups=mesh['tile'=32,'ens'=8] {'tile'}, dimensions={0} | all-to-all | bytes 32768 | tf_op jit(solution)/shard_map/all_to_all | solution.py:398
  83.8 1.8 %shard_map.160 = (f32[10,256,128]{2,1,0:T(8,128)}, f32[256,128]{1,0:T(8,128)}) custom-call(s32[1]{0:T(128)} %bitcast.refs_1_.place, f32[32,128]{1,0:T(8,128)S(1)} %bitcast.30, f32[10,256,128]{2,1,0:T(8,128)S(1)} %shard_map.153.refs_8_.alpha0, f32[10,256,128]{2,1,0:T(8,128)S(1)} %shard_map.158.refs_7_.alpha1, f32[2,128,128]{2,1,0:T(8,128)S(1)} %get-tuple-element.19.mine, ...), custom_call_target="tpu_custom_call" | custom-call | tf_op jit(solution)/shard_map/pallas_call | solution.py:294
  (59 shorter events, 0.2 us)
Async XLA Ops:
  0.6 25.1 %collective-permute-start.2 = (bf16[10,256,128]{2,1,0:T(8,128)(2,1)}, bf16[10,256,128]{2,1,0:T(8,128)(2,1)S(1)}, u32[]{:S(2)}, u32[]{:S(2)}) collective-permute-start(bf16[10,256,128]{2,1,0:T(8,128)(2,1)} %bitcast.13), channel_id=1, source_target_pairs={{8,0},{16,8},{24,16},{32,24},{40,32},{48,40},{56,48},{64,56},{72,6... | collective-permute-start | bytes 1966088 | tf_op jit(solution)/shard_map/ppermute | solution.py:308
  9.3 21.6 %collective-permute-start = (bf16[10,256,128]{2,1,0:T(8,128)(2,1)}, bf16[10,256,128]{2,1,0:T(8,128)(2,1)S(1)}, u32[]{:S(2)}, u32[]{:S(2)}) collective-permute-start(bf16[10,256,128]{2,1,0:T(8,128)(2,1)} %bitcast.14), channel_id=1, source_target_pairs={{0,8},{8,16},{16,24},{24,32},{32,40},{40,48},{48,56},{56,64},{64,7... | collective-permute-start | bytes 1966088 | tf_op jit(solution)/shard_map/ppermute | solution.py:308
  10.0 0.9 %copy-start.8 = (f32[16,2048]{1,0:T(8,128)S(1)}, f32[16,2048]{1,0:T(8,128)}, u32[]{:S(2)}) copy-start(f32[16,2048]{1,0:T(8,128)} %refs_9_.1) | copy-start | bytes 393220
  10.9 0.7 copy-start.21
  11.6 0.7 copy-start.25
  12.3 0.7 copy-start.27
  13.0 12.8 %copy-start.13 = (bf16[512,256]{1,0:T(8,128)(2,1)S(1)}, bf16[512,256]{1,0:T(8,128)(2,1)}, u32[]{:S(2)}) copy-start(bf16[512,256]{1,0:T(8,128)(2,1)} %constant.23.clone.mix) | copy-start | bytes 786436
  13.7 12.0 %collective-permute-start.3 = (f32[256,128]{1,0:T(8,128)S(1)}, f32[256,128]{1,0:T(8,128)S(1)}, u32[]{:S(2)}, u32[]{:S(2)}) collective-permute-start(f32[256,128]{1,0:T(8,128)S(1)} %shard_map.149.g.g1), channel_id=1, source_target_pairs={{8,0},{16,8},{24,16},{32,24},{40,32},{48,40},{56,48},{64,56},{72,6... | collective-permute-start | bytes 393224 | tf_op jit(solution)/shard_map/ppermute | solution.py:308
  18.6 12.4 %collective-permute-start.1 = (f32[256,128]{1,0:T(8,128)S(1)}, f32[256,128]{1,0:T(8,128)S(1)}, u32[]{:S(2)}, u32[]{:S(2)}) collective-permute-start(f32[256,128]{1,0:T(8,128)S(1)} %shard_map.149.g.g1), channel_id=1, source_target_pairs={{0,8},{8,16},{16,24},{24,32},{32,40},{40,48},{48,56},{56,64},{64,7... | collective-permute-start | bytes 393224 | tf_op jit(solution)/shard_map/ppermute | solution.py:308
  18.6 1.1 %copy-start = (bf16[10,16,16,128]{3,2,1,0:T(8,128)(2,1)S(1)}, bf16[10,16,16,128]{3,2,1,0:T(8,128)(2,1)}, u32[]{:S(2)}) copy-start(bf16[10,16,16,128]{3,2,1,0:T(8,128)(2,1)} %param.14) | copy-start | bytes 1966084
  19.6 0.9 %copy-start.2 = (bf16[256,256]{1,0:T(8,128)(2,1)S(1)}, bf16[256,256]{1,0:T(8,128)(2,1)}, u32[]{:S(2)}) copy-start(bf16[256,256]{1,0:T(8,128)(2,1)} %constant.22.clone.pair_low.refs_7_.refs_8_) | copy-start | bytes 393220
  20.5 0.9 %copy-start.4 = (bf16[256,256]{1,0:T(8,128)(2,1)S(1)}, bf16[256,256]{1,0:T(8,128)(2,1)}, u32[]{:S(2)}) copy-start(bf16[256,256]{1,0:T(8,128)(2,1)} %constant.21.clone.pair_high.refs_6_.refs_7_) | copy-start | bytes 393220
  21.5 0.9 %copy-start.15 = (bf16[512,256]{1,0:T(8,128)(2,1)S(1)}, bf16[512,256]{1,0:T(8,128)(2,1)}, u32[]{:S(2)}) copy-start(bf16[512,256]{1,0:T(8,128)(2,1)} %constant.20.clone.mix) | copy-start | bytes 786436
  22.4 3.3 %copy-start.1 = (bf16[10,16,16,128]{3,2,1,0:T(8,128)(2,1)S(1)}, bf16[10,16,16,128]{3,2,1,0:T(8,128)(2,1)}, u32[]{:S(2)}) copy-start(bf16[10,16,16,128]{3,2,1,0:T(8,128)(2,1)} %param.14) | copy-start | bytes 1966084
  23.6 7.3 %copy-start.3 = (bf16[256,256]{1,0:T(8,128)(2,1)S(1)}, bf16[256,256]{1,0:T(8,128)(2,1)}, u32[]{:S(2)}) copy-start(bf16[256,256]{1,0:T(8,128)(2,1)} %constant.22.clone.pair_low.refs_7_.refs_8_) | copy-start | bytes 393220
  23.6 7.3 %copy-start.5 = (bf16[256,256]{1,0:T(8,128)(2,1)S(1)}, bf16[256,256]{1,0:T(8,128)(2,1)}, u32[]{:S(2)}) copy-start(bf16[256,256]{1,0:T(8,128)(2,1)} %constant.21.clone.pair_high.refs_6_.refs_7_) | copy-start | bytes 393220
  23.7 7.3 %copy-start.9 = (f32[16,2048]{1,0:T(8,128)S(1)}, f32[16,2048]{1,0:T(8,128)}, u32[]{:S(2)}) copy-start(f32[16,2048]{1,0:T(8,128)} %refs_9_.1) | copy-start | bytes 393220
  23.7 7.3 %copy-start.11 = (bf16[512,256]{1,0:T(8,128)(2,1)S(1)}, bf16[512,256]{1,0:T(8,128)(2,1)}, u32[]{:S(2)}) copy-start(bf16[512,256]{1,0:T(8,128)(2,1)} %constant.24.clone.refs_5_.refs_6_) | copy-start | bytes 786436
  23.7 7.3 %copy-start.22 = (s32[2048]{0:T(1024)S(1)}, s32[2048]{0:T(1024)}, u32[]{:S(2)}) copy-start(s32[2048]{0:T(1024)} %param.18) | copy-start | bytes 24580
  27.0 12.3 %copy-start.6 = (bf16[512,768]{1,0:T(8,128)(2,1)S(1)}, bf16[512,768]{1,0:T(8,128)(2,1)}, u32[]{:S(2)}) copy-start(bf16[512,768]{1,0:T(8,128)(2,1)} %constant.25.clone.mix) | copy-start | bytes 2359300
  27.0 12.3 %copy-start.17 = (bf16[256,256]{1,0:T(8,128)(2,1)S(1)}, bf16[256,256]{1,0:T(8,128)(2,1)}, u32[]{:S(2)}) copy-start(bf16[256,256]{1,0:T(8,128)(2,1)} %constant.27.clone.pair_low) | copy-start | bytes 393220
  27.0 12.3 %copy-start.19 = (bf16[256,256]{1,0:T(8,128)(2,1)S(1)}, bf16[256,256]{1,0:T(8,128)(2,1)}, u32[]{:S(2)}) copy-start(bf16[256,256]{1,0:T(8,128)(2,1)} %constant.26.clone.pair_high) | copy-start | bytes 393220
  32.7 9.0 %copy-start.23 = (f32[256,128]{1,0:T(8,128)}, f32[256,128]{1,0:T(8,128)S(1)}, u32[]{:S(2)}) copy-start(f32[256,128]{1,0:T(8,128)S(1)} %get-tuple-element.14.refs_11_) | copy-start | bytes 393220
  32.7 2.8 %collective-permute-start.4 = (f32[16,128]{1,0:T(8,128)S(1)}, f32[16,128]{1,0:T(8,128)S(1)}, u32[]{:S(2)}, u32[]{:S(2)}) collective-permute-start(f32[16,128]{1,0:T(8,128)S(1)} %get-tuple-element.12), channel_id=1, source_target_pairs={{0,1},{1,0},{2,3},{3,2},{4,5},{5,4},{6,7},{7,6},{8,9},{9,8},{10,11... | collective-permute-start | bytes 24584 | tf_op jit(solution)/shard_map/ppermute | solution.py:346
  35.5 6.8 %copy-start.26 = (f32[2048]{0:T(1024)S(1)}, f32[2048]{0:T(1024)}, u32[]{:S(2)}) copy-start(f32[2048]{0:T(1024)} %param.16) | copy-start | bytes 24580
  35.5 6.2 %collective-permute-start.7 = (f32[16,128]{1,0:T(8,128)S(1)}, f32[16,128]{1,0:T(8,128)S(1)}, u32[]{:S(2)}, u32[]{:S(2)}) collective-permute-start(f32[16,128]{1,0:T(8,128)S(1)} %add.6.after.refs_1_), channel_id=1, source_target_pairs={{0,6},{1,7},{2,0},{3,1},{4,2},{5,3},{6,4},{7,5},{8,14},{9,15},{10,... | collective-permute-start | bytes 24584 | tf_op jit(solution)/shard_map/ppermute | solution.py:352
  38.2 4.0 %collective-permute-start.6 = (f32[16,128]{1,0:T(8,128)S(1)}, f32[16,128]{1,0:T(8,128)S(1)}, u32[]{:S(2)}, u32[]{:S(2)}) collective-permute-start(f32[16,128]{1,0:T(8,128)S(1)} %add.6.after.refs_1_), channel_id=1, source_target_pairs={{0,4},{1,5},{2,6},{3,7},{4,0},{5,1},{6,2},{7,3},{8,12},{9,13},{10,... | collective-permute-start | bytes 24584 | tf_op jit(solution)/shard_map/ppermute | solution.py:352
  38.5 3.7 %collective-permute-start.5 = (f32[16,128]{1,0:T(8,128)S(1)}, f32[16,128]{1,0:T(8,128)S(1)}, u32[]{:S(2)}, u32[]{:S(2)}) collective-permute-start(f32[16,128]{1,0:T(8,128)S(1)} %add.6.after.refs_1_), channel_id=1, source_target_pairs={{0,2},{1,3},{2,4},{3,5},{4,6},{5,7},{6,0},{7,1},{8,10},{9,11},{10,... | collective-permute-start | bytes 24584 | tf_op jit(solution)/shard_map/ppermute | solution.py:352
  43.7 0.6 copy-start.29
  44.3 4.6 %collective-permute-start.9 = (f32[256,128]{1,0:T(8,128)}, f32[256,128]{1,0:T(8,128)}, u32[]{:S(2)}, u32[]{:S(2)}) collective-permute-start(f32[256,128]{1,0:T(8,128)} %get-tuple-element.13.g.g1), channel_id=1, source_target_pairs={{8,0},{16,8},{24,16},{32,24},{40,32},{48,40},{56,48},{64,56},{72,6... | collective-permute-start | bytes 393224 | tf_op jit(solution)/shard_map/ppermute | solution.py:308
  45.6 7.5 %collective-permute-start.8 = (f32[256,128]{1,0:T(8,128)}, f32[256,128]{1,0:T(8,128)}, u32[]{:S(2)}, u32[]{:S(2)}) collective-permute-start(f32[256,128]{1,0:T(8,128)} %get-tuple-element.13.g.g1), channel_id=1, source_target_pairs={{0,8},{8,16},{16,24},{24,32},{32,40},{40,48},{48,56},{56,64},{64,7... | collective-permute-start | bytes 393224 | tf_op jit(solution)/shard_map/ppermute | solution.py:308
  45.7 0.9 %copy-start.16 = (bf16[512,256]{1,0:T(8,128)(2,1)S(1)}, bf16[512,256]{1,0:T(8,128)(2,1)}, u32[]{:S(2)}) copy-start(bf16[512,256]{1,0:T(8,128)(2,1)} %constant.20.clone.mix) | copy-start | bytes 786436
  46.7 2.2 %copy-start.14 = (bf16[512,256]{1,0:T(8,128)(2,1)S(1)}, bf16[512,256]{1,0:T(8,128)(2,1)}, u32[]{:S(2)}) copy-start(bf16[512,256]{1,0:T(8,128)(2,1)} %constant.23.clone.mix) | copy-start | bytes 786436
  48.8 4.2 %copy-start.10 = (f32[16,2048]{1,0:T(8,128)S(1)}, f32[16,2048]{1,0:T(8,128)}, u32[]{:S(2)}) copy-start(f32[16,2048]{1,0:T(8,128)} %refs_9_.1) | copy-start | bytes 393220
  48.9 4.2 %copy-start.12 = (bf16[512,256]{1,0:T(8,128)(2,1)S(1)}, bf16[512,256]{1,0:T(8,128)(2,1)}, u32[]{:S(2)}) copy-start(bf16[512,256]{1,0:T(8,128)(2,1)} %constant.24.clone.refs_5_.refs_6_) | copy-start | bytes 786436
  48.9 4.2 %copy-start.24 = (f32[256,128]{1,0:T(8,128)S(1)}, f32[256,128]{1,0:T(8,128)}, u32[]{:S(2)}) copy-start(f32[256,128]{1,0:T(8,128)} %copy-done.23) | copy-start | bytes 393220
  53.0 9.7 %copy-start.7 = (bf16[512,768]{1,0:T(8,128)(2,1)S(1)}, bf16[512,768]{1,0:T(8,128)(2,1)}, u32[]{:S(2)}) copy-start(bf16[512,768]{1,0:T(8,128)(2,1)} %constant.25.clone.mix) | copy-start | bytes 2359300
  53.0 9.7 %copy-start.18 = (bf16[256,256]{1,0:T(8,128)(2,1)S(1)}, bf16[256,256]{1,0:T(8,128)(2,1)}, u32[]{:S(2)}) copy-start(bf16[256,256]{1,0:T(8,128)(2,1)} %constant.27.clone.pair_low) | copy-start | bytes 393220
  53.1 9.7 %copy-start.20 = (bf16[256,256]{1,0:T(8,128)(2,1)S(1)}, bf16[256,256]{1,0:T(8,128)(2,1)}, u32[]{:S(2)}) copy-start(bf16[256,256]{1,0:T(8,128)(2,1)} %constant.26.clone.pair_high) | copy-start | bytes 393220
  55.8 4.5 %collective-permute-start.10 = (f32[272,128]{1,0:T(8,128)S(1)}, f32[272,128]{1,0:T(8,128)S(1)}, u32[]{:S(2)}, u32[]{:S(2)}) collective-permute-start(f32[272,128]{1,0:T(8,128)S(1)} %get-tuple-element.16), channel_id=1, source_target_pairs={{0,1},{1,0},{2,3},{3,2},{4,5},{5,4},{6,7},{7,6},{8,9},{9,8},{10,11... | collective-permute-start | bytes 417800 | tf_op jit(solution)/shard_map/ppermute | solution.py:346
  60.3 10.5 %copy-start.28 = (f32[2048]{0:T(1024)S(1)}, f32[2048]{0:T(1024)}, u32[]{:S(2)}) copy-start(f32[2048]{0:T(1024)} %param.15) | copy-start | bytes 24580
  60.4 10.5 %copy-start.30 = (f32[16,128]{1,0:T(8,128)S(1)}, f32[16,128]{1,0:T(8,128)}, u32[]{:S(2)}) copy-start(f32[16,128]{1,0:T(8,128)} %copy-done.29) | copy-start | bytes 24580
  60.4 5.8 %collective-permute-start.13 = (f32[272,128]{1,0:T(8,128)S(1)}, f32[272,128]{1,0:T(8,128)S(1)}, u32[]{:S(2)}, u32[]{:S(2)}) collective-permute-start(f32[272,128]{1,0:T(8,128)S(1)} %add.7.after.refs_0_), channel_id=1, source_target_pairs={{0,6},{1,7},{2,0},{3,1},{4,2},{5,3},{6,4},{7,5},{8,14},{9,15},{10,... | collective-permute-start | bytes 417800 | tf_op jit(solution)/shard_map/ppermute | solution.py:352
  61.0 6.1 %collective-permute-start.12 = (f32[272,128]{1,0:T(8,128)S(1)}, f32[272,128]{1,0:T(8,128)S(1)}, u32[]{:S(2)}, u32[]{:S(2)}) collective-permute-start(f32[272,128]{1,0:T(8,128)S(1)} %add.7.after.refs_0_), channel_id=1, source_target_pairs={{0,4},{1,5},{2,6},{3,7},{4,0},{5,1},{6,2},{7,3},{8,12},{9,13},{10,... | collective-permute-start | bytes 417800 | tf_op jit(solution)/shard_map/ppermute | solution.py:352
  62.4 8.5 %collective-permute-start.11 = (f32[272,128]{1,0:T(8,128)S(1)}, f32[272,128]{1,0:T(8,128)S(1)}, u32[]{:S(2)}, u32[]{:S(2)}) collective-permute-start(f32[272,128]{1,0:T(8,128)S(1)} %add.7.after.refs_0_), channel_id=1, source_target_pairs={{0,2},{1,3},{2,4},{3,5},{4,6},{5,7},{6,0},{7,1},{8,10},{9,11},{10,... | collective-permute-start | bytes 417800 | tf_op jit(solution)/shard_map/ppermute | solution.py:352
  71.1 12.8 %collective-permute-start.14 = (f32[2,128,128]{2,1,0:T(8,128)S(1)}, f32[2,128,128]{2,1,0:T(8,128)S(1)}, u32[]{:S(2)}, u32[]{:S(2)}) collective-permute-start(f32[2,128,128]{2,1,0:T(8,128)S(1)} %get-tuple-element.19.mine), channel_id=1, source_target_pairs={{0,1},{1,0},{2,3},{3,2},{4,5},{5,4},{6,7},{7,6},{8,9},{9,8},{10,11... | collective-permute-start | bytes 393224 | tf_op jit(solution)/shard_map/ppermute | solution.py:346

commit v4 on v3

--- a/solution.py
+++ b/solution.py
@@ -49,12 +49,20 @@
         offset = tile * rows + np.arange(rows)[None, :] - np.arange(rows)[:, None]
         inside = np.abs(offset) <= reach
         along = np.where(inside, kernel[np.clip(offset + reach, 0, 2 * reach)], 0.0)
-        blocks.append(np.kron(vertical, along))
-    rows_high, rows_low = bf16_pair(np.concatenate(blocks, axis=1) * scale)
-    pair_high, pair_low = bf16_pair(np.kron(np.eye(2), lateral))
-    mix = np.concatenate([rows_high, rows_low], axis=0)
-    total = levels * rows
-    return mix, [mix[:, i : i + total] for i in range(0, 3 * total, total)], pair_high, pair_low
+        blocks.append(np.concatenate(bf16_pair(np.kron(vertical, along) * scale)))
+    return blocks, bf16_pair(np.kron(np.eye(CORES), lateral))
+
+
+class Constants:
+    def __init__(self, levels, rows, columns, members):
+        self.places, arrays, start = {}, [], 0
+        for power in (2, 1):
+            blocks, pair = local_matrices(levels, rows, columns, power, float(members) ** (-power / 2))
+            for name, array in list(zip("boa", blocks)) + list(zip("hl", pair)):
+                self.places[power, name] = slice(start, start + array.shape[0])
+                arrays.append(array)
+                start += array.shape[0]
+        self.array = np.concatenate(arrays)
 
 
 def split(x):
@@ -112,30 +120,30 @@
     return jnp.where(lax.broadcasted_iota(jnp.int32, (1, slots), 1) < count_ref[0], 1.0, 0.0)
 
 
-def mixed_pairs(p_refs, g_refs, rows_ref, mixed):
+def mixed_pairs(p_refs, g_refs, rows_matrix, mixed):
     total = g_refs[0].shape[0]
     for pair in range(mixed.shape[0]):
         sides = []
         for member in (2 * pair, 2 * pair + 1):
             sides.append(jnp.concatenate([p[member].astype(F32) * g[...] for p, g in zip(p_refs, g_refs)], axis=0))
         high, low = split(jnp.concatenate(sides, axis=1))
-        product = dot(rows_ref[...], high)
-        high, low = split(product[:total] + product[total:] + dot(rows_ref[:total], low))
+        product = dot(rows_matrix, high)
+        high, low = split(product[:total] + product[total:] + dot(rows_matrix[:total], low))
         mixed[pair, :total] = high
         mixed[pair, total:] = low
 
 
-def across_columns(pair, mixed, pair_high_ref, pair_low_ref):
+def across_columns(pair, mixed, pair_high, pair_low):
     total = mixed.shape[1] // 2
-    product = dot(mixed[pair], pair_high_ref[...])
-    return product[:total] + product[total:] + dot(mixed[pair, :total], pair_low_ref[...])
-
-
-def summed_members(field, weigh, p_refs, g_refs, rows_ref, pair_high_ref, pair_low_ref, mixed):
-    columns = g_refs[0].shape[1]
-    mixed_pairs(p_refs, g_refs, rows_ref, mixed)
+    product = dot(mixed[pair], pair_high)
+    return product[:total] + product[total:] + dot(mixed[pair, :total], pair_low)
+
+
+def summed_members(field, weigh, p_side, g_side, constants, places, which, mixed):
+    columns = g_side.shape[1]
+    mixed_pairs([p_side], [g_side], constants[places[2, which]], mixed)
     for pair in range(mixed.shape[0]):
-        spread = across_columns(pair, mixed, pair_high_ref, pair_low_ref)
+        spread = across_columns(pair, mixed, constants[places[2, "h"]], constants[places[2, "l"]])
         field = field + weigh[2 * pair].astype(F32) * spread[:, :columns]
         field = field + weigh[2 * pair + 1].astype(F32) * spread[:, columns:]
     return field
@@ -149,68 +157,69 @@
     return jnp.concatenate([block[i : i + 1] for i in range(block.shape[0])], axis=1)
 
 
-def start_kernel(rows, columns, count, weights, cell, precision, innovations, field):
-    live = live_slots(count, weights.shape[1])
-    values = live * precision[...] * innovations[...]
-    field[...] = adjoint(values, weights, cell, rows, columns)
-
-
-def own_kernel(p, g, mix, pair_high, pair_low, field, mixed):
-    field[...] = summed_members(jnp.zeros(g.shape, F32), p, [p], [g], mix, pair_high, pair_low, mixed)
-
-
-def side_kernel(p, p_side, g_side, part, mix, pair_high, pair_low, field, mixed):
-    field[...] = summed_members(part[...], p, [p_side], [g_side], mix, pair_high, pair_low, mixed)
-
-
-def first_kernel(rows, columns, count, p, p_side, g_side, part, mix, pair_high, pair_low, weights, cell, observed, field, mixed):
-    whole = summed_members(part[...], p, [p_side], [g_side], mix, pair_high, pair_low, mixed)
-    observed[...] = as_rows(observe(whole, weights, cell, live_slots(count, weights.shape[1]), rows, columns))
-    field[...] = whole
-
-
-def second_kernel(rows, columns, count, place, p, p_side, g_side, part, mix, pair_high, pair_low, weights, cell, field0,
-                  kept, given, field1, mixed):
-    whole = summed_members(part[...], p, [p_side], [g_side], mix, pair_high, pair_low, mixed)
-    field1[...] = whole
-    observed = as_rows(observe(whole, weights, cell, live_slots(count, weights.shape[1]), rows, columns))
+def start_kernel(rows, columns, count, place, weights, cell, precision, innovations, field, precision_rows, c_rows):
+    c = live_slots(count, weights.shape[1]) * precision[...] * innovations[...]
+    field[...] = adjoint(c, weights, cell, rows, columns)
+    precision_rows[...] = as_rows(precision[...])
+    c_rows[...] = as_rows(c)
+
+
+def own_kernel(places, p, g, constants, field, mixed):
+    field[...] = summed_members(jnp.zeros(g.shape, F32), p, p, g, constants, places, "o", mixed)
+
+
+def side_kernel(places, p, p_side, g_side, part, constants, field, mixed):
+    field[...] = summed_members(part[...], p, p_side, g_side, constants, places, "a", mixed)
+
+
+def message_rows(place, observed, field, kept, given):
     lines = observed.shape[0]
-    half = whole.shape[0] // CORES
+    half = field.shape[0] // CORES
     core = lax.rem(place[0], CORES)
     for message, at in ((kept, core), (given, 1 - core)):
-        rows_of_half = pl.ds(pl.multiple_of(at * half, half), half)
         message[:lines] = observed
-        message[lines : lines + half] = field0[rows_of_half]
-        message[lines + half :] = field1[rows_of_half]
+        message[lines:] = field[pl.ds(pl.multiple_of(at * half, half), half)]
+
+
+def observe_kernel(rows, columns, places, count, place, p, p_side, g_side, part, constants, weights, cell, kept, given, field, mixed):
+    field[...] = summed_members(part[...], p, p_side, g_side, constants, places, "b", mixed)
+    observed = as_rows(observe(field[...], weights, cell, live_slots(count, weights.shape[1]), rows, columns))
+    message_rows(place, observed, field, kept, given)
+
+
+def sum_kernel(first, second, total):
+    total[...] = first[...] + second[...]
 
 
 def middle_kernel(rows, columns, count, *refs):
-    *messages, weights, cell, precision, after, field, observed = refs
-    summed = sum(message[...] for message in messages)
+    *messages, weights, cell, precision, after, field, observed, half = refs
+    lines = observed.shape[0]
+    half[...] = sum(message[lines:] for message in messages)
+    summed = sum(message[:lines] for message in messages)
     observed[...] = summed
     field[...] = adjoint(precision[...] * as_line(summed), weights, cell, rows, columns)
 
 
-def alpha_kernel(p0, p1, p2, g0, g1, g2, mix, pair_high, pair_low, after, alpha, mixed):
+def alpha_kernel(places, p0, p1, p2, g0, g1, g2, constants, after, alpha, token, mixed):
     columns = g0.shape[1]
-    mixed_pairs((p0, p1, p2), (g0, g1, g2), mix, mixed)
+    matrix = jnp.concatenate([constants[places[1, name]] for name in "boa"], axis=1)
+    mixed_pairs((p0, p1, p2), (g0, g1, g2), matrix, mixed)
     for pair in range(mixed.shape[0]):
-        spread = across_columns(pair, mixed, pair_high, pair_low)
+        spread = across_columns(pair, mixed, constants[places[1, "h"]], constants[places[1, "l"]])
         alpha[2 * pair] = spread[:, :columns]
         alpha[2 * pair + 1] = spread[:, columns:]
-
-
-def scalars_kernel(count, *refs):
-    *messages, once, precision, innovations, after, scalars, halves = refs
+    token[...] = jnp.zeros(token.shape, F32)
+
+
+def scalars_kernel(*refs):
+    *messages, once, half0, precision, c_rows, after, scalars, halves = refs
     lines = once.shape[0]
     z2 = sum(message[:lines] for message in messages)
-    half = halves.shape[1]
-    for i in range(2):
-        halves[i] = sum(message[lines + i * half : lines + (i + 1) * half] for message in messages)
+    halves[0] = half0[...]
+    halves[1] = sum(message[lines:] for message in messages)
     z1 = once[...]
     rho = precision[...]
-    slot = lax.broadcasted_iota(jnp.int32, rho.shape, 0) * rho.shape[1] + lax.broadcasted_iota(jnp.int32, rho.shape, 1)
-    c = jnp.where(slot < count[0], rho * innovations[...], 0.0)
+    c = c_rows[...]
 
     def total(x):
         return jnp.sum(jnp.sum(x, axis=0, keepdims=True), axis=1, keepdims=True)
@@ -313,20 +322,19 @@
     slots = obs_cell.shape[0]
     cells = levels * rows
     ens, tiles = lax.axis_size("ens"), lax.axis_size("tile")
-    everyone = ens * members
+    constants = Constants(levels, rows, columns, ens * members)
+    places = constants.places
+    constants = jnp.asarray(constants.array)
     lines = slots // 128
-    _, mix2, high2, low2 = local_matrices(levels, rows, columns, 2, 1.0 / everyone)
-    mix1, _, high1, low1 = local_matrices(levels, rows, columns, 1, 1.0 / math.sqrt(everyone))
-
     p = perturbations.reshape(members, cells, columns)
     cell = obs_cell.reshape(1, slots)
     precision = obs_precision.reshape(1, slots)
     innovations_line = innovations.reshape(1, slots)
     shape = (rows, columns)
 
-    def bound(kernel):
+    def bound(kernel, *values):
         def run(*refs):
-            kernel(*shape, *refs)
+            kernel(*values, *refs)
 
         return run
 
@@ -339,8 +347,8 @@
     mixed = pltpu.VMEM((members // 2, 2 * cells, CORES * columns), BF16)
 
     def own_and_after(g, g_after):
-        part = call(own_kernel, field_shape, vmem(p, g, mix2[1], high2, low2), [mixed])
-        return call(side_kernel, field_shape, vmem(p, p_after, g_after, part, mix2[2], high2, low2), [mixed])
+        part = call(bound(own_kernel, places), field_shape, vmem(p, g, constants), [mixed])
+        return call(bound(side_kernel, places), field_shape, vmem(p, p_after, g_after, part, constants), [mixed])
 
     def other_core(x):
         return lax.ppermute(x, "ens", [(i, i ^ 1) for i in range(ens)])
@@ -352,47 +360,49 @@
             arrived.append(lax.ppermute(x, "ens", route))
         return arrived
 
+    def summed(first, second):
+        return call(sum_kernel, first.shape, vmem(first, second))
+
     def alpha_of(g, g_before, g_after, after):
         return call(
-            alpha_kernel, (members, cells, columns),
-            vmem(p_before, p, p_after, g_before, g, g_after, mix1, high1, low1) + [anywhere(after)], [mixed],
+            bound(alpha_kernel, places), [(members, cells, columns), (8, 128)],
+            vmem(p_before, p, p_after, g_before, g, g_after, constants) + [anywhere(after)], [mixed],
         )
 
     p_before, p_after = neighbours(p)
-    g0 = call(
-        bound(start_kernel), field_shape,
-        [in_smem(obs_count)] + vmem(obs_weights, cell, precision, innovations_line),
+    weights = obs_weights
+    g0, precision_rows, c_rows = call(
+        bound(start_kernel, *shape), [field_shape, (lines, 128), (lines, 128)],
+        [in_smem(obs_count), in_smem(place)] + vmem(weights, cell, precision, innovations_line),
     )
     g0_before, g0_after = neighbours(g0)
     part = own_and_after(g0, g0_after)
-    seen, field0 = call(
-        bound(first_kernel), [(lines, columns), field_shape],
-        [in_smem(obs_count)] + vmem(p, p_before, g0_before, part, mix2[0], high2, low2, obs_weights, cell), [mixed],
-    )
-    sent = seen + other_core(seen)
+    message = (lines + half, columns)
+    kept, given = call(
+        bound(observe_kernel, *shape, places), [message, message],
+        [in_smem(obs_count), in_smem(place)] + vmem(p, p_before, g0_before, part, constants, weights, cell),
+        [pltpu.VMEM(field_shape, F32), mixed],
+    )
+    sent = summed(kept, other_core(given))
     messages = from_chips(sent)
-    alpha0 = alpha_of(g0, g0_before, g0_after, sent)
-    g1, once = call(
-        bound(middle_kernel), [field_shape, (lines, 128)],
-        [in_smem(obs_count)] + vmem(*messages, obs_weights, cell, precision) + [anywhere(alpha0)],
+    alpha0, done0 = alpha_of(g0, g0_before, g0_after, sent)
+    g1, once, half0 = call(
+        bound(middle_kernel, *shape), [field_shape, (lines, 128), (half, columns)],
+        [in_smem(obs_count)] + vmem(*messages, weights, cell, precision) + [anywhere(done0)],
     )
     g1_before, g1_after = neighbours(g1)
     part = own_and_after(g1, g1_after)
-    message = (lines + 2 * half, columns)
     kept, given = call(
-        bound(second_kernel), [message, message],
-        [in_smem(obs_count), in_smem(place)]
-        + vmem(p, p_before, g1_before, part, mix2[0], high2, low2, obs_weights, cell, field0),
+        bound(observe_kernel, *shape, places), [message, message],
+        [in_smem(obs_count), in_smem(place)] + vmem(p, p_before, g1_before, part, constants, weights, cell),
         [pltpu.VMEM(field_shape, F32), mixed],
     )
-    sent = kept + other_core(given)
+    sent = summed(kept, other_core(given))
     messages = from_chips(sent)
-    alpha1 = alpha_of(g1, g1_before, g1_after, sent)
+    alpha1, done1 = alpha_of(g1, g1_before, g1_after, sent)
     scalars, mine = call(
         scalars_kernel, [(tiles, 128), (2, half, columns)],
-        [in_smem(obs_count)]
-        + vmem(*messages, once, obs_precision.reshape(lines, 128), innovations.reshape(lines, 128))
-        + [anywhere(alpha1)],
+        vmem(*messages, once, half0, precision_rows, c_rows) + [anywhere(done1)],
     )
     other = other_core(mine)
     scalars = lax.all_to_all(scalars.reshape(tiles, 1, 128), "tile", 0, 0).reshape(tiles, 128)

time: 86.1 us -> 81.6 us (0.948)
  waiting for transfers between devices: 15.1 us -> 20.3 us
  Pallas kernels: 21 us -> 16.6 us
  local copies, waits for them, and re-layouts: 8.5 us -> 5.7 us
  starting transfers between devices: 27.4 us -> 25.8 us
    pallas_call x12 -> x14, Pallas kernels: 21 us -> 16.6 us  [call(): pl.pallas_call(kernel, out_shape=shapes[0] if single else shapes, in_spec...]
    ppermute x6, waiting for transfers between devices: 7.91 us -> 11.6 us  [neighbours(): return (lax.ppermute(x, 'tile', up), lax.ppermute(x, 'tile', down))]
    unnamed x62 -> x22, local copies, waits for them, and re-layouts: 8.5 us -> 5.7 us
    ppermute x6, waiting for transfers between devices: 5.32 us -> 6.82 us  [from_chips(): arrived.append(lax.ppermute(x, 'ens', route))]
    ppermute x3, starting transfers between devices: 6.27 us -> 5.21 us  [other_core(): return lax.ppermute(x, 'ens', [(i, i ^ 1) for i in range(ens)])]
  transfers between devices with their start and end apart: 15 -> 15, of which waited for: 9 -> 10; matrix products, arithmetic and copies ran while one was open for 0% -> 0% of each run, Pallas kernels for 16% -> 13%
where the time goes in v4:
time: 81.6 us; the launch traced here: 81.3 us
  starting transfers between devices  25.8 us (32%)
  waiting for transfers between devices  20.3 us (25%)
  Pallas kernels  16.6 us (20%)
  blocking collectives  11.5 us (14%)
  local copies, waits for them, and re-layouts  5.7 us (7%)
  between operations  1.44 us (2%)
    pallas_call x14, Pallas kernels, call(): pl.pallas_call(kernel, out_shape=shapes[0] if single else shapes, in_spec...  16.6 us
    ppermute x6, starting transfers between devices, neighbours(): return (lax.ppermute(x, 'tile', up), lax.ppermute(x, 'tile', down))  15.1 us
    ppermute x6, waiting for transfers between devices, neighbours(): return (lax.ppermute(x, 'tile', up), lax.ppermute(x, 'tile', down))  11.6 us
    all_to_all x1, blocking collectives, local(): lax.all_to_all(scalars.reshape(tiles, 1, 128), 'tile', 0, 0)  11.5 us
    ppermute x6, waiting for transfers between devices, from_chips(): arrived.append(lax.ppermute(x, 'ens', route))  6.82 us
    unnamed x22, local copies, waits for them, and re-layouts  5.7 us
    ppermute x6, starting transfers between devices, from_chips(): arrived.append(lax.ppermute(x, 'ens', route))  5.47 us
    ppermute x3, starting transfers between devices, other_core(): return lax.ppermute(x, 'ens', [(i, i ^ 1) for i in range(ens)])  5.21 us
  transfers between devices with their start and end apart: 15, of which 10 were waited for; matrix products, arithmetic and copies ran while one was open for 0% of the time, Pallas kernels for 13%

profile of v4, /device:TPU:1, one launch (start us, length us, event | category | flops | bytes accessed | tf_op | source)
XLA Modules:
  0.0 81.3 jit_solution(10327402472327779465)
XLA Ops:
  0.6 8.7 %collective-permute-start.2 = (bf16[10,256,128]{2,1,0:T(8,128)(2,1)}, bf16[10,256,128]{2,1,0:T(8,128)(2,1)S(1)}, u32[]{:S(2)}, u32[]{:S(2)}) collective-permute-start(bf16[10,256,128]{2,1,0:T(8,128)(2,1)} %bitcast.11), channel_id=1, source_target_pairs={{8,0},{16,8},{24,16},{32,24},{40,32},{48,40},{56,48},{64,56},{72,6... | collective-permute-start | bytes 1966088 | tf_op jit(solution)/shard_map/ppermute | solution.py:317
  9.3 0.0 collective-permute-start
  10.0 0.0 copy-start.4
  10.0 0.9 %copy-done.4 = f32[16,2048]{1,0:T(8,128)S(1)} copy-done((f32[16,2048]{1,0:T(8,128)S(1)}, f32[16,2048]{1,0:T(8,128)}, u32[]{:S(2)}) %copy-start.4) | copy-done | bytes 131096
  10.9 0.7 copy-done.6
  11.6 0.7 copy-done.8
  12.3 0.7 copy-done.10
  13.0 0.7 shard_map.86
  13.7 4.9 %collective-permute-start.3 = (f32[256,128]{1,0:T(8,128)S(1)}, f32[256,128]{1,0:T(8,128)S(1)}, u32[]{:S(2)}, u32[]{:S(2)}) collective-permute-start(f32[256,128]{1,0:T(8,128)S(1)} %get-tuple-element.20.refs_1_.refs_4_), channel_id=1, source_target_pairs={{8,0},{16,8},{24,16},{32,24},{40,32},{48,40},{56,48},{64,56},{72,6... | collective-permute-start | bytes 393224 | tf_op jit(solution)/shard_map/ppermute | solution.py:317
  18.6 1.6 %copy-done = bf16[4096,256]{1,0:T(8,128)(2,1)S(1)} copy-done((bf16[4096,256]{1,0:T(8,128)(2,1)S(1)}, bf16[4096,256]{1,0:T(8,128)(2,1)}, u32[]{:S(2)}) %copy-start) | copy-done | bytes 2097176
  20.2 1.1 %copy-done.2 = bf16[10,16,16,128]{3,2,1,0:T(8,128)(2,1)S(1)} copy-done((bf16[10,16,16,128]{3,2,1,0:T(8,128)(2,1)S(1)}, bf16[10,16,16,128]{3,2,1,0:T(8,128)(2,1)}, u32[]{:S(2)}) %copy-start.2) | copy-done | bytes 655384
  21.2 1.2 %shard_map.87.refs_3_ = f32[256,128]{1,0:T(8,128)S(1)} custom-call(bf16[10,256,128]{2,1,0:T(8,128)(2,1)S(1)} %bitcast.13, f32[256,128]{1,0:T(8,128)S(1)} %get-tuple-element.20.refs_1_.refs_4_, bf16[4096,256]{1,0:T(8,128)(2,1)S(1)} %copy-done), custom_call_target="tpu_custom_call" | custom-call | tf_op jit(solution)/shard_map/pallas_call | solution.py:303
  22.5 0.0 copy-start.3
  22.5 0.0 copy-start.5
  22.5 0.0 copy-start.7
  22.5 3.2 %collective-permute-done.3.refs_2_.refs_5_ = f32[256,128]{1,0:T(8,128)S(1)} collective-permute-done((f32[256,128]{1,0:T(8,128)S(1)}, f32[256,128]{1,0:T(8,128)S(1)}, u32[]{:S(2)}, u32[]{:S(2)}) %collective-permute-start.3) | collective-permute-done | bytes 131104 | tf_op jit(solution)/shard_map/ppermute | solution.py:317
  25.7 1.2 %shard_map.88.refs_5_ = f32[256,128]{1,0:T(8,128)S(1)} custom-call(bf16[10,256,128]{2,1,0:T(8,128)(2,1)S(1)} %bitcast.14, bf16[10,256,128]{2,1,0:T(8,128)(2,1)S(1)} %collective-permute-done.2.refs_1_.refs_2_, f32[256,128]{1,0:T(8,128)S(1)} %collective-permute-done.3.refs_2_.refs_5_, f32[256,128]{1,0:T(8,128)S(1)} %shard_map.87.refs_3_, ...), custom_call_target="tpu_custom_call" | custom-call | tf_op jit(solution)/shard_map/pallas_call | solution.py:303
  27.0 4.0 %collective-permute-done.1.refs_4_.refs_3_ = f32[256,128]{1,0:T(8,128)S(1)} collective-permute-done((f32[256,128]{1,0:T(8,128)S(1)}, f32[256,128]{1,0:T(8,128)S(1)}, u32[]{:S(2)}, u32[]{:S(2)}) %collective-permute-start.1) | collective-permute-done | bytes 131104 | tf_op jit(solution)/shard_map/ppermute | solution.py:317
  31.0 1.7 %shard_map.89 = (f32[144,128]{1,0:T(8,128)S(1)}, f32[144,128]{1,0:T(8,128)S(1)}) custom-call(s32[1]{0:T(128)S(6)} %copy.10.refs_0_, s32[1]{0:T(128)} %bitcast.refs_1_.place, bf16[10,256,128]{2,1,0:T(8,128)(2,1)S(1)} %bitcast.15, bf16[10,256,128]{2,1,0:T(8,128)(2,1)S(1)} %collective-permute-done.refs_3_.refs_0_, ...), custom_call_target="tpu_custom_call" | custom-call | tf_op jit(solution)/shard_map/pallas_call | solution.py:303
  32.7 1.9 %collective-permute-start.4 = (f32[144,128]{1,0:T(8,128)S(1)}, f32[144,128]{1,0:T(8,128)S(1)}, u32[]{:S(2)}, u32[]{:S(2)}) collective-permute-start(f32[144,128]{1,0:T(8,128)S(1)} %get-tuple-element.22), channel_id=1, source_target_pairs={{0,1},{1,0},{2,3},{3,2},{4,5},{5,4},{6,7},{7,6},{8,9},{9,8},{10,11... | collective-permute-start | bytes 221192 | tf_op jit(solution)/shard_map/ppermute | solution.py:354
  34.6 0.9 %collective-permute-done.4.second = f32[144,128]{1,0:T(8,128)S(1)} collective-permute-done((f32[144,128]{1,0:T(8,128)S(1)}, f32[144,128]{1,0:T(8,128)S(1)}, u32[]{:S(2)}, u32[]{:S(2)}) %collective-permute-start.4) | collective-permute-done | bytes 73760 | tf_op jit(solution)/shard_map/ppermute | solution.py:354
  35.5 0.0 copy-start.9
  35.6 2.8 %collective-permute-start.7 = (f32[144,128]{1,0:T(8,128)S(1)}, f32[144,128]{1,0:T(8,128)S(1)}, u32[]{:S(2)}, u32[]{:S(2)}) collective-permute-start(f32[144,128]{1,0:T(8,128)S(1)} %shard_map.90.refs_7_.refs_1_), channel_id=1, source_target_pairs={{0,6},{1,7},{2,0},{3,1},{4,2},{5,3},{6,4},{7,5},{8,14},{9,15},{10,... | collective-permute-start | bytes 221192 | tf_op jit(solution)/shard_map/ppermute | solution.py:360
  38.4 0.3 collective-permute-start.6
  38.7 0.7 collective-permute-start.5
  39.4 2.4 %shard_map.91 = (f32[10,256,128]{2,1,0:T(8,128)S(1)}, f32[8,128]{1,0:T(8,128)S(1)}) custom-call(bf16[10,256,128]{2,1,0:T(8,128)(2,1)S(1)} %collective-permute-done.refs_3_.refs_0_, bf16[10,256,128]{2,1,0:T(8,128)(2,1)S(1)} %bitcast.16, bf16[10,256,128]{2,1,0:T(8,128)(2,1)S(1)} %collective-permute-done.2.refs_1_.refs_2_, ...), custom_call_target="tpu_custom_call" | custom-call | tf_op jit(solution)/shard_map/pallas_call | solution.py:303
  41.8 1.4 %collective-permute-done.6.refs_3_ = f32[144,128]{1,0:T(8,128)S(1)} collective-permute-done((f32[144,128]{1,0:T(8,128)S(1)}, f32[144,128]{1,0:T(8,128)S(1)}, u32[]{:S(2)}, u32[]{:S(2)}) %collective-permute-start.6) | collective-permute-done | bytes 73760 | tf_op jit(solution)/shard_map/ppermute | solution.py:360
  43.2 2.1 %collective-permute-done.5.refs_2_ = f32[144,128]{1,0:T(8,128)S(1)} collective-permute-done((f32[144,128]{1,0:T(8,128)S(1)}, f32[144,128]{1,0:T(8,128)S(1)}, u32[]{:S(2)}, u32[]{:S(2)}) %collective-permute-start.5) | collective-permute-done | bytes 73760 | tf_op jit(solution)/shard_map/ppermute | solution.py:360
  45.2 0.7 shard_map.92
  46.0 1.4 %collective-permute-start.9 = (f32[256,128]{1,0:T(8,128)S(1)}, f32[256,128]{1,0:T(8,128)S(1)}, u32[]{:S(2)}, u32[]{:S(2)}) collective-permute-start(f32[256,128]{1,0:T(8,128)S(1)} %get-tuple-element.24.refs_1_.refs_4_), channel_id=1, source_target_pairs={{8,0},{16,8},{24,16},{32,24},{40,32},{48,40},{56,48},{64,56},{72,6... | collective-permute-start | bytes 393224 | tf_op jit(solution)/shard_map/ppermute | solution.py:317
  47.3 0.2 collective-permute-start.8
  47.5 1.3 %shard_map.93.refs_3_ = f32[256,128]{1,0:T(8,128)S(1)} custom-call(bf16[10,256,128]{2,1,0:T(8,128)(2,1)S(1)} %bitcast.17, f32[256,128]{1,0:T(8,128)S(1)} %get-tuple-element.24.refs_1_.refs_4_, bf16[4096,256]{1,0:T(8,128)(2,1)S(1)} %copy-done.1), custom_call_target="tpu_custom_call" | custom-call | tf_op jit(solution)/shard_map/pallas_call | solution.py:303
  48.8 1.1 %collective-permute-done.9.refs_2_.refs_5_ = f32[256,128]{1,0:T(8,128)S(1)} collective-permute-done((f32[256,128]{1,0:T(8,128)S(1)}, f32[256,128]{1,0:T(8,128)S(1)}, u32[]{:S(2)}, u32[]{:S(2)}) %collective-permute-start.9) | collective-permute-done | bytes 131104 | tf_op jit(solution)/shard_map/ppermute | solution.py:317
  49.9 1.2 %shard_map.94.refs_5_ = f32[256,128]{1,0:T(8,128)S(1)} custom-call(bf16[10,256,128]{2,1,0:T(8,128)(2,1)S(1)} %bitcast.18, bf16[10,256,128]{2,1,0:T(8,128)(2,1)S(1)} %collective-permute-done.2.refs_1_.refs_2_, f32[256,128]{1,0:T(8,128)S(1)} %collective-permute-done.9.refs_2_.refs_5_, f32[256,128]{1,0:T(8,128)S(1)} %shard_map.93.refs_3_, ...), custom_call_target="tpu_custom_call" | custom-call | tf_op jit(solution)/shard_map/pallas_call | solution.py:303
  51.1 3.3 %collective-permute-done.8.refs_4_.refs_3_ = f32[256,128]{1,0:T(8,128)S(1)} collective-permute-done((f32[256,128]{1,0:T(8,128)S(1)}, f32[256,128]{1,0:T(8,128)S(1)}, u32[]{:S(2)}, u32[]{:S(2)}) %collective-permute-start.8) | collective-permute-done | bytes 131104 | tf_op jit(solution)/shard_map/ppermute | solution.py:317
  54.5 1.7 %shard_map.95 = (f32[144,128]{1,0:T(8,128)S(1)}, f32[144,128]{1,0:T(8,128)S(1)}) custom-call(s32[1]{0:T(128)S(6)} %copy.10.refs_0_, s32[1]{0:T(128)} %bitcast.refs_1_.place, bf16[10,256,128]{2,1,0:T(8,128)(2,1)S(1)} %bitcast.19, bf16[10,256,128]{2,1,0:T(8,128)(2,1)S(1)} %collective-permute-done.refs_3_.refs_0_, ...), custom_call_target="tpu_custom_call" | custom-call | tf_op jit(solution)/shard_map/pallas_call | solution.py:303
  56.2 2.4 %collective-permute-start.10 = (f32[144,128]{1,0:T(8,128)S(1)}, f32[144,128]{1,0:T(8,128)S(1)}, u32[]{:S(2)}, u32[]{:S(2)}) collective-permute-start(f32[144,128]{1,0:T(8,128)S(1)} %get-tuple-element.26), channel_id=1, source_target_pairs={{0,1},{1,0},{2,3},{3,2},{4,5},{5,4},{6,7},{7,6},{8,9},{9,8},{10,11... | collective-permute-start | bytes 221192 | tf_op jit(solution)/shard_map/ppermute | solution.py:354
  58.6 0.9 %collective-permute-done.10.second = f32[144,128]{1,0:T(8,128)S(1)} collective-permute-done((f32[144,128]{1,0:T(8,128)S(1)}, f32[144,128]{1,0:T(8,128)S(1)}, u32[]{:S(2)}, u32[]{:S(2)}) %collective-permute-start.10) | collective-permute-done | bytes 73760 | tf_op jit(solution)/shard_map/ppermute | solution.py:354
  59.6 0.4 collective-permute-start.13
  59.9 0.5 collective-permute-start.12
  60.4 0.8 collective-permute-start.11
  61.2 2.4 %shard_map.97 = (f32[10,256,128]{2,1,0:T(8,128)S(1)}, f32[8,128]{1,0:T(8,128)S(1)}) custom-call(bf16[10,256,128]{2,1,0:T(8,128)(2,1)S(1)} %collective-permute-done.refs_3_.refs_0_, bf16[10,256,128]{2,1,0:T(8,128)(2,1)S(1)} %bitcast.20, bf16[10,256,128]{2,1,0:T(8,128)(2,1)S(1)} %collective-permute-done.2.refs_1_.refs_2_, ...), custom_call_target="tpu_custom_call" | custom-call | tf_op jit(solution)/shard_map/pallas_call | solution.py:303
  63.6 1.1 %collective-permute-done.12.refs_2_ = f32[144,128]{1,0:T(8,128)S(1)} collective-permute-done((f32[144,128]{1,0:T(8,128)S(1)}, f32[144,128]{1,0:T(8,128)S(1)}, u32[]{:S(2)}, u32[]{:S(2)}) %collective-permute-start.12) | collective-permute-done | bytes 73760 | tf_op jit(solution)/shard_map/ppermute | solution.py:360
  64.7 2.3 %collective-permute-done.11.refs_1_ = f32[144,128]{1,0:T(8,128)S(1)} collective-permute-done((f32[144,128]{1,0:T(8,128)S(1)}, f32[144,128]{1,0:T(8,128)S(1)}, u32[]{:S(2)}, u32[]{:S(2)}) %collective-permute-start.11) | collective-permute-done | bytes 73760 | tf_op jit(solution)/shard_map/ppermute | solution.py:360
  66.9 0.2 shard_map.98
  67.1 0.8 %collective-permute-start.14 = (f32[2,128,128]{2,1,0:T(8,128)S(1)}, f32[2,128,128]{2,1,0:T(8,128)S(1)}, u32[]{:S(2)}, u32[]{:S(2)}) collective-permute-start(f32[2,128,128]{2,1,0:T(8,128)S(1)} %get-tuple-element.35.mine), channel_id=1, source_target_pairs={{0,1},{1,0},{2,3},{3,2},{4,5},{5,4},{6,7},{7,6},{8,9},{9,8},{10,11... | collective-permute-start | bytes 393224 | tf_op jit(solution)/shard_map/ppermute | solution.py:354
  68.0 11.5 %all_to_all.5 = f32[32,1,128]{2,1,0:T(1,128)S(1)} all-to-all(f32[32,1,128]{2,1,0:T(1,128)S(1)} %bitcast.28), channel_id=1, replica_groups=mesh['tile'=32,'ens'=8] {'tile'}, dimensions={0} | all-to-all | bytes 32768 | tf_op jit(solution)/shard_map/all_to_all | solution.py:408
  79.5 1.8 %shard_map.99 = (f32[10,256,128]{2,1,0:T(8,128)}, f32[256,128]{1,0:T(8,128)}) custom-call(s32[1]{0:T(128)} %bitcast.refs_1_.place, f32[32,128]{1,0:T(8,128)S(1)} %bitcast.25, f32[10,256,128]{2,1,0:T(8,128)S(1)} %get-tuple-element.33.alpha0, f32[10,256,128]{2,1,0:T(8,128)S(1)} %get-tuple-element.34.alpha1, f32[2,128,128]{2,1,0:T(8,128)S(1)} %get-tuple-element.35.mine, ...), custom_call_target="tpu_custom_call" | custom-call | tf_op jit(solution)/shard_map/pallas_call | solution.py:303
  (19 shorter events, 0.1 us)
Async XLA Ops:
  0.6 25.1 %collective-permute-start.2 = (bf16[10,256,128]{2,1,0:T(8,128)(2,1)}, bf16[10,256,128]{2,1,0:T(8,128)(2,1)S(1)}, u32[]{:S(2)}, u32[]{:S(2)}) collective-permute-start(bf16[10,256,128]{2,1,0:T(8,128)(2,1)} %bitcast.11), channel_id=1, source_target_pairs={{8,0},{16,8},{24,16},{32,24},{40,32},{48,40},{56,48},{64,56},{72,6... | collective-permute-start | bytes 1966088 | tf_op jit(solution)/shard_map/ppermute | solution.py:317
  9.3 21.6 %collective-permute-start = (bf16[10,256,128]{2,1,0:T(8,128)(2,1)}, bf16[10,256,128]{2,1,0:T(8,128)(2,1)S(1)}, u32[]{:S(2)}, u32[]{:S(2)}) collective-permute-start(bf16[10,256,128]{2,1,0:T(8,128)(2,1)} %bitcast.12), channel_id=1, source_target_pairs={{0,8},{8,16},{16,24},{24,32},{32,40},{40,48},{48,56},{56,64},{64,7... | collective-permute-start | bytes 1966088 | tf_op jit(solution)/shard_map/ppermute | solution.py:317
  10.0 0.9 %copy-start.4 = (f32[16,2048]{1,0:T(8,128)S(1)}, f32[16,2048]{1,0:T(8,128)}, u32[]{:S(2)}) copy-start(f32[16,2048]{1,0:T(8,128)} %refs_7_.3) | copy-start | bytes 393220
  10.9 0.7 copy-start.6
  11.6 0.7 copy-start.8
  12.3 0.7 copy-start.10
  13.7 12.0 %collective-permute-start.3 = (f32[256,128]{1,0:T(8,128)S(1)}, f32[256,128]{1,0:T(8,128)S(1)}, u32[]{:S(2)}, u32[]{:S(2)}) collective-permute-start(f32[256,128]{1,0:T(8,128)S(1)} %get-tuple-element.20.refs_1_.refs_4_), channel_id=1, source_target_pairs={{8,0},{16,8},{24,16},{32,24},{40,32},{48,40},{56,48},{64,56},{72,6... | collective-permute-start | bytes 393224 | tf_op jit(solution)/shard_map/ppermute | solution.py:317
  18.6 12.4 %collective-permute-start.1 = (f32[256,128]{1,0:T(8,128)S(1)}, f32[256,128]{1,0:T(8,128)S(1)}, u32[]{:S(2)}, u32[]{:S(2)}) collective-permute-start(f32[256,128]{1,0:T(8,128)S(1)} %get-tuple-element.20.refs_1_.refs_4_), channel_id=1, source_target_pairs={{0,8},{8,16},{16,24},{24,32},{32,40},{40,48},{48,56},{56,64},{64,7... | collective-permute-start | bytes 393224 | tf_op jit(solution)/shard_map/ppermute | solution.py:317
  18.6 1.6 %copy-start = (bf16[4096,256]{1,0:T(8,128)(2,1)S(1)}, bf16[4096,256]{1,0:T(8,128)(2,1)}, u32[]{:S(2)}) copy-start(bf16[4096,256]{1,0:T(8,128)(2,1)} %constant.6.clone.refs_2_.refs_4_.refs_6_) | copy-start | bytes 6291460
  20.1 1.1 %copy-start.2 = (bf16[10,16,16,128]{3,2,1,0:T(8,128)(2,1)S(1)}, bf16[10,16,16,128]{3,2,1,0:T(8,128)(2,1)}, u32[]{:S(2)}) copy-start(bf16[10,16,16,128]{3,2,1,0:T(8,128)(2,1)} %param.7) | copy-start | bytes 1966084
  21.2 4.5 %copy-start.1 = (bf16[4096,256]{1,0:T(8,128)(2,1)S(1)}, bf16[4096,256]{1,0:T(8,128)(2,1)}, u32[]{:S(2)}) copy-start(bf16[4096,256]{1,0:T(8,128)(2,1)} %constant.6.clone.refs_2_.refs_4_.refs_6_) | copy-start | bytes 6291460
  22.5 8.5 %copy-start.3 = (bf16[10,16,16,128]{3,2,1,0:T(8,128)(2,1)S(1)}, bf16[10,16,16,128]{3,2,1,0:T(8,128)(2,1)}, u32[]{:S(2)}) copy-start(bf16[10,16,16,128]{3,2,1,0:T(8,128)(2,1)} %param.7) | copy-start | bytes 1966084
  22.5 8.5 %copy-start.5 = (f32[16,2048]{1,0:T(8,128)S(1)}, f32[16,2048]{1,0:T(8,128)}, u32[]{:S(2)}) copy-start(f32[16,2048]{1,0:T(8,128)} %refs_7_.3) | copy-start | bytes 393220
  22.5 8.4 %copy-start.7 = (s32[2048]{0:T(1024)S(1)}, s32[2048]{0:T(1024)}, u32[]{:S(2)}) copy-start(s32[2048]{0:T(1024)} %param.11) | copy-start | bytes 24580
  32.7 2.9 %collective-permute-start.4 = (f32[144,128]{1,0:T(8,128)S(1)}, f32[144,128]{1,0:T(8,128)S(1)}, u32[]{:S(2)}, u32[]{:S(2)}) collective-permute-start(f32[144,128]{1,0:T(8,128)S(1)} %get-tuple-element.22), channel_id=1, source_target_pairs={{0,1},{1,0},{2,3},{3,2},{4,5},{5,4},{6,7},{7,6},{8,9},{9,8},{10,11... | collective-permute-start | bytes 221192 | tf_op jit(solution)/shard_map/ppermute | solution.py:354
  35.5 9.7 %copy-start.9 = (f32[2048]{0:T(1024)S(1)}, f32[2048]{0:T(1024)}, u32[]{:S(2)}) copy-start(f32[2048]{0:T(1024)} %param.9) | copy-start | bytes 24580
  35.6 6.2 %collective-permute-start.7 = (f32[144,128]{1,0:T(8,128)S(1)}, f32[144,128]{1,0:T(8,128)S(1)}, u32[]{:S(2)}, u32[]{:S(2)}) collective-permute-start(f32[144,128]{1,0:T(8,128)S(1)} %shard_map.90.refs_7_.refs_1_), channel_id=1, source_target_pairs={{0,6},{1,7},{2,0},{3,1},{4,2},{5,3},{6,4},{7,5},{8,14},{9,15},{10,... | collective-permute-start | bytes 221192 | tf_op jit(solution)/shard_map/ppermute | solution.py:360
  38.4 4.8 %collective-permute-start.6 = (f32[144,128]{1,0:T(8,128)S(1)}, f32[144,128]{1,0:T(8,128)S(1)}, u32[]{:S(2)}, u32[]{:S(2)}) collective-permute-start(f32[144,128]{1,0:T(8,128)S(1)} %shard_map.90.refs_7_.refs_1_), channel_id=1, source_target_pairs={{0,4},{1,5},{2,6},{3,7},{4,0},{5,1},{6,2},{7,3},{8,12},{9,13},{10,... | collective-permute-start | bytes 221192 | tf_op jit(solution)/shard_map/ppermute | solution.py:360
  38.7 6.5 %collective-permute-start.5 = (f32[144,128]{1,0:T(8,128)S(1)}, f32[144,128]{1,0:T(8,128)S(1)}, u32[]{:S(2)}, u32[]{:S(2)}) collective-permute-start(f32[144,128]{1,0:T(8,128)S(1)} %shard_map.90.refs_7_.refs_1_), channel_id=1, source_target_pairs={{0,2},{1,3},{2,4},{3,5},{4,6},{5,7},{6,0},{7,1},{8,10},{9,11},{10,... | collective-permute-start | bytes 221192 | tf_op jit(solution)/shard_map/ppermute | solution.py:360
  46.0 3.9 %collective-permute-start.9 = (f32[256,128]{1,0:T(8,128)S(1)}, f32[256,128]{1,0:T(8,128)S(1)}, u32[]{:S(2)}, u32[]{:S(2)}) collective-permute-start(f32[256,128]{1,0:T(8,128)S(1)} %get-tuple-element.24.refs_1_.refs_4_), channel_id=1, source_target_pairs={{8,0},{16,8},{24,16},{32,24},{40,32},{48,40},{56,48},{64,56},{72,6... | collective-permute-start | bytes 393224 | tf_op jit(solution)/shard_map/ppermute | solution.py:317
  47.3 7.1 %collective-permute-start.8 = (f32[256,128]{1,0:T(8,128)S(1)}, f32[256,128]{1,0:T(8,128)S(1)}, u32[]{:S(2)}, u32[]{:S(2)}) collective-permute-start(f32[256,128]{1,0:T(8,128)S(1)} %get-tuple-element.24.refs_1_.refs_4_), channel_id=1, source_target_pairs={{0,8},{8,16},{16,24},{24,32},{32,40},{40,48},{48,56},{56,64},{64,7... | collective-permute-start | bytes 393224 | tf_op jit(solution)/shard_map/ppermute | solution.py:317
  56.2 3.3 %collective-permute-start.10 = (f32[144,128]{1,0:T(8,128)S(1)}, f32[144,128]{1,0:T(8,128)S(1)}, u32[]{:S(2)}, u32[]{:S(2)}) collective-permute-start(f32[144,128]{1,0:T(8,128)S(1)} %get-tuple-element.26), channel_id=1, source_target_pairs={{0,1},{1,0},{2,3},{3,2},{4,5},{5,4},{6,7},{7,6},{8,9},{9,8},{10,11... | collective-permute-start | bytes 221192 | tf_op jit(solution)/shard_map/ppermute | solution.py:354
  59.6 4.0 %collective-permute-start.13 = (f32[144,128]{1,0:T(8,128)S(1)}, f32[144,128]{1,0:T(8,128)S(1)}, u32[]{:S(2)}, u32[]{:S(2)}) collective-permute-start(f32[144,128]{1,0:T(8,128)S(1)} %shard_map.96.refs_7_.refs_0_), channel_id=1, source_target_pairs={{0,6},{1,7},{2,0},{3,1},{4,2},{5,3},{6,4},{7,5},{8,14},{9,15},{10,... | collective-permute-start | bytes 221192 | tf_op jit(solution)/shard_map/ppermute | solution.py:360
  59.9 4.7 %collective-permute-start.12 = (f32[144,128]{1,0:T(8,128)S(1)}, f32[144,128]{1,0:T(8,128)S(1)}, u32[]{:S(2)}, u32[]{:S(2)}) collective-permute-start(f32[144,128]{1,0:T(8,128)S(1)} %shard_map.96.refs_7_.refs_0_), channel_id=1, source_target_pairs={{0,4},{1,5},{2,6},{3,7},{4,0},{5,1},{6,2},{7,3},{8,12},{9,13},{10,... | collective-permute-start | bytes 221192 | tf_op jit(solution)/shard_map/ppermute | solution.py:360
  60.4 6.5 %collective-permute-start.11 = (f32[144,128]{1,0:T(8,128)S(1)}, f32[144,128]{1,0:T(8,128)S(1)}, u32[]{:S(2)}, u32[]{:S(2)}) collective-permute-start(f32[144,128]{1,0:T(8,128)S(1)} %shard_map.96.refs_7_.refs_0_), channel_id=1, source_target_pairs={{0,2},{1,3},{2,4},{3,5},{4,6},{5,7},{6,0},{7,1},{8,10},{9,11},{10,... | collective-permute-start | bytes 221192 | tf_op jit(solution)/shard_map/ppermute | solution.py:360
  67.1 12.4 %collective-permute-start.14 = (f32[2,128,128]{2,1,0:T(8,128)S(1)}, f32[2,128,128]{2,1,0:T(8,128)S(1)}, u32[]{:S(2)}, u32[]{:S(2)}) collective-permute-start(f32[2,128,128]{2,1,0:T(8,128)S(1)} %get-tuple-element.35.mine), channel_id=1, source_target_pairs={{0,1},{1,0},{2,3},{3,2},{4,5},{5,4},{6,7},{7,6},{8,9},{9,8},{10,11... | collective-permute-start | bytes 393224 | tf_op jit(solution)/shard_map/ppermute | solution.py:354

commit v5 on v4

--- a/solution.py
+++ b/solution.py
@@ -50,15 +50,16 @@
         inside = np.abs(offset) <= reach
         along = np.where(inside, kernel[np.clip(offset + reach, 0, 2 * reach)], 0.0)
         blocks.append(np.concatenate(bf16_pair(np.kron(vertical, along) * scale)))
-    return blocks, bf16_pair(np.kron(np.eye(CORES), lateral))
+    high, low = bf16_pair(lateral)
+    return blocks, np.block([[high, low], [high, np.zeros_like(low)]])
 
 
 class Constants:
     def __init__(self, levels, rows, columns, members):
         self.places, arrays, start = {}, [], 0
         for power in (2, 1):
-            blocks, pair = local_matrices(levels, rows, columns, power, float(members) ** (-power / 2))
-            for name, array in list(zip("boa", blocks)) + list(zip("hl", pair)):
+            blocks, across = local_matrices(levels, rows, columns, power, float(members) ** (-power / 2))
+            for name, array in list(zip("boa", blocks)) + [("y", across)]:
                 self.places[power, name] = slice(start, start + array.shape[0])
                 arrays.append(array)
                 start += array.shape[0]
@@ -120,32 +121,31 @@
     return jnp.where(lax.broadcasted_iota(jnp.int32, (1, slots), 1) < count_ref[0], 1.0, 0.0)
 
 
-def mixed_pairs(p_refs, g_refs, rows_matrix, mixed):
-    total = g_refs[0].shape[0]
-    for pair in range(mixed.shape[0]):
+def mix_rows(p_refs, g_refs, rows_matrix, mixed):
+    total, columns = g_refs[0].shape
+    for first in range(0, mixed.shape[0], 2):
         sides = []
-        for member in (2 * pair, 2 * pair + 1):
+        for member in (first, first + 1):
             sides.append(jnp.concatenate([p[member].astype(F32) * g[...] for p, g in zip(p_refs, g_refs)], axis=0))
         high, low = split(jnp.concatenate(sides, axis=1))
         product = dot(rows_matrix, high)
         high, low = split(product[:total] + product[total:] + dot(rows_matrix[:total], low))
-        mixed[pair, :total] = high
-        mixed[pair, total:] = low
-
-
-def across_columns(pair, mixed, pair_high, pair_low):
-    total = mixed.shape[1] // 2
-    product = dot(mixed[pair], pair_high)
-    return product[:total] + product[total:] + dot(mixed[pair, :total], pair_low)
+        for i in range(2):
+            lanes = slice(i * columns, (i + 1) * columns)
+            mixed[first + i, :, :columns] = high[:, lanes]
+            mixed[first + i, :, columns:] = low[:, lanes]
+
+
+def across_columns(member, mixed, matrix):
+    product = dot(mixed[member], matrix)
+    columns = product.shape[1] // 2
+    return product[:, :columns] + product[:, columns:]
 
 
 def summed_members(field, weigh, p_side, g_side, constants, places, which, mixed):
-    columns = g_side.shape[1]
-    mixed_pairs([p_side], [g_side], constants[places[2, which]], mixed)
-    for pair in range(mixed.shape[0]):
-        spread = across_columns(pair, mixed, constants[places[2, "h"]], constants[places[2, "l"]])
-        field = field + weigh[2 * pair].astype(F32) * spread[:, :columns]
-        field = field + weigh[2 * pair + 1].astype(F32) * spread[:, columns:]
+    mix_rows([p_side], [g_side], constants[places[2, which]], mixed)
+    for member in range(mixed.shape[0]):
+        field = field + weigh[member].astype(F32) * across_columns(member, mixed, constants[places[2, "y"]])
     return field
 
 
@@ -201,13 +201,10 @@
 
 
 def alpha_kernel(places, p0, p1, p2, g0, g1, g2, constants, after, alpha, token, mixed):
-    columns = g0.shape[1]
     matrix = jnp.concatenate([constants[places[1, name]] for name in "boa"], axis=1)
-    mixed_pairs((p0, p1, p2), (g0, g1, g2), matrix, mixed)
-    for pair in range(mixed.shape[0]):
-        spread = across_columns(pair, mixed, constants[places[1, "h"]], constants[places[1, "l"]])
-        alpha[2 * pair] = spread[:, :columns]
-        alpha[2 * pair + 1] = spread[:, columns:]
+    mix_rows((p0, p1, p2), (g0, g1, g2), matrix, mixed)
+    for member in range(mixed.shape[0]):
+        alpha[member] = across_columns(member, mixed, constants[places[1, "y"]])
     token[...] = jnp.zeros(token.shape, F32)
 
 
@@ -274,14 +271,21 @@
     return step0 + step1 * (1.0 - step0 + beta), -step1 * step0
 
 
-def final_kernel(place, scalars, alpha0, alpha1, mine, other, alpha, increment):
+def final_kernel(place, scalars, alpha0, alpha1, mine, other, alpha_out, increment_out, alpha, increment, sems):
     first, second = combination(scalars)
-    for member in range(alpha.shape[0]):
-        alpha[member] = first * alpha0[member] + second * alpha1[member]
     core = lax.rem(place[0], CORES)
     half = mine.shape[1]
     for part, at in ((mine, core), (other, 1 - core)):
         increment[pl.ds(pl.multiple_of(at * half, half), half)] = first * part[0] + second * part[1]
+    copies = [pltpu.make_async_copy(increment, increment_out, sems.at[0])]
+    copies[0].start()
+    for member in range(0, alpha.shape[0], 2):
+        pair = pl.ds(member, 2)
+        alpha[pair] = first * alpha0[pair] + second * alpha1[pair]
+        copies.append(pltpu.make_async_copy(alpha.at[pair], alpha_out.at[pair], sems.at[1 + member // 2]))
+        copies[-1].start()
+    for copy in copies:
+        copy.wait()
 
 
 def in_vmem(x):
@@ -296,10 +300,10 @@
     return x, pl.BlockSpec(memory_space=pl.ANY)
 
 
-def call(kernel, outs, args, scratch=()):
+def call(kernel, outs, args, scratch=(), out_space=pltpu.VMEM):
     single = not isinstance(outs, list)
     shapes = [jax.ShapeDtypeStruct(shape, F32) for shape in ([outs] if single else outs)]
-    out_spec = pl.BlockSpec(memory_space=pltpu.VMEM)
+    out_spec = pl.BlockSpec(memory_space=out_space)
     return pl.pallas_call(
         kernel,
         out_shape=shapes[0] if single else shapes,
@@ -344,7 +348,7 @@
     place = lax.axis_index("ens").reshape(1)
     vmem = lambda *xs: [in_vmem(x) for x in xs]
 
-    mixed = pltpu.VMEM((members // 2, 2 * cells, CORES * columns), BF16)
+    mixed = pltpu.VMEM((members, cells, 2 * columns), BF16)
 
     def own_and_after(g, g_after):
         part = call(bound(own_kernel, places), field_shape, vmem(p, g, constants), [mixed])
@@ -409,6 +413,8 @@
     alpha, increment = call(
         final_kernel, [(members, cells, columns), field_shape],
         [in_smem(place)] + vmem(scalars, alpha0, alpha1, mine, other),
+        [pltpu.VMEM((members, cells, columns), F32), pltpu.VMEM(field_shape, F32), pltpu.SemaphoreType.DMA((members,))],
+        out_space=pl.ANY,
     )
     return alpha.reshape(perturbations.shape), increment.reshape(levels, rows, columns)
 

time: 81.6 us -> 81.2 us (level)
  Pallas kernels: 16.6 us -> 15.2 us
    pallas_call x14, Pallas kernels: 16.6 us -> 15.2 us  [call(): pl.pallas_call(kernel, out_shape=shapes[0] if single else shapes, in_spec...]
  transfers between devices with their start and end apart: 15 -> 15, of which waited for: 10 -> 10; matrix products, arithmetic and copies ran while one was open for 0% -> 0% of each run, Pallas kernels for 13% -> 12%
where the time goes in v5:
time: 81.2 us; the launch traced here: 80.9 us
  starting transfers between devices  25.8 us (32%)
  waiting for transfers between devices  21.1 us (26%)
  Pallas kernels  15.2 us (19%)
  blocking collectives  11.5 us (14%)
  local copies, waits for them, and re-layouts  5.6 us (7%)
  between operations  1.61 us (2%)
    pallas_call x14, Pallas kernels, call(): pl.pallas_call(kernel, out_shape=shapes[0] if single else shapes, in_spec...  15.2 us
    ppermute x6, starting transfers between devices, neighbours(): return (lax.ppermute(x, 'tile', up), lax.ppermute(x, 'tile', down))  15.1 us
    ppermute x6, waiting for transfers between devices, neighbours(): return (lax.ppermute(x, 'tile', up), lax.ppermute(x, 'tile', down))  12.3 us
    all_to_all x1, blocking collectives, local(): lax.all_to_all(scalars.reshape(tiles, 1, 128), 'tile', 0, 0)  11.5 us
    ppermute x6, waiting for transfers between devices, from_chips(): arrived.append(lax.ppermute(x, 'ens', route))  7.03 us
    unnamed x22, local copies, waits for them, and re-layouts  5.6 us
    ppermute x6, starting transfers between devices, from_chips(): arrived.append(lax.ppermute(x, 'ens', route))  5.47 us
    ppermute x3, starting transfers between devices, other_core(): return lax.ppermute(x, 'ens', [(i, i ^ 1) for i in range(ens)])  5.23 us
  transfers between devices with their start and end apart: 15, of which 10 were waited for; matrix products, arithmetic and copies ran while one was open for 0% of the time, Pallas kernels for 12%

profile of v5, /device:TPU:1, one launch (start us, length us, event | category | flops | bytes accessed | tf_op | source)
XLA Modules:
  0.0 80.9 jit_solution(6036295118614968350)
XLA Ops:
  0.6 8.7 %collective-permute-start.2 = (bf16[10,256,128]{2,1,0:T(8,128)(2,1)}, bf16[10,256,128]{2,1,0:T(8,128)(2,1)S(1)}, u32[]{:S(2)}, u32[]{:S(2)}) collective-permute-start(bf16[10,256,128]{2,1,0:T(8,128)(2,1)} %bitcast.11), channel_id=1, source_target_pairs={{8,0},{16,8},{24,16},{32,24},{40,32},{48,40},{56,48},{64,56},{72,6... | collective-permute-start | bytes 1966088 | tf_op jit(solution)/shard_map/ppermute | solution.py:321
  10.0 0.0 copy-start.4
  10.0 0.9 %copy-done.4 = f32[16,2048]{1,0:T(8,128)S(1)} copy-done((f32[16,2048]{1,0:T(8,128)S(1)}, f32[16,2048]{1,0:T(8,128)}, u32[]{:S(2)}) %copy-start.4) | copy-done | bytes 131096
  10.9 0.7 copy-done.6
  11.6 0.7 copy-done.8
  12.3 0.7 copy-done.10
  13.0 0.7 shard_map.86
  13.7 4.9 %collective-permute-start.3 = (f32[256,128]{1,0:T(8,128)S(1)}, f32[256,128]{1,0:T(8,128)S(1)}, u32[]{:S(2)}, u32[]{:S(2)}) collective-permute-start(f32[256,128]{1,0:T(8,128)S(1)} %get-tuple-element.20.refs_1_.refs_4_), channel_id=1, source_target_pairs={{8,0},{16,8},{24,16},{32,24},{40,32},{48,40},{56,48},{64,56},{72,6... | collective-permute-start | bytes 393224 | tf_op jit(solution)/shard_map/ppermute | solution.py:321
  18.6 1.5 %copy-done = bf16[3584,256]{1,0:T(8,128)(2,1)S(1)} copy-done((bf16[3584,256]{1,0:T(8,128)(2,1)S(1)}, bf16[3584,256]{1,0:T(8,128)(2,1)}, u32[]{:S(2)}) %copy-start) | copy-done | bytes 1835032
  20.1 1.1 %copy-done.2 = bf16[10,16,16,128]{3,2,1,0:T(8,128)(2,1)S(1)} copy-done((bf16[10,16,16,128]{3,2,1,0:T(8,128)(2,1)S(1)}, bf16[10,16,16,128]{3,2,1,0:T(8,128)(2,1)}, u32[]{:S(2)}) %copy-start.2) | copy-done | bytes 655384
  21.1 1.0 %shard_map.87.refs_3_ = f32[256,128]{1,0:T(8,128)S(1)} custom-call(bf16[10,256,128]{2,1,0:T(8,128)(2,1)S(1)} %bitcast.13, f32[256,128]{1,0:T(8,128)S(1)} %get-tuple-element.20.refs_1_.refs_4_, bf16[3584,256]{1,0:T(8,128)(2,1)S(1)} %copy-done), custom_call_target="tpu_custom_call" | custom-call | tf_op jit(solution)/shard_map/pallas_call | solution.py:307
  22.2 0.0 copy-start.3
  22.2 0.0 copy-start.5
  22.2 0.0 copy-start.7
  22.2 3.5 %collective-permute-done.3.refs_2_.refs_5_ = f32[256,128]{1,0:T(8,128)S(1)} collective-permute-done((f32[256,128]{1,0:T(8,128)S(1)}, f32[256,128]{1,0:T(8,128)S(1)}, u32[]{:S(2)}, u32[]{:S(2)}) %collective-permute-start.3) | collective-permute-done | bytes 131104 | tf_op jit(solution)/shard_map/ppermute | solution.py:321
  25.7 1.1 %shard_map.88.refs_5_ = f32[256,128]{1,0:T(8,128)S(1)} custom-call(bf16[10,256,128]{2,1,0:T(8,128)(2,1)S(1)} %bitcast.14, bf16[10,256,128]{2,1,0:T(8,128)(2,1)S(1)} %collective-permute-done.2.refs_1_.refs_2_, f32[256,128]{1,0:T(8,128)S(1)} %collective-permute-done.3.refs_2_.refs_5_, f32[256,128]{1,0:T(8,128)S(1)} %shard_map.87.refs_3_, ...), custom_call_target="tpu_custom_call" | custom-call | tf_op jit(solution)/shard_map/pallas_call | solution.py:307
  26.8 4.1 %collective-permute-done.1.refs_4_.refs_3_ = f32[256,128]{1,0:T(8,128)S(1)} collective-permute-done((f32[256,128]{1,0:T(8,128)S(1)}, f32[256,128]{1,0:T(8,128)S(1)}, u32[]{:S(2)}, u32[]{:S(2)}) %collective-permute-start.1) | collective-permute-done | bytes 131104 | tf_op jit(solution)/shard_map/ppermute | solution.py:321
  30.9 0.0 collective-permute-done.refs_3_.refs_0_
  31.0 1.6 %shard_map.89 = (f32[144,128]{1,0:T(8,128)S(1)}, f32[144,128]{1,0:T(8,128)S(1)}) custom-call(s32[1]{0:T(128)S(6)} %copy.10.refs_0_, s32[1]{0:T(128)} %bitcast.refs_1_.place, bf16[10,256,128]{2,1,0:T(8,128)(2,1)S(1)} %bitcast.15, bf16[10,256,128]{2,1,0:T(8,128)(2,1)S(1)} %collective-permute-done.refs_3_.refs_0_, ...), custom_call_target="tpu_custom_call" | custom-call | tf_op jit(solution)/shard_map/pallas_call | solution.py:307
  32.5 2.0 %collective-permute-start.4 = (f32[144,128]{1,0:T(8,128)S(1)}, f32[144,128]{1,0:T(8,128)S(1)}, u32[]{:S(2)}, u32[]{:S(2)}) collective-permute-start(f32[144,128]{1,0:T(8,128)S(1)} %get-tuple-element.22), channel_id=1, source_target_pairs={{0,1},{1,0},{2,3},{3,2},{4,5},{5,4},{6,7},{7,6},{8,9},{9,8},{10,11... | collective-permute-start | bytes 221192 | tf_op jit(solution)/shard_map/ppermute | solution.py:358
  34.5 0.9 %collective-permute-done.4.second = f32[144,128]{1,0:T(8,128)S(1)} collective-permute-done((f32[144,128]{1,0:T(8,128)S(1)}, f32[144,128]{1,0:T(8,128)S(1)}, u32[]{:S(2)}, u32[]{:S(2)}) %collective-permute-start.4) | collective-permute-done | bytes 73760 | tf_op jit(solution)/shard_map/ppermute | solution.py:358
  35.4 0.0 copy-start.9
  35.4 2.8 %collective-permute-start.7 = (f32[144,128]{1,0:T(8,128)S(1)}, f32[144,128]{1,0:T(8,128)S(1)}, u32[]{:S(2)}, u32[]{:S(2)}) collective-permute-start(f32[144,128]{1,0:T(8,128)S(1)} %shard_map.90.refs_7_.refs_1_), channel_id=1, source_target_pairs={{0,6},{1,7},{2,0},{3,1},{4,2},{5,3},{6,4},{7,5},{8,14},{9,15},{10,... | collective-permute-start | bytes 221192 | tf_op jit(solution)/shard_map/ppermute | solution.py:364
  38.2 0.3 collective-permute-start.6
  38.6 0.7 collective-permute-start.5
  39.3 2.2 %shard_map.91 = (f32[10,256,128]{2,1,0:T(8,128)S(1)}, f32[8,128]{1,0:T(8,128)S(1)}) custom-call(bf16[10,256,128]{2,1,0:T(8,128)(2,1)S(1)} %collective-permute-done.refs_3_.refs_0_, bf16[10,256,128]{2,1,0:T(8,128)(2,1)S(1)} %bitcast.16, bf16[10,256,128]{2,1,0:T(8,128)(2,1)S(1)} %collective-permute-done.2.refs_1_.refs_2_, ...), custom_call_target="tpu_custom_call" | custom-call | tf_op jit(solution)/shard_map/pallas_call | solution.py:307
  41.5 1.5 %collective-permute-done.6.refs_3_ = f32[144,128]{1,0:T(8,128)S(1)} collective-permute-done((f32[144,128]{1,0:T(8,128)S(1)}, f32[144,128]{1,0:T(8,128)S(1)}, u32[]{:S(2)}, u32[]{:S(2)}) %collective-permute-start.6) | collective-permute-done | bytes 73760 | tf_op jit(solution)/shard_map/ppermute | solution.py:364
  43.0 2.1 %collective-permute-done.5.refs_2_ = f32[144,128]{1,0:T(8,128)S(1)} collective-permute-done((f32[144,128]{1,0:T(8,128)S(1)}, f32[144,128]{1,0:T(8,128)S(1)}, u32[]{:S(2)}, u32[]{:S(2)}) %collective-permute-start.5) | collective-permute-done | bytes 73760 | tf_op jit(solution)/shard_map/ppermute | solution.py:364
  45.1 0.7 shard_map.92
  45.8 1.2 %collective-permute-start.9 = (f32[256,128]{1,0:T(8,128)S(1)}, f32[256,128]{1,0:T(8,128)S(1)}, u32[]{:S(2)}, u32[]{:S(2)}) collective-permute-start(f32[256,128]{1,0:T(8,128)S(1)} %get-tuple-element.24.refs_1_.refs_4_), channel_id=1, source_target_pairs={{8,0},{16,8},{24,16},{32,24},{40,32},{48,40},{56,48},{64,56},{72,6... | collective-permute-start | bytes 393224 | tf_op jit(solution)/shard_map/ppermute | solution.py:321
  47.0 0.4 collective-permute-start.8
  47.4 1.1 %shard_map.93.refs_3_ = f32[256,128]{1,0:T(8,128)S(1)} custom-call(bf16[10,256,128]{2,1,0:T(8,128)(2,1)S(1)} %bitcast.17, f32[256,128]{1,0:T(8,128)S(1)} %get-tuple-element.24.refs_1_.refs_4_, bf16[3584,256]{1,0:T(8,128)(2,1)S(1)} %copy-done.1), custom_call_target="tpu_custom_call" | custom-call | tf_op jit(solution)/shard_map/pallas_call | solution.py:307
  48.4 1.3 %collective-permute-done.9.refs_2_.refs_5_ = f32[256,128]{1,0:T(8,128)S(1)} collective-permute-done((f32[256,128]{1,0:T(8,128)S(1)}, f32[256,128]{1,0:T(8,128)S(1)}, u32[]{:S(2)}, u32[]{:S(2)}) %collective-permute-start.9) | collective-permute-done | bytes 131104 | tf_op jit(solution)/shard_map/ppermute | solution.py:321
  49.7 1.1 %shard_map.94.refs_5_ = f32[256,128]{1,0:T(8,128)S(1)} custom-call(bf16[10,256,128]{2,1,0:T(8,128)(2,1)S(1)} %bitcast.18, bf16[10,256,128]{2,1,0:T(8,128)(2,1)S(1)} %collective-permute-done.2.refs_1_.refs_2_, f32[256,128]{1,0:T(8,128)S(1)} %collective-permute-done.9.refs_2_.refs_5_, f32[256,128]{1,0:T(8,128)S(1)} %shard_map.93.refs_3_, ...), custom_call_target="tpu_custom_call" | custom-call | tf_op jit(solution)/shard_map/pallas_call | solution.py:307
  50.8 3.3 %collective-permute-done.8.refs_4_.refs_3_ = f32[256,128]{1,0:T(8,128)S(1)} collective-permute-done((f32[256,128]{1,0:T(8,128)S(1)}, f32[256,128]{1,0:T(8,128)S(1)}, u32[]{:S(2)}, u32[]{:S(2)}) %collective-permute-start.8) | collective-permute-done | bytes 131104 | tf_op jit(solution)/shard_map/ppermute | solution.py:321
  54.1 1.6 %shard_map.95 = (f32[144,128]{1,0:T(8,128)S(1)}, f32[144,128]{1,0:T(8,128)S(1)}) custom-call(s32[1]{0:T(128)S(6)} %copy.10.refs_0_, s32[1]{0:T(128)} %bitcast.refs_1_.place, bf16[10,256,128]{2,1,0:T(8,128)(2,1)S(1)} %bitcast.19, bf16[10,256,128]{2,1,0:T(8,128)(2,1)S(1)} %collective-permute-done.refs_3_.refs_0_, ...), custom_call_target="tpu_custom_call" | custom-call | tf_op jit(solution)/shard_map/pallas_call | solution.py:307
  55.7 2.4 %collective-permute-start.10 = (f32[144,128]{1,0:T(8,128)S(1)}, f32[144,128]{1,0:T(8,128)S(1)}, u32[]{:S(2)}, u32[]{:S(2)}) collective-permute-start(f32[144,128]{1,0:T(8,128)S(1)} %get-tuple-element.26), channel_id=1, source_target_pairs={{0,1},{1,0},{2,3},{3,2},{4,5},{5,4},{6,7},{7,6},{8,9},{9,8},{10,11... | collective-permute-start | bytes 221192 | tf_op jit(solution)/shard_map/ppermute | solution.py:358
  58.2 0.9 %collective-permute-done.10.second = f32[144,128]{1,0:T(8,128)S(1)} collective-permute-done((f32[144,128]{1,0:T(8,128)S(1)}, f32[144,128]{1,0:T(8,128)S(1)}, u32[]{:S(2)}, u32[]{:S(2)}) %collective-permute-start.10) | collective-permute-done | bytes 73760 | tf_op jit(solution)/shard_map/ppermute | solution.py:358
  59.1 0.4 collective-permute-start.13
  59.4 0.5 collective-permute-start.12
  59.9 0.8 collective-permute-start.11
  60.7 2.3 %shard_map.97 = (f32[10,256,128]{2,1,0:T(8,128)S(1)}, f32[8,128]{1,0:T(8,128)S(1)}) custom-call(bf16[10,256,128]{2,1,0:T(8,128)(2,1)S(1)} %collective-permute-done.refs_3_.refs_0_, bf16[10,256,128]{2,1,0:T(8,128)(2,1)S(1)} %bitcast.20, bf16[10,256,128]{2,1,0:T(8,128)(2,1)S(1)} %collective-permute-done.2.refs_1_.refs_2_, ...), custom_call_target="tpu_custom_call" | custom-call | tf_op jit(solution)/shard_map/pallas_call | solution.py:307
  63.0 1.2 %collective-permute-done.12.refs_2_ = f32[144,128]{1,0:T(8,128)S(1)} collective-permute-done((f32[144,128]{1,0:T(8,128)S(1)}, f32[144,128]{1,0:T(8,128)S(1)}, u32[]{:S(2)}, u32[]{:S(2)}) %collective-permute-start.12) | collective-permute-done | bytes 73760 | tf_op jit(solution)/shard_map/ppermute | solution.py:364
  64.2 2.3 %collective-permute-done.11.refs_1_ = f32[144,128]{1,0:T(8,128)S(1)} collective-permute-done((f32[144,128]{1,0:T(8,128)S(1)}, f32[144,128]{1,0:T(8,128)S(1)}, u32[]{:S(2)}, u32[]{:S(2)}) %collective-permute-start.11) | collective-permute-done | bytes 73760 | tf_op jit(solution)/shard_map/ppermute | solution.py:364
  66.4 0.2 shard_map.98
  66.6 0.8 %collective-permute-start.14 = (f32[2,128,128]{2,1,0:T(8,128)S(1)}, f32[2,128,128]{2,1,0:T(8,128)S(1)}, u32[]{:S(2)}, u32[]{:S(2)}) collective-permute-start(f32[2,128,128]{2,1,0:T(8,128)S(1)} %get-tuple-element.35.mine), channel_id=1, source_target_pairs={{0,1},{1,0},{2,3},{3,2},{4,5},{5,4},{6,7},{7,6},{8,9},{9,8},{10,11... | collective-permute-start | bytes 393224 | tf_op jit(solution)/shard_map/ppermute | solution.py:358
  67.5 11.5 %all_to_all.5 = f32[32,1,128]{2,1,0:T(1,128)S(1)} all-to-all(f32[32,1,128]{2,1,0:T(1,128)S(1)} %bitcast.28), channel_id=1, replica_groups=mesh['tile'=32,'ens'=8] {'tile'}, dimensions={0} | all-to-all | bytes 32768 | tf_op jit(solution)/shard_map/all_to_all | solution.py:412
  79.0 1.7 %shard_map.99 = (f32[10,256,128]{2,1,0:T(8,128)}, f32[256,128]{1,0:T(8,128)}) custom-call(s32[1]{0:T(128)} %bitcast.refs_1_.place, f32[32,128]{1,0:T(8,128)S(1)} %bitcast.25, f32[10,256,128]{2,1,0:T(8,128)S(1)} %get-tuple-element.33.alpha0, f32[10,256,128]{2,1,0:T(8,128)S(1)} %get-tuple-element.34.alpha1, f32[2,128,128]{2,1,0:T(8,128)S(1)} %get-tuple-element.35.mine, ...), custom_call_target="tpu_custom_call" | custom-call | tf_op jit(solution)/shard_map/pallas_call | solution.py:307
  (19 shorter events, 0.1 us)
Async XLA Ops:
  0.6 25.1 %collective-permute-start.2 = (bf16[10,256,128]{2,1,0:T(8,128)(2,1)}, bf16[10,256,128]{2,1,0:T(8,128)(2,1)S(1)}, u32[]{:S(2)}, u32[]{:S(2)}) collective-permute-start(bf16[10,256,128]{2,1,0:T(8,128)(2,1)} %bitcast.11), channel_id=1, source_target_pairs={{8,0},{16,8},{24,16},{32,24},{40,32},{48,40},{56,48},{64,56},{72,6... | collective-permute-start | bytes 1966088 | tf_op jit(solution)/shard_map/ppermute | solution.py:321
  9.3 21.6 %collective-permute-start = (bf16[10,256,128]{2,1,0:T(8,128)(2,1)}, bf16[10,256,128]{2,1,0:T(8,128)(2,1)S(1)}, u32[]{:S(2)}, u32[]{:S(2)}) collective-permute-start(bf16[10,256,128]{2,1,0:T(8,128)(2,1)} %bitcast.12), channel_id=1, source_target_pairs={{0,8},{8,16},{16,24},{24,32},{32,40},{40,48},{48,56},{56,64},{64,7... | collective-permute-start | bytes 1966088 | tf_op jit(solution)/shard_map/ppermute | solution.py:321
  10.0 0.9 %copy-start.4 = (f32[16,2048]{1,0:T(8,128)S(1)}, f32[16,2048]{1,0:T(8,128)}, u32[]{:S(2)}) copy-start(f32[16,2048]{1,0:T(8,128)} %refs_7_.3) | copy-start | bytes 393220
  10.9 0.7 copy-start.6
  11.6 0.7 copy-start.8
  12.3 0.7 copy-start.10
  13.7 12.0 %collective-permute-start.3 = (f32[256,128]{1,0:T(8,128)S(1)}, f32[256,128]{1,0:T(8,128)S(1)}, u32[]{:S(2)}, u32[]{:S(2)}) collective-permute-start(f32[256,128]{1,0:T(8,128)S(1)} %get-tuple-element.20.refs_1_.refs_4_), channel_id=1, source_target_pairs={{8,0},{16,8},{24,16},{32,24},{40,32},{48,40},{56,48},{64,56},{72,6... | collective-permute-start | bytes 393224 | tf_op jit(solution)/shard_map/ppermute | solution.py:321
  18.6 12.4 %collective-permute-start.1 = (f32[256,128]{1,0:T(8,128)S(1)}, f32[256,128]{1,0:T(8,128)S(1)}, u32[]{:S(2)}, u32[]{:S(2)}) collective-permute-start(f32[256,128]{1,0:T(8,128)S(1)} %get-tuple-element.20.refs_1_.refs_4_), channel_id=1, source_target_pairs={{0,8},{8,16},{16,24},{24,32},{32,40},{40,48},{48,56},{56,64},{64,7... | collective-permute-start | bytes 393224 | tf_op jit(solution)/shard_map/ppermute | solution.py:321
  18.6 1.5 %copy-start = (bf16[3584,256]{1,0:T(8,128)(2,1)S(1)}, bf16[3584,256]{1,0:T(8,128)(2,1)}, u32[]{:S(2)}) copy-start(bf16[3584,256]{1,0:T(8,128)(2,1)} %constant.6.clone.refs_2_.refs_4_.refs_6_) | copy-start | bytes 5505028
  20.1 1.1 %copy-start.2 = (bf16[10,16,16,128]{3,2,1,0:T(8,128)(2,1)S(1)}, bf16[10,16,16,128]{3,2,1,0:T(8,128)(2,1)}, u32[]{:S(2)}) copy-start(bf16[10,16,16,128]{3,2,1,0:T(8,128)(2,1)} %param.7) | copy-start | bytes 1966084
  21.1 4.6 %copy-start.1 = (bf16[3584,256]{1,0:T(8,128)(2,1)S(1)}, bf16[3584,256]{1,0:T(8,128)(2,1)}, u32[]{:S(2)}) copy-start(bf16[3584,256]{1,0:T(8,128)(2,1)} %constant.6.clone.refs_2_.refs_4_.refs_6_) | copy-start | bytes 5505028
  22.2 8.7 %copy-start.3 = (bf16[10,16,16,128]{3,2,1,0:T(8,128)(2,1)S(1)}, bf16[10,16,16,128]{3,2,1,0:T(8,128)(2,1)}, u32[]{:S(2)}) copy-start(bf16[10,16,16,128]{3,2,1,0:T(8,128)(2,1)} %param.7) | copy-start | bytes 1966084
  22.2 8.7 %copy-start.5 = (f32[16,2048]{1,0:T(8,128)S(1)}, f32[16,2048]{1,0:T(8,128)}, u32[]{:S(2)}) copy-start(f32[16,2048]{1,0:T(8,128)} %refs_7_.3) | copy-start | bytes 393220
  22.2 8.7 %copy-start.7 = (s32[2048]{0:T(1024)S(1)}, s32[2048]{0:T(1024)}, u32[]{:S(2)}) copy-start(s32[2048]{0:T(1024)} %param.11) | copy-start | bytes 24580
  32.5 2.9 %collective-permute-start.4 = (f32[144,128]{1,0:T(8,128)S(1)}, f32[144,128]{1,0:T(8,128)S(1)}, u32[]{:S(2)}, u32[]{:S(2)}) collective-permute-start(f32[144,128]{1,0:T(8,128)S(1)} %get-tuple-element.22), channel_id=1, source_target_pairs={{0,1},{1,0},{2,3},{3,2},{4,5},{5,4},{6,7},{7,6},{8,9},{9,8},{10,11... | collective-permute-start | bytes 221192 | tf_op jit(solution)/shard_map/ppermute | solution.py:358
  35.4 9.7 %copy-start.9 = (f32[2048]{0:T(1024)S(1)}, f32[2048]{0:T(1024)}, u32[]{:S(2)}) copy-start(f32[2048]{0:T(1024)} %param.9) | copy-start | bytes 24580
  35.4 6.1 %collective-permute-start.7 = (f32[144,128]{1,0:T(8,128)S(1)}, f32[144,128]{1,0:T(8,128)S(1)}, u32[]{:S(2)}, u32[]{:S(2)}) collective-permute-start(f32[144,128]{1,0:T(8,128)S(1)} %shard_map.90.refs_7_.refs_1_), channel_id=1, source_target_pairs={{0,6},{1,7},{2,0},{3,1},{4,2},{5,3},{6,4},{7,5},{8,14},{9,15},{10,... | collective-permute-start | bytes 221192 | tf_op jit(solution)/shard_map/ppermute | solution.py:364
  38.2 4.8 %collective-permute-start.6 = (f32[144,128]{1,0:T(8,128)S(1)}, f32[144,128]{1,0:T(8,128)S(1)}, u32[]{:S(2)}, u32[]{:S(2)}) collective-permute-start(f32[144,128]{1,0:T(8,128)S(1)} %shard_map.90.refs_7_.refs_1_), channel_id=1, source_target_pairs={{0,4},{1,5},{2,6},{3,7},{4,0},{5,1},{6,2},{7,3},{8,12},{9,13},{10,... | collective-permute-start | bytes 221192 | tf_op jit(solution)/shard_map/ppermute | solution.py:364
  38.6 6.5 %collective-permute-start.5 = (f32[144,128]{1,0:T(8,128)S(1)}, f32[144,128]{1,0:T(8,128)S(1)}, u32[]{:S(2)}, u32[]{:S(2)}) collective-permute-start(f32[144,128]{1,0:T(8,128)S(1)} %shard_map.90.refs_7_.refs_1_), channel_id=1, source_target_pairs={{0,2},{1,3},{2,4},{3,5},{4,6},{5,7},{6,0},{7,1},{8,10},{9,11},{10,... | collective-permute-start | bytes 221192 | tf_op jit(solution)/shard_map/ppermute | solution.py:364
  45.8 3.9 %collective-permute-start.9 = (f32[256,128]{1,0:T(8,128)S(1)}, f32[256,128]{1,0:T(8,128)S(1)}, u32[]{:S(2)}, u32[]{:S(2)}) collective-permute-start(f32[256,128]{1,0:T(8,128)S(1)} %get-tuple-element.24.refs_1_.refs_4_), channel_id=1, source_target_pairs={{8,0},{16,8},{24,16},{32,24},{40,32},{48,40},{56,48},{64,56},{72,6... | collective-permute-start | bytes 393224 | tf_op jit(solution)/shard_map/ppermute | solution.py:321
  47.0 7.1 %collective-permute-start.8 = (f32[256,128]{1,0:T(8,128)S(1)}, f32[256,128]{1,0:T(8,128)S(1)}, u32[]{:S(2)}, u32[]{:S(2)}) collective-permute-start(f32[256,128]{1,0:T(8,128)S(1)} %get-tuple-element.24.refs_1_.refs_4_), channel_id=1, source_target_pairs={{0,8},{8,16},{16,24},{24,32},{32,40},{40,48},{48,56},{56,64},{64,7... | collective-permute-start | bytes 393224 | tf_op jit(solution)/shard_map/ppermute | solution.py:321
  55.7 3.4 %collective-permute-start.10 = (f32[144,128]{1,0:T(8,128)S(1)}, f32[144,128]{1,0:T(8,128)S(1)}, u32[]{:S(2)}, u32[]{:S(2)}) collective-permute-start(f32[144,128]{1,0:T(8,128)S(1)} %get-tuple-element.26), channel_id=1, source_target_pairs={{0,1},{1,0},{2,3},{3,2},{4,5},{5,4},{6,7},{7,6},{8,9},{9,8},{10,11... | collective-permute-start | bytes 221192 | tf_op jit(solution)/shard_map/ppermute | solution.py:358
  59.1 3.9 %collective-permute-start.13 = (f32[144,128]{1,0:T(8,128)S(1)}, f32[144,128]{1,0:T(8,128)S(1)}, u32[]{:S(2)}, u32[]{:S(2)}) collective-permute-start(f32[144,128]{1,0:T(8,128)S(1)} %shard_map.96.refs_7_.refs_0_), channel_id=1, source_target_pairs={{0,6},{1,7},{2,0},{3,1},{4,2},{5,3},{6,4},{7,5},{8,14},{9,15},{10,... | collective-permute-start | bytes 221192 | tf_op jit(solution)/shard_map/ppermute | solution.py:364
  59.4 4.7 %collective-permute-start.12 = (f32[144,128]{1,0:T(8,128)S(1)}, f32[144,128]{1,0:T(8,128)S(1)}, u32[]{:S(2)}, u32[]{:S(2)}) collective-permute-start(f32[144,128]{1,0:T(8,128)S(1)} %shard_map.96.refs_7_.refs_0_), channel_id=1, source_target_pairs={{0,4},{1,5},{2,6},{3,7},{4,0},{5,1},{6,2},{7,3},{8,12},{9,13},{10,... | collective-permute-start | bytes 221192 | tf_op jit(solution)/shard_map/ppermute | solution.py:364
  59.9 6.5 %collective-permute-start.11 = (f32[144,128]{1,0:T(8,128)S(1)}, f32[144,128]{1,0:T(8,128)S(1)}, u32[]{:S(2)}, u32[]{:S(2)}) collective-permute-start(f32[144,128]{1,0:T(8,128)S(1)} %shard_map.96.refs_7_.refs_0_), channel_id=1, source_target_pairs={{0,2},{1,3},{2,4},{3,5},{4,6},{5,7},{6,0},{7,1},{8,10},{9,11},{10,... | collective-permute-start | bytes 221192 | tf_op jit(solution)/shard_map/ppermute | solution.py:364
  66.6 12.4 %collective-permute-start.14 = (f32[2,128,128]{2,1,0:T(8,128)S(1)}, f32[2,128,128]{2,1,0:T(8,128)S(1)}, u32[]{:S(2)}, u32[]{:S(2)}) collective-permute-start(f32[2,128,128]{2,1,0:T(8,128)S(1)} %get-tuple-element.35.mine), channel_id=1, source_target_pairs={{0,1},{1,0},{2,3},{3,2},{4,5},{5,4},{6,7},{7,6},{8,9},{9,8},{10,11... | collective-permute-start | bytes 393224 | tf_op jit(solution)/shard_map/ppermute | solution.py:358

commit v6 on v5

--- a/solution.py
+++ b/solution.py
@@ -225,6 +225,7 @@
     e = z1 + z2
     size = total(d * d)
     shift = jnp.where(size > 0.0, total(c * d) / jnp.where(size > 0.0, size, 1.0), 0.0)
+    shift = jnp.clip(shift, 0.0, 1.0)
     v = c - shift * d
     w = z1 - shift * e
     values = [

time: 81.2 us -> 81.2 us (level)
  no operation moved by 1% of the time
where the time goes in v6:
time: 81.2 us; the launch traced here: 80.9 us
  starting transfers between devices  25.8 us (32%)
  waiting for transfers between devices  21.1 us (26%)
  Pallas kernels  15.2 us (19%)
  blocking collectives  11.5 us (14%)
  local copies, waits for them, and re-layouts  5.6 us (7%)
  between operations  1.61 us (2%)
    pallas_call x14, Pallas kernels, call(): pl.pallas_call(kernel, out_shape=shapes[0] if single else shapes, in_spec...  15.2 us
    ppermute x6, starting transfers between devices, neighbours(): return (lax.ppermute(x, 'tile', up), lax.ppermute(x, 'tile', down))  15.1 us
    ppermute x6, waiting for transfers between devices, neighbours(): return (lax.ppermute(x, 'tile', up), lax.ppermute(x, 'tile', down))  12.3 us
    all_to_all x1, blocking collectives, local(): lax.all_to_all(scalars.reshape(tiles, 1, 128), 'tile', 0, 0)  11.5 us
    ppermute x6, waiting for transfers between devices, from_chips(): arrived.append(lax.ppermute(x, 'ens', route))  7.03 us
    unnamed x22, local copies, waits for them, and re-layouts  5.6 us
    ppermute x6, starting transfers between devices, from_chips(): arrived.append(lax.ppermute(x, 'ens', route))  5.47 us
    ppermute x3, starting transfers between devices, other_core(): return lax.ppermute(x, 'ens', [(i, i ^ 1) for i in range(ens)])  5.23 us
  transfers between devices with their start and end apart: 15, of which 10 were waited for; matrix products, arithmetic and copies ran while one was open for 0% of the time, Pallas kernels for 12%

profile of v6, /device:TPU:1, one launch (start us, length us, event | category | flops | bytes accessed | tf_op | source)
XLA Modules:
  0.0 80.9 jit_solution(17363414125780150532)
XLA Ops:
  0.6 8.7 %collective-permute-start.2 = (bf16[10,256,128]{2,1,0:T(8,128)(2,1)}, bf16[10,256,128]{2,1,0:T(8,128)(2,1)S(1)}, u32[]{:S(2)}, u32[]{:S(2)}) collective-permute-start(bf16[10,256,128]{2,1,0:T(8,128)(2,1)} %bitcast.11), channel_id=1, source_target_pairs={{8,0},{16,8},{24,16},{32,24},{40,32},{48,40},{56,48},{64,56},{72,6... | collective-permute-start | bytes 1966088 | tf_op jit(solution)/shard_map/ppermute | solution.py:322
  10.0 0.0 copy-start.4
  10.0 0.9 %copy-done.4 = f32[16,2048]{1,0:T(8,128)S(1)} copy-done((f32[16,2048]{1,0:T(8,128)S(1)}, f32[16,2048]{1,0:T(8,128)}, u32[]{:S(2)}) %copy-start.4) | copy-done | bytes 131096
  10.9 0.7 copy-done.6
  11.6 0.7 copy-done.8
  12.3 0.7 copy-done.10
  13.0 0.7 shard_map.86
  13.7 4.9 %collective-permute-start.3 = (f32[256,128]{1,0:T(8,128)S(1)}, f32[256,128]{1,0:T(8,128)S(1)}, u32[]{:S(2)}, u32[]{:S(2)}) collective-permute-start(f32[256,128]{1,0:T(8,128)S(1)} %get-tuple-element.20.refs_1_.refs_4_), channel_id=1, source_target_pairs={{8,0},{16,8},{24,16},{32,24},{40,32},{48,40},{56,48},{64,56},{72,6... | collective-permute-start | bytes 393224 | tf_op jit(solution)/shard_map/ppermute | solution.py:322
  18.6 1.5 %copy-done = bf16[3584,256]{1,0:T(8,128)(2,1)S(1)} copy-done((bf16[3584,256]{1,0:T(8,128)(2,1)S(1)}, bf16[3584,256]{1,0:T(8,128)(2,1)}, u32[]{:S(2)}) %copy-start) | copy-done | bytes 1835032
  20.1 1.1 %copy-done.2 = bf16[10,16,16,128]{3,2,1,0:T(8,128)(2,1)S(1)} copy-done((bf16[10,16,16,128]{3,2,1,0:T(8,128)(2,1)S(1)}, bf16[10,16,16,128]{3,2,1,0:T(8,128)(2,1)}, u32[]{:S(2)}) %copy-start.2) | copy-done | bytes 655384
  21.1 1.0 %shard_map.87.refs_3_ = f32[256,128]{1,0:T(8,128)S(1)} custom-call(bf16[10,256,128]{2,1,0:T(8,128)(2,1)S(1)} %bitcast.13, f32[256,128]{1,0:T(8,128)S(1)} %get-tuple-element.20.refs_1_.refs_4_, bf16[3584,256]{1,0:T(8,128)(2,1)S(1)} %copy-done), custom_call_target="tpu_custom_call" | custom-call | tf_op jit(solution)/shard_map/pallas_call | solution.py:308
  22.2 0.0 copy-start.3
  22.2 0.0 copy-start.5
  22.2 0.0 copy-start.7
  22.2 3.5 %collective-permute-done.3.refs_2_.refs_5_ = f32[256,128]{1,0:T(8,128)S(1)} collective-permute-done((f32[256,128]{1,0:T(8,128)S(1)}, f32[256,128]{1,0:T(8,128)S(1)}, u32[]{:S(2)}, u32[]{:S(2)}) %collective-permute-start.3) | collective-permute-done | bytes 131104 | tf_op jit(solution)/shard_map/ppermute | solution.py:322
  25.7 1.1 %shard_map.88.refs_5_ = f32[256,128]{1,0:T(8,128)S(1)} custom-call(bf16[10,256,128]{2,1,0:T(8,128)(2,1)S(1)} %bitcast.14, bf16[10,256,128]{2,1,0:T(8,128)(2,1)S(1)} %collective-permute-done.2.refs_1_.refs_2_, f32[256,128]{1,0:T(8,128)S(1)} %collective-permute-done.3.refs_2_.refs_5_, f32[256,128]{1,0:T(8,128)S(1)} %shard_map.87.refs_3_, ...), custom_call_target="tpu_custom_call" | custom-call | tf_op jit(solution)/shard_map/pallas_call | solution.py:308
  26.8 4.1 %collective-permute-done.1.refs_4_.refs_3_ = f32[256,128]{1,0:T(8,128)S(1)} collective-permute-done((f32[256,128]{1,0:T(8,128)S(1)}, f32[256,128]{1,0:T(8,128)S(1)}, u32[]{:S(2)}, u32[]{:S(2)}) %collective-permute-start.1) | collective-permute-done | bytes 131104 | tf_op jit(solution)/shard_map/ppermute | solution.py:322
  30.9 0.0 collective-permute-done.refs_3_.refs_0_
  31.0 1.6 %shard_map.89 = (f32[144,128]{1,0:T(8,128)S(1)}, f32[144,128]{1,0:T(8,128)S(1)}) custom-call(s32[1]{0:T(128)S(6)} %copy.10.refs_0_, s32[1]{0:T(128)} %bitcast.refs_1_.place, bf16[10,256,128]{2,1,0:T(8,128)(2,1)S(1)} %bitcast.15, bf16[10,256,128]{2,1,0:T(8,128)(2,1)S(1)} %collective-permute-done.refs_3_.refs_0_, ...), custom_call_target="tpu_custom_call" | custom-call | tf_op jit(solution)/shard_map/pallas_call | solution.py:308
  32.5 2.0 %collective-permute-start.4 = (f32[144,128]{1,0:T(8,128)S(1)}, f32[144,128]{1,0:T(8,128)S(1)}, u32[]{:S(2)}, u32[]{:S(2)}) collective-permute-start(f32[144,128]{1,0:T(8,128)S(1)} %get-tuple-element.22), channel_id=1, source_target_pairs={{0,1},{1,0},{2,3},{3,2},{4,5},{5,4},{6,7},{7,6},{8,9},{9,8},{10,11... | collective-permute-start | bytes 221192 | tf_op jit(solution)/shard_map/ppermute | solution.py:359
  34.5 0.9 %collective-permute-done.4.second = f32[144,128]{1,0:T(8,128)S(1)} collective-permute-done((f32[144,128]{1,0:T(8,128)S(1)}, f32[144,128]{1,0:T(8,128)S(1)}, u32[]{:S(2)}, u32[]{:S(2)}) %collective-permute-start.4) | collective-permute-done | bytes 73760 | tf_op jit(solution)/shard_map/ppermute | solution.py:359
  35.4 0.0 copy-start.9
  35.4 2.8 %collective-permute-start.7 = (f32[144,128]{1,0:T(8,128)S(1)}, f32[144,128]{1,0:T(8,128)S(1)}, u32[]{:S(2)}, u32[]{:S(2)}) collective-permute-start(f32[144,128]{1,0:T(8,128)S(1)} %shard_map.90.refs_7_.refs_1_), channel_id=1, source_target_pairs={{0,6},{1,7},{2,0},{3,1},{4,2},{5,3},{6,4},{7,5},{8,14},{9,15},{10,... | collective-permute-start | bytes 221192 | tf_op jit(solution)/shard_map/ppermute | solution.py:365
  38.2 0.3 collective-permute-start.6
  38.6 0.7 collective-permute-start.5
  39.3 2.2 %shard_map.91 = (f32[10,256,128]{2,1,0:T(8,128)S(1)}, f32[8,128]{1,0:T(8,128)S(1)}) custom-call(bf16[10,256,128]{2,1,0:T(8,128)(2,1)S(1)} %collective-permute-done.refs_3_.refs_0_, bf16[10,256,128]{2,1,0:T(8,128)(2,1)S(1)} %bitcast.16, bf16[10,256,128]{2,1,0:T(8,128)(2,1)S(1)} %collective-permute-done.2.refs_1_.refs_2_, ...), custom_call_target="tpu_custom_call" | custom-call | tf_op jit(solution)/shard_map/pallas_call | solution.py:308
  41.5 1.5 %collective-permute-done.6.refs_3_ = f32[144,128]{1,0:T(8,128)S(1)} collective-permute-done((f32[144,128]{1,0:T(8,128)S(1)}, f32[144,128]{1,0:T(8,128)S(1)}, u32[]{:S(2)}, u32[]{:S(2)}) %collective-permute-start.6) | collective-permute-done | bytes 73760 | tf_op jit(solution)/shard_map/ppermute | solution.py:365
  43.0 2.1 %collective-permute-done.5.refs_2_ = f32[144,128]{1,0:T(8,128)S(1)} collective-permute-done((f32[144,128]{1,0:T(8,128)S(1)}, f32[144,128]{1,0:T(8,128)S(1)}, u32[]{:S(2)}, u32[]{:S(2)}) %collective-permute-start.5) | collective-permute-done | bytes 73760 | tf_op jit(solution)/shard_map/ppermute | solution.py:365
  45.1 0.7 shard_map.92
  45.8 1.2 %collective-permute-start.9 = (f32[256,128]{1,0:T(8,128)S(1)}, f32[256,128]{1,0:T(8,128)S(1)}, u32[]{:S(2)}, u32[]{:S(2)}) collective-permute-start(f32[256,128]{1,0:T(8,128)S(1)} %get-tuple-element.24.refs_1_.refs_4_), channel_id=1, source_target_pairs={{8,0},{16,8},{24,16},{32,24},{40,32},{48,40},{56,48},{64,56},{72,6... | collective-permute-start | bytes 393224 | tf_op jit(solution)/shard_map/ppermute | solution.py:322
  47.0 0.4 collective-permute-start.8
  47.4 1.1 %shard_map.93.refs_3_ = f32[256,128]{1,0:T(8,128)S(1)} custom-call(bf16[10,256,128]{2,1,0:T(8,128)(2,1)S(1)} %bitcast.17, f32[256,128]{1,0:T(8,128)S(1)} %get-tuple-element.24.refs_1_.refs_4_, bf16[3584,256]{1,0:T(8,128)(2,1)S(1)} %copy-done.1), custom_call_target="tpu_custom_call" | custom-call | tf_op jit(solution)/shard_map/pallas_call | solution.py:308
  48.4 1.3 %collective-permute-done.9.refs_2_.refs_5_ = f32[256,128]{1,0:T(8,128)S(1)} collective-permute-done((f32[256,128]{1,0:T(8,128)S(1)}, f32[256,128]{1,0:T(8,128)S(1)}, u32[]{:S(2)}, u32[]{:S(2)}) %collective-permute-start.9) | collective-permute-done | bytes 131104 | tf_op jit(solution)/shard_map/ppermute | solution.py:322
  49.7 1.1 %shard_map.94.refs_5_ = f32[256,128]{1,0:T(8,128)S(1)} custom-call(bf16[10,256,128]{2,1,0:T(8,128)(2,1)S(1)} %bitcast.18, bf16[10,256,128]{2,1,0:T(8,128)(2,1)S(1)} %collective-permute-done.2.refs_1_.refs_2_, f32[256,128]{1,0:T(8,128)S(1)} %collective-permute-done.9.refs_2_.refs_5_, f32[256,128]{1,0:T(8,128)S(1)} %shard_map.93.refs_3_, ...), custom_call_target="tpu_custom_call" | custom-call | tf_op jit(solution)/shard_map/pallas_call | solution.py:308
  50.8 3.3 %collective-permute-done.8.refs_4_.refs_3_ = f32[256,128]{1,0:T(8,128)S(1)} collective-permute-done((f32[256,128]{1,0:T(8,128)S(1)}, f32[256,128]{1,0:T(8,128)S(1)}, u32[]{:S(2)}, u32[]{:S(2)}) %collective-permute-start.8) | collective-permute-done | bytes 131104 | tf_op jit(solution)/shard_map/ppermute | solution.py:322
  54.1 1.6 %shard_map.95 = (f32[144,128]{1,0:T(8,128)S(1)}, f32[144,128]{1,0:T(8,128)S(1)}) custom-call(s32[1]{0:T(128)S(6)} %copy.10.refs_0_, s32[1]{0:T(128)} %bitcast.refs_1_.place, bf16[10,256,128]{2,1,0:T(8,128)(2,1)S(1)} %bitcast.19, bf16[10,256,128]{2,1,0:T(8,128)(2,1)S(1)} %collective-permute-done.refs_3_.refs_0_, ...), custom_call_target="tpu_custom_call" | custom-call | tf_op jit(solution)/shard_map/pallas_call | solution.py:308
  55.7 2.4 %collective-permute-start.10 = (f32[144,128]{1,0:T(8,128)S(1)}, f32[144,128]{1,0:T(8,128)S(1)}, u32[]{:S(2)}, u32[]{:S(2)}) collective-permute-start(f32[144,128]{1,0:T(8,128)S(1)} %get-tuple-element.26), channel_id=1, source_target_pairs={{0,1},{1,0},{2,3},{3,2},{4,5},{5,4},{6,7},{7,6},{8,9},{9,8},{10,11... | collective-permute-start | bytes 221192 | tf_op jit(solution)/shard_map/ppermute | solution.py:359
  58.2 0.9 %collective-permute-done.10.second = f32[144,128]{1,0:T(8,128)S(1)} collective-permute-done((f32[144,128]{1,0:T(8,128)S(1)}, f32[144,128]{1,0:T(8,128)S(1)}, u32[]{:S(2)}, u32[]{:S(2)}) %collective-permute-start.10) | collective-permute-done | bytes 73760 | tf_op jit(solution)/shard_map/ppermute | solution.py:359
  59.1 0.4 collective-permute-start.13
  59.4 0.5 collective-permute-start.12
  59.9 0.8 collective-permute-start.11
  60.7 2.3 %shard_map.97 = (f32[10,256,128]{2,1,0:T(8,128)S(1)}, f32[8,128]{1,0:T(8,128)S(1)}) custom-call(bf16[10,256,128]{2,1,0:T(8,128)(2,1)S(1)} %collective-permute-done.refs_3_.refs_0_, bf16[10,256,128]{2,1,0:T(8,128)(2,1)S(1)} %bitcast.20, bf16[10,256,128]{2,1,0:T(8,128)(2,1)S(1)} %collective-permute-done.2.refs_1_.refs_2_, ...), custom_call_target="tpu_custom_call" | custom-call | tf_op jit(solution)/shard_map/pallas_call | solution.py:308
  63.0 1.2 %collective-permute-done.12.refs_2_ = f32[144,128]{1,0:T(8,128)S(1)} collective-permute-done((f32[144,128]{1,0:T(8,128)S(1)}, f32[144,128]{1,0:T(8,128)S(1)}, u32[]{:S(2)}, u32[]{:S(2)}) %collective-permute-start.12) | collective-permute-done | bytes 73760 | tf_op jit(solution)/shard_map/ppermute | solution.py:365
  64.2 2.3 %collective-permute-done.11.refs_1_ = f32[144,128]{1,0:T(8,128)S(1)} collective-permute-done((f32[144,128]{1,0:T(8,128)S(1)}, f32[144,128]{1,0:T(8,128)S(1)}, u32[]{:S(2)}, u32[]{:S(2)}) %collective-permute-start.11) | collective-permute-done | bytes 73760 | tf_op jit(solution)/shard_map/ppermute | solution.py:365
  66.4 0.2 shard_map.98
  66.6 0.8 %collective-permute-start.14 = (f32[2,128,128]{2,1,0:T(8,128)S(1)}, f32[2,128,128]{2,1,0:T(8,128)S(1)}, u32[]{:S(2)}, u32[]{:S(2)}) collective-permute-start(f32[2,128,128]{2,1,0:T(8,128)S(1)} %get-tuple-element.35.mine), channel_id=1, source_target_pairs={{0,1},{1,0},{2,3},{3,2},{4,5},{5,4},{6,7},{7,6},{8,9},{9,8},{10,11... | collective-permute-start | bytes 393224 | tf_op jit(solution)/shard_map/ppermute | solution.py:359
  67.5 11.5 %all_to_all.5 = f32[32,1,128]{2,1,0:T(1,128)S(1)} all-to-all(f32[32,1,128]{2,1,0:T(1,128)S(1)} %bitcast.28), channel_id=1, replica_groups=mesh['tile'=32,'ens'=8] {'tile'}, dimensions={0} | all-to-all | bytes 32768 | tf_op jit(solution)/shard_map/all_to_all | solution.py:413
  79.0 1.7 %shard_map.99 = (f32[10,256,128]{2,1,0:T(8,128)}, f32[256,128]{1,0:T(8,128)}) custom-call(s32[1]{0:T(128)} %bitcast.refs_1_.place, f32[32,128]{1,0:T(8,128)S(1)} %bitcast.25, f32[10,256,128]{2,1,0:T(8,128)S(1)} %get-tuple-element.33.alpha0, f32[10,256,128]{2,1,0:T(8,128)S(1)} %get-tuple-element.34.alpha1, f32[2,128,128]{2,1,0:T(8,128)S(1)} %get-tuple-element.35.mine, ...), custom_call_target="tpu_custom_call" | custom-call | tf_op jit(solution)/shard_map/pallas_call | solution.py:308
  (19 shorter events, 0.1 us)
Async XLA Ops:
  0.6 25.1 %collective-permute-start.2 = (bf16[10,256,128]{2,1,0:T(8,128)(2,1)}, bf16[10,256,128]{2,1,0:T(8,128)(2,1)S(1)}, u32[]{:S(2)}, u32[]{:S(2)}) collective-permute-start(bf16[10,256,128]{2,1,0:T(8,128)(2,1)} %bitcast.11), channel_id=1, source_target_pairs={{8,0},{16,8},{24,16},{32,24},{40,32},{48,40},{56,48},{64,56},{72,6... | collective-permute-start | bytes 1966088 | tf_op jit(solution)/shard_map/ppermute | solution.py:322
  9.3 21.6 %collective-permute-start = (bf16[10,256,128]{2,1,0:T(8,128)(2,1)}, bf16[10,256,128]{2,1,0:T(8,128)(2,1)S(1)}, u32[]{:S(2)}, u32[]{:S(2)}) collective-permute-start(bf16[10,256,128]{2,1,0:T(8,128)(2,1)} %bitcast.12), channel_id=1, source_target_pairs={{0,8},{8,16},{16,24},{24,32},{32,40},{40,48},{48,56},{56,64},{64,7... | collective-permute-start | bytes 1966088 | tf_op jit(solution)/shard_map/ppermute | solution.py:322
  10.0 0.9 %copy-start.4 = (f32[16,2048]{1,0:T(8,128)S(1)}, f32[16,2048]{1,0:T(8,128)}, u32[]{:S(2)}) copy-start(f32[16,2048]{1,0:T(8,128)} %refs_7_.3) | copy-start | bytes 393220
  10.9 0.7 copy-start.6
  11.6 0.7 copy-start.8
  12.3 0.7 copy-start.10
  13.7 12.0 %collective-permute-start.3 = (f32[256,128]{1,0:T(8,128)S(1)}, f32[256,128]{1,0:T(8,128)S(1)}, u32[]{:S(2)}, u32[]{:S(2)}) collective-permute-start(f32[256,128]{1,0:T(8,128)S(1)} %get-tuple-element.20.refs_1_.refs_4_), channel_id=1, source_target_pairs={{8,0},{16,8},{24,16},{32,24},{40,32},{48,40},{56,48},{64,56},{72,6... | collective-permute-start | bytes 393224 | tf_op jit(solution)/shard_map/ppermute | solution.py:322
  18.6 12.4 %collective-permute-start.1 = (f32[256,128]{1,0:T(8,128)S(1)}, f32[256,128]{1,0:T(8,128)S(1)}, u32[]{:S(2)}, u32[]{:S(2)}) collective-permute-start(f32[256,128]{1,0:T(8,128)S(1)} %get-tuple-element.20.refs_1_.refs_4_), channel_id=1, source_target_pairs={{0,8},{8,16},{16,24},{24,32},{32,40},{40,48},{48,56},{56,64},{64,7... | collective-permute-start | bytes 393224 | tf_op jit(solution)/shard_map/ppermute | solution.py:322
  18.6 1.5 %copy-start = (bf16[3584,256]{1,0:T(8,128)(2,1)S(1)}, bf16[3584,256]{1,0:T(8,128)(2,1)}, u32[]{:S(2)}) copy-start(bf16[3584,256]{1,0:T(8,128)(2,1)} %constant.6.clone.refs_2_.refs_4_.refs_6_) | copy-start | bytes 5505028
  20.1 1.1 %copy-start.2 = (bf16[10,16,16,128]{3,2,1,0:T(8,128)(2,1)S(1)}, bf16[10,16,16,128]{3,2,1,0:T(8,128)(2,1)}, u32[]{:S(2)}) copy-start(bf16[10,16,16,128]{3,2,1,0:T(8,128)(2,1)} %param.7) | copy-start | bytes 1966084
  21.1 4.6 %copy-start.1 = (bf16[3584,256]{1,0:T(8,128)(2,1)S(1)}, bf16[3584,256]{1,0:T(8,128)(2,1)}, u32[]{:S(2)}) copy-start(bf16[3584,256]{1,0:T(8,128)(2,1)} %constant.6.clone.refs_2_.refs_4_.refs_6_) | copy-start | bytes 5505028
  22.2 8.7 %copy-start.3 = (bf16[10,16,16,128]{3,2,1,0:T(8,128)(2,1)S(1)}, bf16[10,16,16,128]{3,2,1,0:T(8,128)(2,1)}, u32[]{:S(2)}) copy-start(bf16[10,16,16,128]{3,2,1,0:T(8,128)(2,1)} %param.7) | copy-start | bytes 1966084
  22.2 8.7 %copy-start.5 = (f32[16,2048]{1,0:T(8,128)S(1)}, f32[16,2048]{1,0:T(8,128)}, u32[]{:S(2)}) copy-start(f32[16,2048]{1,0:T(8,128)} %refs_7_.3) | copy-start | bytes 393220
  22.2 8.7 %copy-start.7 = (s32[2048]{0:T(1024)S(1)}, s32[2048]{0:T(1024)}, u32[]{:S(2)}) copy-start(s32[2048]{0:T(1024)} %param.11) | copy-start | bytes 24580
  32.5 2.9 %collective-permute-start.4 = (f32[144,128]{1,0:T(8,128)S(1)}, f32[144,128]{1,0:T(8,128)S(1)}, u32[]{:S(2)}, u32[]{:S(2)}) collective-permute-start(f32[144,128]{1,0:T(8,128)S(1)} %get-tuple-element.22), channel_id=1, source_target_pairs={{0,1},{1,0},{2,3},{3,2},{4,5},{5,4},{6,7},{7,6},{8,9},{9,8},{10,11... | collective-permute-start | bytes 221192 | tf_op jit(solution)/shard_map/ppermute | solution.py:359
  35.4 9.7 %copy-start.9 = (f32[2048]{0:T(1024)S(1)}, f32[2048]{0:T(1024)}, u32[]{:S(2)}) copy-start(f32[2048]{0:T(1024)} %param.9) | copy-start | bytes 24580
  35.4 6.1 %collective-permute-start.7 = (f32[144,128]{1,0:T(8,128)S(1)}, f32[144,128]{1,0:T(8,128)S(1)}, u32[]{:S(2)}, u32[]{:S(2)}) collective-permute-start(f32[144,128]{1,0:T(8,128)S(1)} %shard_map.90.refs_7_.refs_1_), channel_id=1, source_target_pairs={{0,6},{1,7},{2,0},{3,1},{4,2},{5,3},{6,4},{7,5},{8,14},{9,15},{10,... | collective-permute-start | bytes 221192 | tf_op jit(solution)/shard_map/ppermute | solution.py:365
  38.2 4.8 %collective-permute-start.6 = (f32[144,128]{1,0:T(8,128)S(1)}, f32[144,128]{1,0:T(8,128)S(1)}, u32[]{:S(2)}, u32[]{:S(2)}) collective-permute-start(f32[144,128]{1,0:T(8,128)S(1)} %shard_map.90.refs_7_.refs_1_), channel_id=1, source_target_pairs={{0,4},{1,5},{2,6},{3,7},{4,0},{5,1},{6,2},{7,3},{8,12},{9,13},{10,... | collective-permute-start | bytes 221192 | tf_op jit(solution)/shard_map/ppermute | solution.py:365
  38.6 6.5 %collective-permute-start.5 = (f32[144,128]{1,0:T(8,128)S(1)}, f32[144,128]{1,0:T(8,128)S(1)}, u32[]{:S(2)}, u32[]{:S(2)}) collective-permute-start(f32[144,128]{1,0:T(8,128)S(1)} %shard_map.90.refs_7_.refs_1_), channel_id=1, source_target_pairs={{0,2},{1,3},{2,4},{3,5},{4,6},{5,7},{6,0},{7,1},{8,10},{9,11},{10,... | collective-permute-start | bytes 221192 | tf_op jit(solution)/shard_map/ppermute | solution.py:365
  45.8 3.9 %collective-permute-start.9 = (f32[256,128]{1,0:T(8,128)S(1)}, f32[256,128]{1,0:T(8,128)S(1)}, u32[]{:S(2)}, u32[]{:S(2)}) collective-permute-start(f32[256,128]{1,0:T(8,128)S(1)} %get-tuple-element.24.refs_1_.refs_4_), channel_id=1, source_target_pairs={{8,0},{16,8},{24,16},{32,24},{40,32},{48,40},{56,48},{64,56},{72,6... | collective-permute-start | bytes 393224 | tf_op jit(solution)/shard_map/ppermute | solution.py:322
  47.0 7.1 %collective-permute-start.8 = (f32[256,128]{1,0:T(8,128)S(1)}, f32[256,128]{1,0:T(8,128)S(1)}, u32[]{:S(2)}, u32[]{:S(2)}) collective-permute-start(f32[256,128]{1,0:T(8,128)S(1)} %get-tuple-element.24.refs_1_.refs_4_), channel_id=1, source_target_pairs={{0,8},{8,16},{16,24},{24,32},{32,40},{40,48},{48,56},{56,64},{64,7... | collective-permute-start | bytes 393224 | tf_op jit(solution)/shard_map/ppermute | solution.py:322
  55.7 3.4 %collective-permute-start.10 = (f32[144,128]{1,0:T(8,128)S(1)}, f32[144,128]{1,0:T(8,128)S(1)}, u32[]{:S(2)}, u32[]{:S(2)}) collective-permute-start(f32[144,128]{1,0:T(8,128)S(1)} %get-tuple-element.26), channel_id=1, source_target_pairs={{0,1},{1,0},{2,3},{3,2},{4,5},{5,4},{6,7},{7,6},{8,9},{9,8},{10,11... | collective-permute-start | bytes 221192 | tf_op jit(solution)/shard_map/ppermute | solution.py:359
  59.1 3.9 %collective-permute-start.13 = (f32[144,128]{1,0:T(8,128)S(1)}, f32[144,128]{1,0:T(8,128)S(1)}, u32[]{:S(2)}, u32[]{:S(2)}) collective-permute-start(f32[144,128]{1,0:T(8,128)S(1)} %shard_map.96.refs_7_.refs_0_), channel_id=1, source_target_pairs={{0,6},{1,7},{2,0},{3,1},{4,2},{5,3},{6,4},{7,5},{8,14},{9,15},{10,... | collective-permute-start | bytes 221192 | tf_op jit(solution)/shard_map/ppermute | solution.py:365
  59.4 4.7 %collective-permute-start.12 = (f32[144,128]{1,0:T(8,128)S(1)}, f32[144,128]{1,0:T(8,128)S(1)}, u32[]{:S(2)}, u32[]{:S(2)}) collective-permute-start(f32[144,128]{1,0:T(8,128)S(1)} %shard_map.96.refs_7_.refs_0_), channel_id=1, source_target_pairs={{0,4},{1,5},{2,6},{3,7},{4,0},{5,1},{6,2},{7,3},{8,12},{9,13},{10,... | collective-permute-start | bytes 221192 | tf_op jit(solution)/shard_map/ppermute | solution.py:365
  59.9 6.5 %collective-permute-start.11 = (f32[144,128]{1,0:T(8,128)S(1)}, f32[144,128]{1,0:T(8,128)S(1)}, u32[]{:S(2)}, u32[]{:S(2)}) collective-permute-start(f32[144,128]{1,0:T(8,128)S(1)} %shard_map.96.refs_7_.refs_0_), channel_id=1, source_target_pairs={{0,2},{1,3},{2,4},{3,5},{4,6},{5,7},{6,0},{7,1},{8,10},{9,11},{10,... | collective-permute-start | bytes 221192 | tf_op jit(solution)/shard_map/ppermute | solution.py:365
  66.6 12.4 %collective-permute-start.14 = (f32[2,128,128]{2,1,0:T(8,128)S(1)}, f32[2,128,128]{2,1,0:T(8,128)S(1)}, u32[]{:S(2)}, u32[]{:S(2)}) collective-permute-start(f32[2,128,128]{2,1,0:T(8,128)S(1)} %get-tuple-element.35.mine), channel_id=1, source_target_pairs={{0,1},{1,0},{2,3},{3,2},{4,5},{5,4},{6,7},{7,6},{8,9},{9,8},{10,11... | collective-permute-start | bytes 393224 | tf_op jit(solution)/shard_map/ppermute | solution.py:359

commit v7 on v6

--- a/solution.py
+++ b/solution.py
@@ -76,39 +76,44 @@
 
 
 def column_hits(cell, columns):
-    return jnp.where(
-        lax.broadcasted_iota(jnp.int32, (columns, cell.shape[1]), 0) == cell % columns, 1.0, 0.0
-    ).astype(BF16)
-
-
-def adjoint(values, weights_ref, cell_ref, rows, columns):
+    column = lax.rem(cell, columns) if columns & (columns - 1) else cell & (columns - 1)
+    return jnp.where(lax.broadcasted_iota(jnp.int32, (columns, cell.shape[1]), 0) == column, 1.0, 0.0).astype(BF16)
+
+
+def row_hits(cell, rows, columns):
+    row = lax.div(cell, columns) if columns & (columns - 1) else cell >> (columns.bit_length() - 1)
+    return lax.broadcasted_iota(jnp.int32, (rows, cell.shape[1]), 0) == row
+
+
+def adjoint(values, weights_ref, cell_ref, hits_ref, rows, parts_ref):
     levels, slots = weights_ref.shape
+    columns = hits_ref.shape[0]
     total = levels * rows
     chunk = 256
-    field = jnp.zeros((2 * total, columns), F32)
     for start in range(0, slots, chunk):
-        cell = cell_ref[:, start : start + chunk]
-        hits = column_hits(cell, columns)
-        here = lax.broadcasted_iota(jnp.int32, (rows, chunk), 0) == cell // columns
-        weighted = weights_ref[:, start : start + chunk] * values[:, start : start + chunk]
+        lanes = slice(start, start + chunk)
+        here = row_hits(cell_ref[:, lanes], rows, columns)
+        weighted = weights_ref[:, lanes] * values[:, lanes]
         parts = [jnp.where(here, weighted[level : level + 1], 0.0) for level in range(levels)]
         high, low = split(jnp.concatenate(parts, axis=0))
-        both = jnp.concatenate([high, low], axis=0)
-        field = field + lax.dot_general(both, hits, (((1,), (1,)), ((), ())), preferred_element_type=F32)
+        parts_ref[:total, lanes] = high
+        parts_ref[total:, lanes] = low
+    field = lax.dot_general(
+        parts_ref[...], hits_ref[...], (((1,), (1,)), ((), ())), preferred_element_type=F32
+    )
     return field[:total] + field[total:]
 
 
-def observe(field, weights_ref, cell_ref, live, rows, columns):
+def observe(field, weights_ref, cell_ref, hits_ref, live, rows):
     levels, slots = weights_ref.shape
     chunk = 256
     high, low = split(field)
     both = jnp.concatenate([high, low], axis=1)
     observed = []
     for start in range(0, slots, chunk):
-        cell = cell_ref[:, start : start + chunk]
-        hits = column_hits(cell, columns)
+        hits = hits_ref[:, start : start + chunk]
         picked = dot(both, jnp.concatenate([hits, hits], axis=0))
-        here = lax.broadcasted_iota(jnp.int32, (rows, chunk), 0) == cell // columns
+        here = row_hits(cell_ref[:, start : start + chunk], rows, hits.shape[0])
         total = jnp.zeros((rows, chunk), F32)
         for level in range(levels):
             weight = weights_ref[level : level + 1, start : start + chunk]
@@ -157,9 +162,10 @@
     return jnp.concatenate([block[i : i + 1] for i in range(block.shape[0])], axis=1)
 
 
-def start_kernel(rows, columns, count, place, weights, cell, precision, innovations, field, precision_rows, c_rows):
+def start_kernel(rows, columns, count, place, weights, cell, precision, innovations, field, precision_rows, c_rows, hits, parts):
     c = live_slots(count, weights.shape[1]) * precision[...] * innovations[...]
-    field[...] = adjoint(c, weights, cell, rows, columns)
+    hits[...] = column_hits(cell[...], columns)
+    field[...] = adjoint(c, weights, cell, hits, rows, parts)
     precision_rows[...] = as_rows(precision[...])
     c_rows[...] = as_rows(c)
 
@@ -181,9 +187,9 @@
         message[lines:] = field[pl.ds(pl.multiple_of(at * half, half), half)]
 
 
-def observe_kernel(rows, columns, places, count, place, p, p_side, g_side, part, constants, weights, cell, kept, given, field, mixed):
+def observe_kernel(rows, places, count, place, p, p_side, g_side, part, constants, weights, cell, hits, kept, given, field, mixed):
     field[...] = summed_members(part[...], p, p_side, g_side, constants, places, "b", mixed)
-    observed = as_rows(observe(field[...], weights, cell, live_slots(count, weights.shape[1]), rows, columns))
+    observed = as_rows(observe(field[...], weights, cell, hits, live_slots(count, weights.shape[1]), rows))
     message_rows(place, observed, field, kept, given)
 
 
@@ -191,13 +197,13 @@
     total[...] = first[...] + second[...]
 
 
-def middle_kernel(rows, columns, count, *refs):
-    *messages, weights, cell, precision, after, field, observed, half = refs
+def middle_kernel(rows, count, *refs):
+    *messages, weights, cell, hits, precision, after, field, observed, half, parts = refs
     lines = observed.shape[0]
     half[...] = sum(message[lines:] for message in messages)
     summed = sum(message[:lines] for message in messages)
     observed[...] = summed
-    field[...] = adjoint(precision[...] * as_line(summed), weights, cell, rows, columns)
+    field[...] = adjoint(precision[...] * as_line(summed), weights, cell, hits, rows, parts)
 
 
 def alpha_kernel(places, p0, p1, p2, g0, g1, g2, constants, after, alpha, token, mixed):
@@ -303,7 +309,8 @@
 
 def call(kernel, outs, args, scratch=(), out_space=pltpu.VMEM):
     single = not isinstance(outs, list)
-    shapes = [jax.ShapeDtypeStruct(shape, F32) for shape in ([outs] if single else outs)]
+    outs = [outs] if single else outs
+    shapes = [out if isinstance(out, jax.ShapeDtypeStruct) else jax.ShapeDtypeStruct(out, F32) for out in outs]
     out_spec = pl.BlockSpec(memory_space=out_space)
     return pl.pallas_call(
         kernel,
@@ -376,30 +383,33 @@
 
     p_before, p_after = neighbours(p)
     weights = obs_weights
-    g0, precision_rows, c_rows = call(
-        bound(start_kernel, *shape), [field_shape, (lines, 128), (lines, 128)],
-        [in_smem(obs_count), in_smem(place)] + vmem(weights, cell, precision, innovations_line),
+    parts = pltpu.VMEM((2 * cells, slots), BF16)
+    g0, precision_rows, c_rows, hits = call(
+        bound(start_kernel, *shape),
+        [field_shape, (lines, 128), (lines, 128), jax.ShapeDtypeStruct((columns, slots), BF16)],
+        [in_smem(obs_count), in_smem(place)] + vmem(weights, cell, precision, innovations_line), [parts],
     )
     g0_before, g0_after = neighbours(g0)
     part = own_and_after(g0, g0_after)
     message = (lines + half, columns)
     kept, given = call(
-        bound(observe_kernel, *shape, places), [message, message],
-        [in_smem(obs_count), in_smem(place)] + vmem(p, p_before, g0_before, part, constants, weights, cell),
+        bound(observe_kernel, rows, places), [message, message],
+        [in_smem(obs_count), in_smem(place)] + vmem(p, p_before, g0_before, part, constants, weights, cell, hits),
         [pltpu.VMEM(field_shape, F32), mixed],
     )
     sent = summed(kept, other_core(given))
     messages = from_chips(sent)
     alpha0, done0 = alpha_of(g0, g0_before, g0_after, sent)
     g1, once, half0 = call(
-        bound(middle_kernel, *shape), [field_shape, (lines, 128), (half, columns)],
-        [in_smem(obs_count)] + vmem(*messages, weights, cell, precision) + [anywhere(done0)],
+        bound(middle_kernel, rows), [field_shape, (lines, 128), (half, columns)],
+        [in_smem(obs_count)] + vmem(*messages, weights, cell, hits, precision) + [anywhere(done0)],
+        [parts],
     )
     g1_before, g1_after = neighbours(g1)
     part = own_and_after(g1, g1_after)
     kept, given = call(
-        bound(observe_kernel, *shape, places), [message, message],
-        [in_smem(obs_count), in_smem(place)] + vmem(p, p_before, g1_before, part, constants, weights, cell),
+        bound(observe_kernel, rows, places), [message, message],
+        [in_smem(obs_count), in_smem(place)] + vmem(p, p_before, g1_before, part, constants, weights, cell, hits),
         [pltpu.VMEM(field_shape, F32), mixed],
     )
     sent = summed(kept, other_core(given))

time: 81.2 us -> 81 us (level)
  no operation moved by 1% of the time
where the time goes in v7:
time: 81 us; the launch traced here: 80.7 us
  starting transfers between devices  25.8 us (32%)
  waiting for transfers between devices  21.2 us (26%)
  Pallas kernels  15 us (19%)
  blocking collectives  11.5 us (14%)
  local copies, waits for them, and re-layouts  5.6 us (7%)
  between operations  1.62 us (2%)
    ppermute x6, starting transfers between devices, neighbours(): return (lax.ppermute(x, 'tile', up), lax.ppermute(x, 'tile', down))  15.1 us
    pallas_call x14, Pallas kernels, call(): pl.pallas_call(kernel, out_shape=shapes[0] if single else shapes, in_spec...  15 us
    ppermute x6, waiting for transfers between devices, neighbours(): return (lax.ppermute(x, 'tile', up), lax.ppermute(x, 'tile', down))  12.3 us
    all_to_all x1, blocking collectives, local(): lax.all_to_all(scalars.reshape(tiles, 1, 128), 'tile', 0, 0)  11.5 us
    ppermute x6, waiting for transfers between devices, from_chips(): arrived.append(lax.ppermute(x, 'ens', route))  7.04 us
    unnamed x22, local copies, waits for them, and re-layouts  5.6 us
    ppermute x6, starting transfers between devices, from_chips(): arrived.append(lax.ppermute(x, 'ens', route))  5.46 us
    ppermute x3, starting transfers between devices, other_core(): return lax.ppermute(x, 'ens', [(i, i ^ 1) for i in range(ens)])  5.22 us
  transfers between devices with their start and end apart: 15, of which 10 were waited for; matrix products, arithmetic and copies ran while one was open for 0% of the time, Pallas kernels for 12%

profile of v7, /device:TPU:1, one launch (start us, length us, event | category | flops | bytes accessed | tf_op | source)
XLA Modules:
  0.0 80.7 jit_solution(15485042312163542999)
XLA Ops:
  0.6 8.7 %collective-permute-start.2 = (bf16[10,256,128]{2,1,0:T(8,128)(2,1)}, bf16[10,256,128]{2,1,0:T(8,128)(2,1)S(1)}, u32[]{:S(2)}, u32[]{:S(2)}) collective-permute-start(bf16[10,256,128]{2,1,0:T(8,128)(2,1)} %bitcast.11), channel_id=1, source_target_pairs={{8,0},{16,8},{24,16},{32,24},{40,32},{48,40},{56,48},{64,56},{72,6... | collective-permute-start | bytes 1966088 | tf_op jit(solution)/shard_map/ppermute | solution.py:329
  10.0 0.0 copy-start.4
  10.0 0.9 %copy-done.4 = f32[16,2048]{1,0:T(8,128)S(1)} copy-done((f32[16,2048]{1,0:T(8,128)S(1)}, f32[16,2048]{1,0:T(8,128)}, u32[]{:S(2)}) %copy-start.4) | copy-done | bytes 131096
  10.9 0.7 copy-done.6
  11.6 0.7 copy-done.8
  12.3 0.7 copy-done.10
  13.0 0.7 shard_map.86
  13.7 4.9 %collective-permute-start.3 = (f32[256,128]{1,0:T(8,128)S(1)}, f32[256,128]{1,0:T(8,128)S(1)}, u32[]{:S(2)}, u32[]{:S(2)}) collective-permute-start(f32[256,128]{1,0:T(8,128)S(1)} %get-tuple-element.21.refs_1_.refs_4_), channel_id=1, source_target_pairs={{8,0},{16,8},{24,16},{32,24},{40,32},{48,40},{56,48},{64,56},{72,6... | collective-permute-start | bytes 393224 | tf_op jit(solution)/shard_map/ppermute | solution.py:329
  18.6 0.0 collective-permute-start.1
  18.6 1.5 %copy-done = bf16[3584,256]{1,0:T(8,128)(2,1)S(1)} copy-done((bf16[3584,256]{1,0:T(8,128)(2,1)S(1)}, bf16[3584,256]{1,0:T(8,128)(2,1)}, u32[]{:S(2)}) %copy-start) | copy-done | bytes 1835032
  20.1 1.1 %copy-done.2 = bf16[10,16,16,128]{3,2,1,0:T(8,128)(2,1)S(1)} copy-done((bf16[10,16,16,128]{3,2,1,0:T(8,128)(2,1)S(1)}, bf16[10,16,16,128]{3,2,1,0:T(8,128)(2,1)}, u32[]{:S(2)}) %copy-start.2) | copy-done | bytes 655384
  21.2 1.0 %shard_map.87.refs_3_ = f32[256,128]{1,0:T(8,128)S(1)} custom-call(bf16[10,256,128]{2,1,0:T(8,128)(2,1)S(1)} %bitcast.13, f32[256,128]{1,0:T(8,128)S(1)} %get-tuple-element.21.refs_1_.refs_4_, bf16[3584,256]{1,0:T(8,128)(2,1)S(1)} %copy-done), custom_call_target="tpu_custom_call" | custom-call | tf_op jit(solution)/shard_map/pallas_call | solution.py:315
  22.2 0.0 copy-start.3
  22.2 0.0 copy-start.5
  22.2 0.0 copy-start.7
  22.2 3.5 %collective-permute-done.3.refs_2_.refs_5_ = f32[256,128]{1,0:T(8,128)S(1)} collective-permute-done((f32[256,128]{1,0:T(8,128)S(1)}, f32[256,128]{1,0:T(8,128)S(1)}, u32[]{:S(2)}, u32[]{:S(2)}) %collective-permute-start.3) | collective-permute-done | bytes 131104 | tf_op jit(solution)/shard_map/ppermute | solution.py:329
  25.7 1.1 %shard_map.88.refs_5_ = f32[256,128]{1,0:T(8,128)S(1)} custom-call(bf16[10,256,128]{2,1,0:T(8,128)(2,1)S(1)} %bitcast.14, bf16[10,256,128]{2,1,0:T(8,128)(2,1)S(1)} %collective-permute-done.2.refs_1_.refs_2_, f32[256,128]{1,0:T(8,128)S(1)} %collective-permute-done.3.refs_2_.refs_5_, f32[256,128]{1,0:T(8,128)S(1)} %shard_map.87.refs_3_, ...), custom_call_target="tpu_custom_call" | custom-call | tf_op jit(solution)/shard_map/pallas_call | solution.py:315
  26.8 4.1 %collective-permute-done.1.refs_4_.refs_3_ = f32[256,128]{1,0:T(8,128)S(1)} collective-permute-done((f32[256,128]{1,0:T(8,128)S(1)}, f32[256,128]{1,0:T(8,128)S(1)}, u32[]{:S(2)}, u32[]{:S(2)}) %collective-permute-start.1) | collective-permute-done | bytes 131104 | tf_op jit(solution)/shard_map/ppermute | solution.py:329
  31.0 1.5 %shard_map.89 = (f32[144,128]{1,0:T(8,128)S(1)}, f32[144,128]{1,0:T(8,128)S(1)}) custom-call(s32[1]{0:T(128)S(6)} %copy.10.refs_0_, s32[1]{0:T(128)} %bitcast.refs_1_.place, bf16[10,256,128]{2,1,0:T(8,128)(2,1)S(1)} %bitcast.15, bf16[10,256,128]{2,1,0:T(8,128)(2,1)S(1)} %collective-permute-done.refs_3_.refs_0_, ...), custom_call_target="tpu_custom_call" | custom-call | tf_op jit(solution)/shard_map/pallas_call | solution.py:315
  32.4 2.0 %collective-permute-start.4 = (f32[144,128]{1,0:T(8,128)S(1)}, f32[144,128]{1,0:T(8,128)S(1)}, u32[]{:S(2)}, u32[]{:S(2)}) collective-permute-start(f32[144,128]{1,0:T(8,128)S(1)} %get-tuple-element.24), channel_id=1, source_target_pairs={{0,1},{1,0},{2,3},{3,2},{4,5},{5,4},{6,7},{7,6},{8,9},{9,8},{10,11... | collective-permute-start | bytes 221192 | tf_op jit(solution)/shard_map/ppermute | solution.py:366
  34.4 0.9 %collective-permute-done.4.second = f32[144,128]{1,0:T(8,128)S(1)} collective-permute-done((f32[144,128]{1,0:T(8,128)S(1)}, f32[144,128]{1,0:T(8,128)S(1)}, u32[]{:S(2)}, u32[]{:S(2)}) %collective-permute-start.4) | collective-permute-done | bytes 73760 | tf_op jit(solution)/shard_map/ppermute | solution.py:366
  35.3 0.0 copy-start.9
  35.3 2.8 %collective-permute-start.7 = (f32[144,128]{1,0:T(8,128)S(1)}, f32[144,128]{1,0:T(8,128)S(1)}, u32[]{:S(2)}, u32[]{:S(2)}) collective-permute-start(f32[144,128]{1,0:T(8,128)S(1)} %shard_map.90.refs_7_.refs_1_), channel_id=1, source_target_pairs={{0,6},{1,7},{2,0},{3,1},{4,2},{5,3},{6,4},{7,5},{8,14},{9,15},{10,... | collective-permute-start | bytes 221192 | tf_op jit(solution)/shard_map/ppermute | solution.py:372
  38.1 0.3 collective-permute-start.6
  38.5 0.7 collective-permute-start.5
  39.2 2.2 %shard_map.91 = (f32[10,256,128]{2,1,0:T(8,128)S(1)}, f32[8,128]{1,0:T(8,128)S(1)}) custom-call(bf16[10,256,128]{2,1,0:T(8,128)(2,1)S(1)} %collective-permute-done.refs_3_.refs_0_, bf16[10,256,128]{2,1,0:T(8,128)(2,1)S(1)} %bitcast.16, bf16[10,256,128]{2,1,0:T(8,128)(2,1)S(1)} %collective-permute-done.2.refs_1_.refs_2_, ...), custom_call_target="tpu_custom_call" | custom-call | tf_op jit(solution)/shard_map/pallas_call | solution.py:315
  41.4 1.5 %collective-permute-done.6.refs_3_ = f32[144,128]{1,0:T(8,128)S(1)} collective-permute-done((f32[144,128]{1,0:T(8,128)S(1)}, f32[144,128]{1,0:T(8,128)S(1)}, u32[]{:S(2)}, u32[]{:S(2)}) %collective-permute-start.6) | collective-permute-done | bytes 73760 | tf_op jit(solution)/shard_map/ppermute | solution.py:372
  42.9 2.1 %collective-permute-done.5.refs_2_ = f32[144,128]{1,0:T(8,128)S(1)} collective-permute-done((f32[144,128]{1,0:T(8,128)S(1)}, f32[144,128]{1,0:T(8,128)S(1)}, u32[]{:S(2)}, u32[]{:S(2)}) %collective-permute-start.5) | collective-permute-done | bytes 73760 | tf_op jit(solution)/shard_map/ppermute | solution.py:372
  45.0 0.7 shard_map.92
  45.7 1.2 %collective-permute-start.9 = (f32[256,128]{1,0:T(8,128)S(1)}, f32[256,128]{1,0:T(8,128)S(1)}, u32[]{:S(2)}, u32[]{:S(2)}) collective-permute-start(f32[256,128]{1,0:T(8,128)S(1)} %get-tuple-element.26.refs_1_.refs_4_), channel_id=1, source_target_pairs={{8,0},{16,8},{24,16},{32,24},{40,32},{48,40},{56,48},{64,56},{72,6... | collective-permute-start | bytes 393224 | tf_op jit(solution)/shard_map/ppermute | solution.py:329
  46.9 0.3 collective-permute-start.8
  47.2 1.1 %shard_map.93.refs_3_ = f32[256,128]{1,0:T(8,128)S(1)} custom-call(bf16[10,256,128]{2,1,0:T(8,128)(2,1)S(1)} %bitcast.17, f32[256,128]{1,0:T(8,128)S(1)} %get-tuple-element.26.refs_1_.refs_4_, bf16[3584,256]{1,0:T(8,128)(2,1)S(1)} %copy-done.1), custom_call_target="tpu_custom_call" | custom-call | tf_op jit(solution)/shard_map/pallas_call | solution.py:315
  48.3 1.3 %collective-permute-done.9.refs_2_.refs_5_ = f32[256,128]{1,0:T(8,128)S(1)} collective-permute-done((f32[256,128]{1,0:T(8,128)S(1)}, f32[256,128]{1,0:T(8,128)S(1)}, u32[]{:S(2)}, u32[]{:S(2)}) %collective-permute-start.9) | collective-permute-done | bytes 131104 | tf_op jit(solution)/shard_map/ppermute | solution.py:329
  49.6 1.1 %shard_map.94.refs_5_ = f32[256,128]{1,0:T(8,128)S(1)} custom-call(bf16[10,256,128]{2,1,0:T(8,128)(2,1)S(1)} %bitcast.18, bf16[10,256,128]{2,1,0:T(8,128)(2,1)S(1)} %collective-permute-done.2.refs_1_.refs_2_, f32[256,128]{1,0:T(8,128)S(1)} %collective-permute-done.9.refs_2_.refs_5_, f32[256,128]{1,0:T(8,128)S(1)} %shard_map.93.refs_3_, ...), custom_call_target="tpu_custom_call" | custom-call | tf_op jit(solution)/shard_map/pallas_call | solution.py:315
  50.7 3.4 %collective-permute-done.8.refs_4_.refs_3_ = f32[256,128]{1,0:T(8,128)S(1)} collective-permute-done((f32[256,128]{1,0:T(8,128)S(1)}, f32[256,128]{1,0:T(8,128)S(1)}, u32[]{:S(2)}, u32[]{:S(2)}) %collective-permute-start.8) | collective-permute-done | bytes 131104 | tf_op jit(solution)/shard_map/ppermute | solution.py:329
  54.0 1.5 %shard_map.95 = (f32[144,128]{1,0:T(8,128)S(1)}, f32[144,128]{1,0:T(8,128)S(1)}) custom-call(s32[1]{0:T(128)S(6)} %copy.10.refs_0_, s32[1]{0:T(128)} %bitcast.refs_1_.place, bf16[10,256,128]{2,1,0:T(8,128)(2,1)S(1)} %bitcast.19, bf16[10,256,128]{2,1,0:T(8,128)(2,1)S(1)} %collective-permute-done.refs_3_.refs_0_, ...), custom_call_target="tpu_custom_call" | custom-call | tf_op jit(solution)/shard_map/pallas_call | solution.py:315
  55.5 2.4 %collective-permute-start.10 = (f32[144,128]{1,0:T(8,128)S(1)}, f32[144,128]{1,0:T(8,128)S(1)}, u32[]{:S(2)}, u32[]{:S(2)}) collective-permute-start(f32[144,128]{1,0:T(8,128)S(1)} %get-tuple-element.28), channel_id=1, source_target_pairs={{0,1},{1,0},{2,3},{3,2},{4,5},{5,4},{6,7},{7,6},{8,9},{9,8},{10,11... | collective-permute-start | bytes 221192 | tf_op jit(solution)/shard_map/ppermute | solution.py:366
  57.9 0.9 %collective-permute-done.10.second = f32[144,128]{1,0:T(8,128)S(1)} collective-permute-done((f32[144,128]{1,0:T(8,128)S(1)}, f32[144,128]{1,0:T(8,128)S(1)}, u32[]{:S(2)}, u32[]{:S(2)}) %collective-permute-start.10) | collective-permute-done | bytes 73760 | tf_op jit(solution)/shard_map/ppermute | solution.py:366
  58.9 0.4 collective-permute-start.13
  59.2 0.5 collective-permute-start.12
  59.7 0.8 collective-permute-start.11
  60.5 2.3 %shard_map.97 = (f32[10,256,128]{2,1,0:T(8,128)S(1)}, f32[8,128]{1,0:T(8,128)S(1)}) custom-call(bf16[10,256,128]{2,1,0:T(8,128)(2,1)S(1)} %collective-permute-done.refs_3_.refs_0_, bf16[10,256,128]{2,1,0:T(8,128)(2,1)S(1)} %bitcast.20, bf16[10,256,128]{2,1,0:T(8,128)(2,1)S(1)} %collective-permute-done.2.refs_1_.refs_2_, ...), custom_call_target="tpu_custom_call" | custom-call | tf_op jit(solution)/shard_map/pallas_call | solution.py:315
  62.7 1.2 %collective-permute-done.12.refs_2_ = f32[144,128]{1,0:T(8,128)S(1)} collective-permute-done((f32[144,128]{1,0:T(8,128)S(1)}, f32[144,128]{1,0:T(8,128)S(1)}, u32[]{:S(2)}, u32[]{:S(2)}) %collective-permute-start.12) | collective-permute-done | bytes 73760 | tf_op jit(solution)/shard_map/ppermute | solution.py:372
  64.0 2.3 %collective-permute-done.11.refs_1_ = f32[144,128]{1,0:T(8,128)S(1)} collective-permute-done((f32[144,128]{1,0:T(8,128)S(1)}, f32[144,128]{1,0:T(8,128)S(1)}, u32[]{:S(2)}, u32[]{:S(2)}) %collective-permute-start.11) | collective-permute-done | bytes 73760 | tf_op jit(solution)/shard_map/ppermute | solution.py:372
  66.2 0.2 shard_map.98
  66.4 0.8 %collective-permute-start.14 = (f32[2,128,128]{2,1,0:T(8,128)S(1)}, f32[2,128,128]{2,1,0:T(8,128)S(1)}, u32[]{:S(2)}, u32[]{:S(2)}) collective-permute-start(f32[2,128,128]{2,1,0:T(8,128)S(1)} %get-tuple-element.37.mine), channel_id=1, source_target_pairs={{0,1},{1,0},{2,3},{3,2},{4,5},{5,4},{6,7},{7,6},{8,9},{9,8},{10,11... | collective-permute-start | bytes 393224 | tf_op jit(solution)/shard_map/ppermute | solution.py:366
  67.3 11.5 %all_to_all.5 = f32[32,1,128]{2,1,0:T(1,128)S(1)} all-to-all(f32[32,1,128]{2,1,0:T(1,128)S(1)} %bitcast.28), channel_id=1, replica_groups=mesh['tile'=32,'ens'=8] {'tile'}, dimensions={0} | all-to-all | bytes 32768 | tf_op jit(solution)/shard_map/all_to_all | solution.py:423
  78.8 1.7 %shard_map.99 = (f32[10,256,128]{2,1,0:T(8,128)}, f32[256,128]{1,0:T(8,128)}) custom-call(s32[1]{0:T(128)} %bitcast.refs_1_.place, f32[32,128]{1,0:T(8,128)S(1)} %bitcast.25, f32[10,256,128]{2,1,0:T(8,128)S(1)} %get-tuple-element.35.alpha0, f32[10,256,128]{2,1,0:T(8,128)S(1)} %get-tuple-element.36.alpha1, f32[2,128,128]{2,1,0:T(8,128)S(1)} %get-tuple-element.37.mine, ...), custom_call_target="tpu_custom_call" | custom-call | tf_op jit(solution)/shard_map/pallas_call | solution.py:315
  (19 shorter events, 0.1 us)
Async XLA Ops:
  0.6 25.1 %collective-permute-start.2 = (bf16[10,256,128]{2,1,0:T(8,128)(2,1)}, bf16[10,256,128]{2,1,0:T(8,128)(2,1)S(1)}, u32[]{:S(2)}, u32[]{:S(2)}) collective-permute-start(bf16[10,256,128]{2,1,0:T(8,128)(2,1)} %bitcast.11), channel_id=1, source_target_pairs={{8,0},{16,8},{24,16},{32,24},{40,32},{48,40},{56,48},{64,56},{72,6... | collective-permute-start | bytes 1966088 | tf_op jit(solution)/shard_map/ppermute | solution.py:329
  9.3 21.6 %collective-permute-start = (bf16[10,256,128]{2,1,0:T(8,128)(2,1)}, bf16[10,256,128]{2,1,0:T(8,128)(2,1)S(1)}, u32[]{:S(2)}, u32[]{:S(2)}) collective-permute-start(bf16[10,256,128]{2,1,0:T(8,128)(2,1)} %bitcast.12), channel_id=1, source_target_pairs={{0,8},{8,16},{16,24},{24,32},{32,40},{40,48},{48,56},{56,64},{64,7... | collective-permute-start | bytes 1966088 | tf_op jit(solution)/shard_map/ppermute | solution.py:329
  10.0 0.9 %copy-start.4 = (f32[16,2048]{1,0:T(8,128)S(1)}, f32[16,2048]{1,0:T(8,128)}, u32[]{:S(2)}) copy-start(f32[16,2048]{1,0:T(8,128)} %refs_7_.3) | copy-start | bytes 393220
  10.9 0.7 copy-start.6
  11.6 0.7 copy-start.8
  12.3 0.7 copy-start.10
  13.7 12.0 %collective-permute-start.3 = (f32[256,128]{1,0:T(8,128)S(1)}, f32[256,128]{1,0:T(8,128)S(1)}, u32[]{:S(2)}, u32[]{:S(2)}) collective-permute-start(f32[256,128]{1,0:T(8,128)S(1)} %get-tuple-element.21.refs_1_.refs_4_), channel_id=1, source_target_pairs={{8,0},{16,8},{24,16},{32,24},{40,32},{48,40},{56,48},{64,56},{72,6... | collective-permute-start | bytes 393224 | tf_op jit(solution)/shard_map/ppermute | solution.py:329
  18.6 12.4 %collective-permute-start.1 = (f32[256,128]{1,0:T(8,128)S(1)}, f32[256,128]{1,0:T(8,128)S(1)}, u32[]{:S(2)}, u32[]{:S(2)}) collective-permute-start(f32[256,128]{1,0:T(8,128)S(1)} %get-tuple-element.21.refs_1_.refs_4_), channel_id=1, source_target_pairs={{0,8},{8,16},{16,24},{24,32},{32,40},{40,48},{48,56},{56,64},{64,7... | collective-permute-start | bytes 393224 | tf_op jit(solution)/shard_map/ppermute | solution.py:329
  18.6 1.5 %copy-start = (bf16[3584,256]{1,0:T(8,128)(2,1)S(1)}, bf16[3584,256]{1,0:T(8,128)(2,1)}, u32[]{:S(2)}) copy-start(bf16[3584,256]{1,0:T(8,128)(2,1)} %constant.6.clone.refs_2_.refs_4_.refs_6_) | copy-start | bytes 5505028
  20.1 1.1 %copy-start.2 = (bf16[10,16,16,128]{3,2,1,0:T(8,128)(2,1)S(1)}, bf16[10,16,16,128]{3,2,1,0:T(8,128)(2,1)}, u32[]{:S(2)}) copy-start(bf16[10,16,16,128]{3,2,1,0:T(8,128)(2,1)} %param.7) | copy-start | bytes 1966084
  21.2 4.6 %copy-start.1 = (bf16[3584,256]{1,0:T(8,128)(2,1)S(1)}, bf16[3584,256]{1,0:T(8,128)(2,1)}, u32[]{:S(2)}) copy-start(bf16[3584,256]{1,0:T(8,128)(2,1)} %constant.6.clone.refs_2_.refs_4_.refs_6_) | copy-start | bytes 5505028
  22.2 8.7 %copy-start.3 = (bf16[10,16,16,128]{3,2,1,0:T(8,128)(2,1)S(1)}, bf16[10,16,16,128]{3,2,1,0:T(8,128)(2,1)}, u32[]{:S(2)}) copy-start(bf16[10,16,16,128]{3,2,1,0:T(8,128)(2,1)} %param.7) | copy-start | bytes 1966084
  22.2 8.7 %copy-start.5 = (f32[16,2048]{1,0:T(8,128)S(1)}, f32[16,2048]{1,0:T(8,128)}, u32[]{:S(2)}) copy-start(f32[16,2048]{1,0:T(8,128)} %refs_7_.3) | copy-start | bytes 393220
  22.2 8.7 %copy-start.7 = (s32[2048]{0:T(1024)S(1)}, s32[2048]{0:T(1024)}, u32[]{:S(2)}) copy-start(s32[2048]{0:T(1024)} %param.11) | copy-start | bytes 24580
  32.4 2.9 %collective-permute-start.4 = (f32[144,128]{1,0:T(8,128)S(1)}, f32[144,128]{1,0:T(8,128)S(1)}, u32[]{:S(2)}, u32[]{:S(2)}) collective-permute-start(f32[144,128]{1,0:T(8,128)S(1)} %get-tuple-element.24), channel_id=1, source_target_pairs={{0,1},{1,0},{2,3},{3,2},{4,5},{5,4},{6,7},{7,6},{8,9},{9,8},{10,11... | collective-permute-start | bytes 221192 | tf_op jit(solution)/shard_map/ppermute | solution.py:366
  35.3 9.7 %copy-start.9 = (f32[2048]{0:T(1024)S(1)}, f32[2048]{0:T(1024)}, u32[]{:S(2)}) copy-start(f32[2048]{0:T(1024)} %param.9) | copy-start | bytes 24580
  35.3 6.1 %collective-permute-start.7 = (f32[144,128]{1,0:T(8,128)S(1)}, f32[144,128]{1,0:T(8,128)S(1)}, u32[]{:S(2)}, u32[]{:S(2)}) collective-permute-start(f32[144,128]{1,0:T(8,128)S(1)} %shard_map.90.refs_7_.refs_1_), channel_id=1, source_target_pairs={{0,6},{1,7},{2,0},{3,1},{4,2},{5,3},{6,4},{7,5},{8,14},{9,15},{10,... | collective-permute-start | bytes 221192 | tf_op jit(solution)/shard_map/ppermute | solution.py:372
  38.1 4.8 %collective-permute-start.6 = (f32[144,128]{1,0:T(8,128)S(1)}, f32[144,128]{1,0:T(8,128)S(1)}, u32[]{:S(2)}, u32[]{:S(2)}) collective-permute-start(f32[144,128]{1,0:T(8,128)S(1)} %shard_map.90.refs_7_.refs_1_), channel_id=1, source_target_pairs={{0,4},{1,5},{2,6},{3,7},{4,0},{5,1},{6,2},{7,3},{8,12},{9,13},{10,... | collective-permute-start | bytes 221192 | tf_op jit(solution)/shard_map/ppermute | solution.py:372
  38.5 6.5 %collective-permute-start.5 = (f32[144,128]{1,0:T(8,128)S(1)}, f32[144,128]{1,0:T(8,128)S(1)}, u32[]{:S(2)}, u32[]{:S(2)}) collective-permute-start(f32[144,128]{1,0:T(8,128)S(1)} %shard_map.90.refs_7_.refs_1_), channel_id=1, source_target_pairs={{0,2},{1,3},{2,4},{3,5},{4,6},{5,7},{6,0},{7,1},{8,10},{9,11},{10,... | collective-permute-start | bytes 221192 | tf_op jit(solution)/shard_map/ppermute | solution.py:372
  45.7 3.9 %collective-permute-start.9 = (f32[256,128]{1,0:T(8,128)S(1)}, f32[256,128]{1,0:T(8,128)S(1)}, u32[]{:S(2)}, u32[]{:S(2)}) collective-permute-start(f32[256,128]{1,0:T(8,128)S(1)} %get-tuple-element.26.refs_1_.refs_4_), channel_id=1, source_target_pairs={{8,0},{16,8},{24,16},{32,24},{40,32},{48,40},{56,48},{64,56},{72,6... | collective-permute-start | bytes 393224 | tf_op jit(solution)/shard_map/ppermute | solution.py:329
  46.9 7.1 %collective-permute-start.8 = (f32[256,128]{1,0:T(8,128)S(1)}, f32[256,128]{1,0:T(8,128)S(1)}, u32[]{:S(2)}, u32[]{:S(2)}) collective-permute-start(f32[256,128]{1,0:T(8,128)S(1)} %get-tuple-element.26.refs_1_.refs_4_), channel_id=1, source_target_pairs={{0,8},{8,16},{16,24},{24,32},{32,40},{40,48},{48,56},{56,64},{64,7... | collective-permute-start | bytes 393224 | tf_op jit(solution)/shard_map/ppermute | solution.py:329
  55.5 3.3 %collective-permute-start.10 = (f32[144,128]{1,0:T(8,128)S(1)}, f32[144,128]{1,0:T(8,128)S(1)}, u32[]{:S(2)}, u32[]{:S(2)}) collective-permute-start(f32[144,128]{1,0:T(8,128)S(1)} %get-tuple-element.28), channel_id=1, source_target_pairs={{0,1},{1,0},{2,3},{3,2},{4,5},{5,4},{6,7},{7,6},{8,9},{9,8},{10,11... | collective-permute-start | bytes 221192 | tf_op jit(solution)/shard_map/ppermute | solution.py:366
  58.9 3.9 %collective-permute-start.13 = (f32[144,128]{1,0:T(8,128)S(1)}, f32[144,128]{1,0:T(8,128)S(1)}, u32[]{:S(2)}, u32[]{:S(2)}) collective-permute-start(f32[144,128]{1,0:T(8,128)S(1)} %shard_map.96.refs_7_.refs_0_), channel_id=1, source_target_pairs={{0,6},{1,7},{2,0},{3,1},{4,2},{5,3},{6,4},{7,5},{8,14},{9,15},{10,... | collective-permute-start | bytes 221192 | tf_op jit(solution)/shard_map/ppermute | solution.py:372
  59.2 4.7 %collective-permute-start.12 = (f32[144,128]{1,0:T(8,128)S(1)}, f32[144,128]{1,0:T(8,128)S(1)}, u32[]{:S(2)}, u32[]{:S(2)}) collective-permute-start(f32[144,128]{1,0:T(8,128)S(1)} %shard_map.96.refs_7_.refs_0_), channel_id=1, source_target_pairs={{0,4},{1,5},{2,6},{3,7},{4,0},{5,1},{6,2},{7,3},{8,12},{9,13},{10,... | collective-permute-start | bytes 221192 | tf_op jit(solution)/shard_map/ppermute | solution.py:372
  59.7 6.5 %collective-permute-start.11 = (f32[144,128]{1,0:T(8,128)S(1)}, f32[144,128]{1,0:T(8,128)S(1)}, u32[]{:S(2)}, u32[]{:S(2)}) collective-permute-start(f32[144,128]{1,0:T(8,128)S(1)} %shard_map.96.refs_7_.refs_0_), channel_id=1, source_target_pairs={{0,2},{1,3},{2,4},{3,5},{4,6},{5,7},{6,0},{7,1},{8,10},{9,11},{10,... | collective-permute-start | bytes 221192 | tf_op jit(solution)/shard_map/ppermute | solution.py:372
  66.4 12.4 %collective-permute-start.14 = (f32[2,128,128]{2,1,0:T(8,128)S(1)}, f32[2,128,128]{2,1,0:T(8,128)S(1)}, u32[]{:S(2)}, u32[]{:S(2)}) collective-permute-start(f32[2,128,128]{2,1,0:T(8,128)S(1)} %get-tuple-element.37.mine), channel_id=1, source_target_pairs={{0,1},{1,0},{2,3},{3,2},{4,5},{5,4},{6,7},{7,6},{8,9},{9,8},{10,11... | collective-permute-start | bytes 393224 | tf_op jit(solution)/shard_map/ppermute | solution.py:366

commit v8 on v6

--- a/solution.py
+++ b/solution.py
@@ -168,8 +168,8 @@
     field[...] = summed_members(jnp.zeros(g.shape, F32), p, p, g, constants, places, "o", mixed)
 
 
-def side_kernel(places, p, p_side, g_side, part, constants, field, mixed):
-    field[...] = summed_members(part[...], p, p_side, g_side, constants, places, "a", mixed)
+def side_kernel(places, which, p, p_side, g_side, part, constants, field, mixed):
+    field[...] = summed_members(part[...], p, p_side, g_side, constants, places, which, mixed)
 
 
 def message_rows(place, observed, field, kept, given):
@@ -181,8 +181,8 @@
         message[lines:] = field[pl.ds(pl.multiple_of(at * half, half), half)]
 
 
-def observe_kernel(rows, columns, places, count, place, p, p_side, g_side, part, constants, weights, cell, kept, given, field, mixed):
-    field[...] = summed_members(part[...], p, p_side, g_side, constants, places, "b", mixed)
+def observe_kernel(rows, columns, places, which, count, place, p, p_side, g_side, part, constants, weights, cell, kept, given, field, mixed):
+    field[...] = summed_members(part[...], p, p_side, g_side, constants, places, which, mixed)
     observed = as_rows(observe(field[...], weights, cell, live_slots(count, weights.shape[1]), rows, columns))
     message_rows(place, observed, field, kept, given)
 
@@ -351,9 +351,9 @@
 
     mixed = pltpu.VMEM((members, cells, 2 * columns), BF16)
 
-    def own_and_after(g, g_after):
+    def own_and_side(which, g, p_side, g_side):
         part = call(bound(own_kernel, places), field_shape, vmem(p, g, constants), [mixed])
-        return call(bound(side_kernel, places), field_shape, vmem(p, p_after, g_after, part, constants), [mixed])
+        return call(bound(side_kernel, places, which), field_shape, vmem(p, p_side, g_side, part, constants), [mixed])
 
     def other_core(x):
         return lax.ppermute(x, "ens", [(i, i ^ 1) for i in range(ens)])
@@ -381,11 +381,11 @@
         [in_smem(obs_count), in_smem(place)] + vmem(weights, cell, precision, innovations_line),
     )
     g0_before, g0_after = neighbours(g0)
-    part = own_and_after(g0, g0_after)
+    part = own_and_side("b", g0, p_before, g0_before)
     message = (lines + half, columns)
     kept, given = call(
-        bound(observe_kernel, *shape, places), [message, message],
-        [in_smem(obs_count), in_smem(place)] + vmem(p, p_before, g0_before, part, constants, weights, cell),
+        bound(observe_kernel, *shape, places, "a"), [message, message],
+        [in_smem(obs_count), in_smem(place)] + vmem(p, p_after, g0_after, part, constants, weights, cell),
         [pltpu.VMEM(field_shape, F32), mixed],
     )
     sent = summed(kept, other_core(given))
@@ -396,10 +396,10 @@
         [in_smem(obs_count)] + vmem(*messages, weights, cell, precision) + [anywhere(done0)],
     )
     g1_before, g1_after = neighbours(g1)
-    part = own_and_after(g1, g1_after)
+    part = own_and_side("b", g1, p_before, g1_before)
     kept, given = call(
-        bound(observe_kernel, *shape, places), [message, message],
-        [in_smem(obs_count), in_smem(place)] + vmem(p, p_before, g1_before, part, constants, weights, cell),
+        bound(observe_kernel, *shape, places, "a"), [message, message],
+        [in_smem(obs_count), in_smem(place)] + vmem(p, p_after, g1_after, part, constants, weights, cell),
         [pltpu.VMEM(field_shape, F32), mixed],
     )
     sent = summed(kept, other_core(given))

time: 81.2 us -> 81.2 us (level)
  waiting for transfers between devices: 21.1 us -> 14.6 us
  blocking collectives: 11.5 us -> 15.5 us
  starting transfers between devices: 25.8 us -> 28.2 us
    ppermute x6, waiting for transfers between devices: 12.3 us -> 5.76 us  [neighbours(): return (lax.ppermute(x, 'tile', up), lax.ppermute(x, 'tile', down))]
    all_to_all x1, blocking collectives: 11.5 us -> 15.5 us  [local(): lax.all_to_all(scalars.reshape(tiles, 1, 128), 'tile', 0, 0)]
    ppermute x6, starting transfers between devices: 15.1 us -> 18.5 us  [neighbours(): return (lax.ppermute(x, 'tile', up), lax.ppermute(x, 'tile', down))]
    ppermute x3, starting transfers between devices: 5.23 us -> 4.33 us  [other_core(): return lax.ppermute(x, 'ens', [(i, i ^ 1) for i in range(ens)])]
  transfers between devices with their start and end apart: 15 -> 15, of which waited for: 10 -> 8; matrix products, arithmetic and copies ran while one was open for 0% -> 0% of each run, Pallas kernels for 12% -> 12%
where the time goes in v8:
time: 81.2 us; the launch traced here: 80.9 us
  starting transfers between devices  28.2 us (35%)
  blocking collectives  15.5 us (19%)
  Pallas kernels  15.3 us (19%)
  waiting for transfers between devices  14.6 us (18%)
  local copies, waits for them, and re-layouts  5.6 us (7%)
  between operations  1.66 us (2%)
    ppermute x6, starting transfers between devices, neighbours(): return (lax.ppermute(x, 'tile', up), lax.ppermute(x, 'tile', down))  18.5 us
    all_to_all x1, blocking collectives, local(): lax.all_to_all(scalars.reshape(tiles, 1, 128), 'tile', 0, 0)  15.5 us
    pallas_call x14, Pallas kernels, call(): pl.pallas_call(kernel, out_shape=shapes[0] if single else shapes, in_spec...  15.3 us
    ppermute x6, waiting for transfers between devices, from_chips(): arrived.append(lax.ppermute(x, 'ens', route))  7.02 us
    ppermute x6, waiting for transfers between devices, neighbours(): return (lax.ppermute(x, 'tile', up), lax.ppermute(x, 'tile', down))  5.76 us
    unnamed x22, local copies, waits for them, and re-layouts  5.6 us
    ppermute x6, starting transfers between devices, from_chips(): arrived.append(lax.ppermute(x, 'ens', route))  5.44 us
    ppermute x3, starting transfers between devices, other_core(): return lax.ppermute(x, 'ens', [(i, i ^ 1) for i in range(ens)])  4.33 us
  transfers between devices with their start and end apart: 15, of which 8 were waited for; matrix products, arithmetic and copies ran while one was open for 0% of the time, Pallas kernels for 12%

profile of v8, /device:TPU:1, one launch (start us, length us, event | category | flops | bytes accessed | tf_op | source)
XLA Modules:
  0.0 80.9 jit_solution(14585809394350603917)
XLA Ops:
  0.6 2.1 %collective-permute-start.2 = (bf16[10,256,128]{2,1,0:T(8,128)(2,1)}, bf16[10,256,128]{2,1,0:T(8,128)(2,1)S(1)}, u32[]{:S(2)}, u32[]{:S(2)}) collective-permute-start(bf16[10,256,128]{2,1,0:T(8,128)(2,1)} %bitcast.11), channel_id=1, source_target_pairs={{0,8},{8,16},{16,24},{24,32},{32,40},{40,48},{48,56},{56,64},{64,7... | collective-permute-start | bytes 1966088 | tf_op jit(solution)/shard_map/ppermute | solution.py:322
  2.7 6.7 %collective-permute-start = (bf16[10,256,128]{2,1,0:T(8,128)(2,1)}, bf16[10,256,128]{2,1,0:T(8,128)(2,1)S(1)}, u32[]{:S(2)}, u32[]{:S(2)}) collective-permute-start(bf16[10,256,128]{2,1,0:T(8,128)(2,1)} %bitcast.12), channel_id=1, source_target_pairs={{8,0},{16,8},{24,16},{32,24},{40,32},{48,40},{56,48},{64,56},{72,6... | collective-permute-start | bytes 1966088 | tf_op jit(solution)/shard_map/ppermute | solution.py:322
  10.1 0.0 copy-start.4
  10.1 0.9 %copy-done.4 = f32[16,2048]{1,0:T(8,128)S(1)} copy-done((f32[16,2048]{1,0:T(8,128)S(1)}, f32[16,2048]{1,0:T(8,128)}, u32[]{:S(2)}) %copy-start.4) | copy-done | bytes 131096
  11.0 0.7 copy-done.6
  11.7 0.7 copy-done.8
  12.4 0.7 copy-done.10
  13.1 0.7 shard_map.86
  13.8 0.1 collective-permute-start.3
  13.9 4.8 %collective-permute-start.1 = (f32[256,128]{1,0:T(8,128)S(1)}, f32[256,128]{1,0:T(8,128)S(1)}, u32[]{:S(2)}, u32[]{:S(2)}) collective-permute-start(f32[256,128]{1,0:T(8,128)S(1)} %get-tuple-element.20.refs_1_.refs_4_), channel_id=1, source_target_pairs={{8,0},{16,8},{24,16},{32,24},{40,32},{48,40},{56,48},{64,56},{72,6... | collective-permute-start | bytes 393224 | tf_op jit(solution)/shard_map/ppermute | solution.py:322
  18.7 1.5 %copy-done = bf16[3584,256]{1,0:T(8,128)(2,1)S(1)} copy-done((bf16[3584,256]{1,0:T(8,128)(2,1)S(1)}, bf16[3584,256]{1,0:T(8,128)(2,1)}, u32[]{:S(2)}) %copy-start) | copy-done | bytes 1835032
  20.2 1.1 %copy-done.2 = bf16[10,16,16,128]{3,2,1,0:T(8,128)(2,1)S(1)} copy-done((bf16[10,16,16,128]{3,2,1,0:T(8,128)(2,1)S(1)}, bf16[10,16,16,128]{3,2,1,0:T(8,128)(2,1)}, u32[]{:S(2)}) %copy-start.2) | copy-done | bytes 655384
  21.2 1.0 %shard_map.87.refs_3_ = f32[256,128]{1,0:T(8,128)S(1)} custom-call(bf16[10,256,128]{2,1,0:T(8,128)(2,1)S(1)} %bitcast.13, f32[256,128]{1,0:T(8,128)S(1)} %get-tuple-element.20.refs_1_.refs_4_, bf16[3584,256]{1,0:T(8,128)(2,1)S(1)} %copy-done), custom_call_target="tpu_custom_call" | custom-call | tf_op jit(solution)/shard_map/pallas_call | solution.py:308
  22.3 0.0 copy-start.3
  22.3 0.0 copy-start.5
  22.3 0.0 copy-start.7
  22.3 4.5 %collective-permute-done.3.refs_2_.refs_3_ = f32[256,128]{1,0:T(8,128)S(1)} collective-permute-done((f32[256,128]{1,0:T(8,128)S(1)}, f32[256,128]{1,0:T(8,128)S(1)}, u32[]{:S(2)}, u32[]{:S(2)}) %collective-permute-start.3) | collective-permute-done | bytes 131104 | tf_op jit(solution)/shard_map/ppermute | solution.py:322
  26.8 1.1 %shard_map.88.refs_5_ = f32[256,128]{1,0:T(8,128)S(1)} custom-call(bf16[10,256,128]{2,1,0:T(8,128)(2,1)S(1)} %bitcast.14, bf16[10,256,128]{2,1,0:T(8,128)(2,1)S(1)} %collective-permute-done.2.refs_1_.refs_0_, f32[256,128]{1,0:T(8,128)S(1)} %collective-permute-done.3.refs_2_.refs_3_, f32[256,128]{1,0:T(8,128)S(1)} %shard_map.87.refs_3_, ...), custom_call_target="tpu_custom_call" | custom-call | tf_op jit(solution)/shard_map/pallas_call | solution.py:308
  27.9 0.0 collective-permute-done.refs_3_.refs_2_
  27.9 1.6 %shard_map.89 = (f32[144,128]{1,0:T(8,128)S(1)}, f32[144,128]{1,0:T(8,128)S(1)}) custom-call(s32[1]{0:T(128)S(6)} %copy.10.refs_0_, s32[1]{0:T(128)} %bitcast.refs_1_.place, bf16[10,256,128]{2,1,0:T(8,128)(2,1)S(1)} %bitcast.15, bf16[10,256,128]{2,1,0:T(8,128)(2,1)S(1)} %collective-permute-done.refs_3_.refs_2_, ...), custom_call_target="tpu_custom_call" | custom-call | tf_op jit(solution)/shard_map/pallas_call | solution.py:308
  29.5 1.3 %collective-permute-start.4 = (f32[144,128]{1,0:T(8,128)S(1)}, f32[144,128]{1,0:T(8,128)S(1)}, u32[]{:S(2)}, u32[]{:S(2)}) collective-permute-start(f32[144,128]{1,0:T(8,128)S(1)} %get-tuple-element.22), channel_id=1, source_target_pairs={{0,1},{1,0},{2,3},{3,2},{4,5},{5,4},{6,7},{7,6},{8,9},{9,8},{10,11... | collective-permute-start | bytes 221192 | tf_op jit(solution)/shard_map/ppermute | solution.py:359
  30.8 0.9 %collective-permute-done.4.second = f32[144,128]{1,0:T(8,128)S(1)} collective-permute-done((f32[144,128]{1,0:T(8,128)S(1)}, f32[144,128]{1,0:T(8,128)S(1)}, u32[]{:S(2)}, u32[]{:S(2)}) %collective-permute-start.4) | collective-permute-done | bytes 73760 | tf_op jit(solution)/shard_map/ppermute | solution.py:359
  31.7 0.0 copy-start.9
  31.7 2.8 %collective-permute-start.7 = (f32[144,128]{1,0:T(8,128)S(1)}, f32[144,128]{1,0:T(8,128)S(1)}, u32[]{:S(2)}, u32[]{:S(2)}) collective-permute-start(f32[144,128]{1,0:T(8,128)S(1)} %shard_map.90.refs_7_.refs_1_), channel_id=1, source_target_pairs={{0,6},{1,7},{2,0},{3,1},{4,2},{5,3},{6,4},{7,5},{8,14},{9,15},{10,... | collective-permute-start | bytes 221192 | tf_op jit(solution)/shard_map/ppermute | solution.py:365
  34.6 0.3 collective-permute-start.6
  34.9 0.7 collective-permute-start.5
  35.6 2.2 %shard_map.91 = (f32[10,256,128]{2,1,0:T(8,128)S(1)}, f32[8,128]{1,0:T(8,128)S(1)}) custom-call(bf16[10,256,128]{2,1,0:T(8,128)(2,1)S(1)} %collective-permute-done.2.refs_1_.refs_0_, bf16[10,256,128]{2,1,0:T(8,128)(2,1)S(1)} %bitcast.16, bf16[10,256,128]{2,1,0:T(8,128)(2,1)S(1)} %collective-permute-done.refs_3_.refs_2_, ...), custom_call_target="tpu_custom_call" | custom-call | tf_op jit(solution)/shard_map/pallas_call | solution.py:308
  37.9 1.5 %collective-permute-done.6.refs_3_ = f32[144,128]{1,0:T(8,128)S(1)} collective-permute-done((f32[144,128]{1,0:T(8,128)S(1)}, f32[144,128]{1,0:T(8,128)S(1)}, u32[]{:S(2)}, u32[]{:S(2)}) %collective-permute-start.6) | collective-permute-done | bytes 73760 | tf_op jit(solution)/shard_map/ppermute | solution.py:365
  39.3 2.1 %collective-permute-done.5.refs_2_ = f32[144,128]{1,0:T(8,128)S(1)} collective-permute-done((f32[144,128]{1,0:T(8,128)S(1)}, f32[144,128]{1,0:T(8,128)S(1)}, u32[]{:S(2)}, u32[]{:S(2)}) %collective-permute-start.5) | collective-permute-done | bytes 73760 | tf_op jit(solution)/shard_map/ppermute | solution.py:365
  41.4 0.7 shard_map.92
  42.1 0.1 collective-permute-start.9
  42.2 4.8 %collective-permute-start.8 = (f32[256,128]{1,0:T(8,128)S(1)}, f32[256,128]{1,0:T(8,128)S(1)}, u32[]{:S(2)}, u32[]{:S(2)}) collective-permute-start(f32[256,128]{1,0:T(8,128)S(1)} %get-tuple-element.24.refs_1_.refs_4_), channel_id=1, source_target_pairs={{8,0},{16,8},{24,16},{32,24},{40,32},{48,40},{56,48},{64,56},{72,6... | collective-permute-start | bytes 393224 | tf_op jit(solution)/shard_map/ppermute | solution.py:322
  47.0 1.1 %shard_map.93.refs_3_ = f32[256,128]{1,0:T(8,128)S(1)} custom-call(bf16[10,256,128]{2,1,0:T(8,128)(2,1)S(1)} %bitcast.17, f32[256,128]{1,0:T(8,128)S(1)} %get-tuple-element.24.refs_1_.refs_4_, bf16[3584,256]{1,0:T(8,128)(2,1)S(1)} %copy-done.1), custom_call_target="tpu_custom_call" | custom-call | tf_op jit(solution)/shard_map/pallas_call | solution.py:308
  48.1 1.3 %collective-permute-done.9.refs_2_.refs_3_ = f32[256,128]{1,0:T(8,128)S(1)} collective-permute-done((f32[256,128]{1,0:T(8,128)S(1)}, f32[256,128]{1,0:T(8,128)S(1)}, u32[]{:S(2)}, u32[]{:S(2)}) %collective-permute-start.9) | collective-permute-done | bytes 131104 | tf_op jit(solution)/shard_map/ppermute | solution.py:322
  49.4 1.1 %shard_map.94.refs_5_ = f32[256,128]{1,0:T(8,128)S(1)} custom-call(bf16[10,256,128]{2,1,0:T(8,128)(2,1)S(1)} %bitcast.18, bf16[10,256,128]{2,1,0:T(8,128)(2,1)S(1)} %collective-permute-done.2.refs_1_.refs_0_, f32[256,128]{1,0:T(8,128)S(1)} %collective-permute-done.9.refs_2_.refs_3_, f32[256,128]{1,0:T(8,128)S(1)} %shard_map.93.refs_3_, ...), custom_call_target="tpu_custom_call" | custom-call | tf_op jit(solution)/shard_map/pallas_call | solution.py:308
  50.5 1.6 %shard_map.95 = (f32[144,128]{1,0:T(8,128)S(1)}, f32[144,128]{1,0:T(8,128)S(1)}) custom-call(s32[1]{0:T(128)S(6)} %copy.10.refs_0_, s32[1]{0:T(128)} %bitcast.refs_1_.place, bf16[10,256,128]{2,1,0:T(8,128)(2,1)S(1)} %bitcast.19, bf16[10,256,128]{2,1,0:T(8,128)(2,1)S(1)} %collective-permute-done.refs_3_.refs_2_, ...), custom_call_target="tpu_custom_call" | custom-call | tf_op jit(solution)/shard_map/pallas_call | solution.py:308
  52.0 2.2 %collective-permute-start.10 = (f32[144,128]{1,0:T(8,128)S(1)}, f32[144,128]{1,0:T(8,128)S(1)}, u32[]{:S(2)}, u32[]{:S(2)}) collective-permute-start(f32[144,128]{1,0:T(8,128)S(1)} %get-tuple-element.26), channel_id=1, source_target_pairs={{0,1},{1,0},{2,3},{3,2},{4,5},{5,4},{6,7},{7,6},{8,9},{9,8},{10,11... | collective-permute-start | bytes 221192 | tf_op jit(solution)/shard_map/ppermute | solution.py:359
  54.2 0.9 %collective-permute-done.10.second = f32[144,128]{1,0:T(8,128)S(1)} collective-permute-done((f32[144,128]{1,0:T(8,128)S(1)}, f32[144,128]{1,0:T(8,128)S(1)}, u32[]{:S(2)}, u32[]{:S(2)}) %collective-permute-start.10) | collective-permute-done | bytes 73760 | tf_op jit(solution)/shard_map/ppermute | solution.py:359
  55.1 0.3 collective-permute-start.13
  55.5 0.5 collective-permute-start.12
  56.0 0.8 collective-permute-start.11
  56.7 2.3 %shard_map.97 = (f32[10,256,128]{2,1,0:T(8,128)S(1)}, f32[8,128]{1,0:T(8,128)S(1)}) custom-call(bf16[10,256,128]{2,1,0:T(8,128)(2,1)S(1)} %collective-permute-done.2.refs_1_.refs_0_, bf16[10,256,128]{2,1,0:T(8,128)(2,1)S(1)} %bitcast.20, bf16[10,256,128]{2,1,0:T(8,128)(2,1)S(1)} %collective-permute-done.refs_3_.refs_2_, ...), custom_call_target="tpu_custom_call" | custom-call | tf_op jit(solution)/shard_map/pallas_call | solution.py:308
  59.0 1.2 %collective-permute-done.12.refs_2_ = f32[144,128]{1,0:T(8,128)S(1)} collective-permute-done((f32[144,128]{1,0:T(8,128)S(1)}, f32[144,128]{1,0:T(8,128)S(1)}, u32[]{:S(2)}, u32[]{:S(2)}) %collective-permute-start.12) | collective-permute-done | bytes 73760 | tf_op jit(solution)/shard_map/ppermute | solution.py:365
  60.2 2.3 %collective-permute-done.11.refs_1_ = f32[144,128]{1,0:T(8,128)S(1)} collective-permute-done((f32[144,128]{1,0:T(8,128)S(1)}, f32[144,128]{1,0:T(8,128)S(1)}, u32[]{:S(2)}, u32[]{:S(2)}) %collective-permute-start.11) | collective-permute-done | bytes 73760 | tf_op jit(solution)/shard_map/ppermute | solution.py:365
  62.5 0.2 shard_map.98
  62.7 0.8 %collective-permute-start.14 = (f32[2,128,128]{2,1,0:T(8,128)S(1)}, f32[2,128,128]{2,1,0:T(8,128)S(1)}, u32[]{:S(2)}, u32[]{:S(2)}) collective-permute-start(f32[2,128,128]{2,1,0:T(8,128)S(1)} %get-tuple-element.35.mine), channel_id=1, source_target_pairs={{0,1},{1,0},{2,3},{3,2},{4,5},{5,4},{6,7},{7,6},{8,9},{9,8},{10,11... | collective-permute-start | bytes 393224 | tf_op jit(solution)/shard_map/ppermute | solution.py:359
  63.5 15.5 %all_to_all.5 = f32[32,1,128]{2,1,0:T(1,128)S(1)} all-to-all(f32[32,1,128]{2,1,0:T(1,128)S(1)} %bitcast.28), channel_id=1, replica_groups=mesh['tile'=32,'ens'=8] {'tile'}, dimensions={0} | all-to-all | bytes 32768 | tf_op jit(solution)/shard_map/all_to_all | solution.py:413
  79.0 1.7 %shard_map.99 = (f32[10,256,128]{2,1,0:T(8,128)}, f32[256,128]{1,0:T(8,128)}) custom-call(s32[1]{0:T(128)} %bitcast.refs_1_.place, f32[32,128]{1,0:T(8,128)S(1)} %bitcast.25, f32[10,256,128]{2,1,0:T(8,128)S(1)} %get-tuple-element.33.alpha0, f32[10,256,128]{2,1,0:T(8,128)S(1)} %get-tuple-element.34.alpha1, f32[2,128,128]{2,1,0:T(8,128)S(1)} %get-tuple-element.35.mine, ...), custom_call_target="tpu_custom_call" | custom-call | tf_op jit(solution)/shard_map/pallas_call | solution.py:308
  (19 shorter events, 0.1 us)
Async XLA Ops:
  0.6 26.2 %collective-permute-start.2 = (bf16[10,256,128]{2,1,0:T(8,128)(2,1)}, bf16[10,256,128]{2,1,0:T(8,128)(2,1)S(1)}, u32[]{:S(2)}, u32[]{:S(2)}) collective-permute-start(bf16[10,256,128]{2,1,0:T(8,128)(2,1)} %bitcast.11), channel_id=1, source_target_pairs={{0,8},{8,16},{16,24},{24,32},{32,40},{40,48},{48,56},{56,64},{64,7... | collective-permute-start | bytes 1966088 | tf_op jit(solution)/shard_map/ppermute | solution.py:322
  2.7 25.1 %collective-permute-start = (bf16[10,256,128]{2,1,0:T(8,128)(2,1)}, bf16[10,256,128]{2,1,0:T(8,128)(2,1)S(1)}, u32[]{:S(2)}, u32[]{:S(2)}) collective-permute-start(bf16[10,256,128]{2,1,0:T(8,128)(2,1)} %bitcast.12), channel_id=1, source_target_pairs={{8,0},{16,8},{24,16},{32,24},{40,32},{48,40},{56,48},{64,56},{72,6... | collective-permute-start | bytes 1966088 | tf_op jit(solution)/shard_map/ppermute | solution.py:322
  10.1 0.9 %copy-start.4 = (f32[16,2048]{1,0:T(8,128)S(1)}, f32[16,2048]{1,0:T(8,128)}, u32[]{:S(2)}) copy-start(f32[16,2048]{1,0:T(8,128)} %refs_7_.3) | copy-start | bytes 393220
  11.0 0.7 copy-start.6
  11.7 0.7 copy-start.8
  12.4 0.7 copy-start.10
  13.8 13.0 %collective-permute-start.3 = (f32[256,128]{1,0:T(8,128)S(1)}, f32[256,128]{1,0:T(8,128)S(1)}, u32[]{:S(2)}, u32[]{:S(2)}) collective-permute-start(f32[256,128]{1,0:T(8,128)S(1)} %get-tuple-element.20.refs_1_.refs_4_), channel_id=1, source_target_pairs={{0,8},{8,16},{16,24},{24,32},{32,40},{40,48},{48,56},{56,64},{64,7... | collective-permute-start | bytes 393224 | tf_op jit(solution)/shard_map/ppermute | solution.py:322
  13.9 14.0 %collective-permute-start.1 = (f32[256,128]{1,0:T(8,128)S(1)}, f32[256,128]{1,0:T(8,128)S(1)}, u32[]{:S(2)}, u32[]{:S(2)}) collective-permute-start(f32[256,128]{1,0:T(8,128)S(1)} %get-tuple-element.20.refs_1_.refs_4_), channel_id=1, source_target_pairs={{8,0},{16,8},{24,16},{32,24},{40,32},{48,40},{56,48},{64,56},{72,6... | collective-permute-start | bytes 393224 | tf_op jit(solution)/shard_map/ppermute | solution.py:322
  18.7 1.5 %copy-start = (bf16[3584,256]{1,0:T(8,128)(2,1)S(1)}, bf16[3584,256]{1,0:T(8,128)(2,1)}, u32[]{:S(2)}) copy-start(bf16[3584,256]{1,0:T(8,128)(2,1)} %constant.6.clone.refs_2_.refs_4_.refs_6_) | copy-start | bytes 5505028
  20.2 1.1 %copy-start.2 = (bf16[10,16,16,128]{3,2,1,0:T(8,128)(2,1)S(1)}, bf16[10,16,16,128]{3,2,1,0:T(8,128)(2,1)}, u32[]{:S(2)}) copy-start(bf16[10,16,16,128]{3,2,1,0:T(8,128)(2,1)} %param.7) | copy-start | bytes 1966084
  21.2 5.6 %copy-start.1 = (bf16[3584,256]{1,0:T(8,128)(2,1)S(1)}, bf16[3584,256]{1,0:T(8,128)(2,1)}, u32[]{:S(2)}) copy-start(bf16[3584,256]{1,0:T(8,128)(2,1)} %constant.6.clone.refs_2_.refs_4_.refs_6_) | copy-start | bytes 5505028
  22.3 5.6 %copy-start.3 = (bf16[10,16,16,128]{3,2,1,0:T(8,128)(2,1)S(1)}, bf16[10,16,16,128]{3,2,1,0:T(8,128)(2,1)}, u32[]{:S(2)}) copy-start(bf16[10,16,16,128]{3,2,1,0:T(8,128)(2,1)} %param.7) | copy-start | bytes 1966084
  22.3 5.6 %copy-start.5 = (f32[16,2048]{1,0:T(8,128)S(1)}, f32[16,2048]{1,0:T(8,128)}, u32[]{:S(2)}) copy-start(f32[16,2048]{1,0:T(8,128)} %refs_7_.3) | copy-start | bytes 393220
  22.3 5.6 %copy-start.7 = (s32[2048]{0:T(1024)S(1)}, s32[2048]{0:T(1024)}, u32[]{:S(2)}) copy-start(s32[2048]{0:T(1024)} %param.11) | copy-start | bytes 24580
  29.5 2.2 %collective-permute-start.4 = (f32[144,128]{1,0:T(8,128)S(1)}, f32[144,128]{1,0:T(8,128)S(1)}, u32[]{:S(2)}, u32[]{:S(2)}) collective-permute-start(f32[144,128]{1,0:T(8,128)S(1)} %get-tuple-element.22), channel_id=1, source_target_pairs={{0,1},{1,0},{2,3},{3,2},{4,5},{5,4},{6,7},{7,6},{8,9},{9,8},{10,11... | collective-permute-start | bytes 221192 | tf_op jit(solution)/shard_map/ppermute | solution.py:359
  31.7 9.7 %copy-start.9 = (f32[2048]{0:T(1024)S(1)}, f32[2048]{0:T(1024)}, u32[]{:S(2)}) copy-start(f32[2048]{0:T(1024)} %param.9) | copy-start | bytes 24580
  31.7 6.1 %collective-permute-start.7 = (f32[144,128]{1,0:T(8,128)S(1)}, f32[144,128]{1,0:T(8,128)S(1)}, u32[]{:S(2)}, u32[]{:S(2)}) collective-permute-start(f32[144,128]{1,0:T(8,128)S(1)} %shard_map.90.refs_7_.refs_1_), channel_id=1, source_target_pairs={{0,6},{1,7},{2,0},{3,1},{4,2},{5,3},{6,4},{7,5},{8,14},{9,15},{10,... | collective-permute-start | bytes 221192 | tf_op jit(solution)/shard_map/ppermute | solution.py:365
  34.6 4.8 %collective-permute-start.6 = (f32[144,128]{1,0:T(8,128)S(1)}, f32[144,128]{1,0:T(8,128)S(1)}, u32[]{:S(2)}, u32[]{:S(2)}) collective-permute-start(f32[144,128]{1,0:T(8,128)S(1)} %shard_map.90.refs_7_.refs_1_), channel_id=1, source_target_pairs={{0,4},{1,5},{2,6},{3,7},{4,0},{5,1},{6,2},{7,3},{8,12},{9,13},{10,... | collective-permute-start | bytes 221192 | tf_op jit(solution)/shard_map/ppermute | solution.py:365
  34.9 6.5 %collective-permute-start.5 = (f32[144,128]{1,0:T(8,128)S(1)}, f32[144,128]{1,0:T(8,128)S(1)}, u32[]{:S(2)}, u32[]{:S(2)}) collective-permute-start(f32[144,128]{1,0:T(8,128)S(1)} %shard_map.90.refs_7_.refs_1_), channel_id=1, source_target_pairs={{0,2},{1,3},{2,4},{3,5},{4,6},{5,7},{6,0},{7,1},{8,10},{9,11},{10,... | collective-permute-start | bytes 221192 | tf_op jit(solution)/shard_map/ppermute | solution.py:365
  42.1 7.2 %collective-permute-start.9 = (f32[256,128]{1,0:T(8,128)S(1)}, f32[256,128]{1,0:T(8,128)S(1)}, u32[]{:S(2)}, u32[]{:S(2)}) collective-permute-start(f32[256,128]{1,0:T(8,128)S(1)} %get-tuple-element.24.refs_1_.refs_4_), channel_id=1, source_target_pairs={{0,8},{8,16},{16,24},{24,32},{32,40},{40,48},{48,56},{56,64},{64,7... | collective-permute-start | bytes 393224 | tf_op jit(solution)/shard_map/ppermute | solution.py:322
  42.2 8.2 %collective-permute-start.8 = (f32[256,128]{1,0:T(8,128)S(1)}, f32[256,128]{1,0:T(8,128)S(1)}, u32[]{:S(2)}, u32[]{:S(2)}) collective-permute-start(f32[256,128]{1,0:T(8,128)S(1)} %get-tuple-element.24.refs_1_.refs_4_), channel_id=1, source_target_pairs={{8,0},{16,8},{24,16},{32,24},{40,32},{48,40},{56,48},{64,56},{72,6... | collective-permute-start | bytes 393224 | tf_op jit(solution)/shard_map/ppermute | solution.py:322
  52.0 3.1 %collective-permute-start.10 = (f32[144,128]{1,0:T(8,128)S(1)}, f32[144,128]{1,0:T(8,128)S(1)}, u32[]{:S(2)}, u32[]{:S(2)}) collective-permute-start(f32[144,128]{1,0:T(8,128)S(1)} %get-tuple-element.26), channel_id=1, source_target_pairs={{0,1},{1,0},{2,3},{3,2},{4,5},{5,4},{6,7},{7,6},{8,9},{9,8},{10,11... | collective-permute-start | bytes 221192 | tf_op jit(solution)/shard_map/ppermute | solution.py:359
  55.1 3.9 %collective-permute-start.13 = (f32[144,128]{1,0:T(8,128)S(1)}, f32[144,128]{1,0:T(8,128)S(1)}, u32[]{:S(2)}, u32[]{:S(2)}) collective-permute-start(f32[144,128]{1,0:T(8,128)S(1)} %shard_map.96.refs_7_.refs_0_), channel_id=1, source_target_pairs={{0,6},{1,7},{2,0},{3,1},{4,2},{5,3},{6,4},{7,5},{8,14},{9,15},{10,... | collective-permute-start | bytes 221192 | tf_op jit(solution)/shard_map/ppermute | solution.py:365
  55.5 4.7 %collective-permute-start.12 = (f32[144,128]{1,0:T(8,128)S(1)}, f32[144,128]{1,0:T(8,128)S(1)}, u32[]{:S(2)}, u32[]{:S(2)}) collective-permute-start(f32[144,128]{1,0:T(8,128)S(1)} %shard_map.96.refs_7_.refs_0_), channel_id=1, source_target_pairs={{0,4},{1,5},{2,6},{3,7},{4,0},{5,1},{6,2},{7,3},{8,12},{9,13},{10,... | collective-permute-start | bytes 221192 | tf_op jit(solution)/shard_map/ppermute | solution.py:365
  56.0 6.5 %collective-permute-start.11 = (f32[144,128]{1,0:T(8,128)S(1)}, f32[144,128]{1,0:T(8,128)S(1)}, u32[]{:S(2)}, u32[]{:S(2)}) collective-permute-start(f32[144,128]{1,0:T(8,128)S(1)} %shard_map.96.refs_7_.refs_0_), channel_id=1, source_target_pairs={{0,2},{1,3},{2,4},{3,5},{4,6},{5,7},{6,0},{7,1},{8,10},{9,11},{10,... | collective-permute-start | bytes 221192 | tf_op jit(solution)/shard_map/ppermute | solution.py:365
  62.7 16.4 %collective-permute-start.14 = (f32[2,128,128]{2,1,0:T(8,128)S(1)}, f32[2,128,128]{2,1,0:T(8,128)S(1)}, u32[]{:S(2)}, u32[]{:S(2)}) collective-permute-start(f32[2,128,128]{2,1,0:T(8,128)S(1)} %get-tuple-element.35.mine), channel_id=1, source_target_pairs={{0,1},{1,0},{2,3},{3,2},{4,5},{5,4},{6,7},{7,6},{8,9},{9,8},{10,11... | collective-permute-start | bytes 393224 | tf_op jit(solution)/shard_map/ppermute | solution.py:359
